TPU v7x, 128 devices: a whole 4x4x4 slice. The times are simulated.
128 devices in a mesh: seq: 32 (over z_hi, y, x), batch: 4 (over z_lo, core).
Axes of the slice: x: 4, y: 4, z: 4 (z_hi: 2, z_lo: 2; z = z_hi * 2 + z_lo), core: 2. Of those that a mesh axis runs over, the one named last changes fastest.
Arguments:
- ids: int32 [4, 32768], P('batch', 'seq'), may hold values from 0 to 15
- embed: float32 [16, 256], replicated, may hold values from -6 to 6
- low_filter: float32 [2, 256], replicated, may hold values from 0.62 to 0.78
- high_filter: float32 [2, 256], replicated, may hold values from -3 to 3
- level_weights: float32 [14, 256], replicated, may hold values from -3 to 3
- mix: bfloat16 [256, 256], replicated, may hold values from -0.375 to 0.375
- cotangent: bfloat16 [4, 32768, 256], P('batch', 'seq'), may hold values from -6 to 6
Outputs:
- out: float32 [4, 32768, 256], P('batch', 'seq')
- grad_filters: float32 [2, 2, 256], replicated
- grad_levels: float32 [14, 256], replicated
- grad_mix: float32 [256, 256], replicated
- grad_embed: float32 [16, 256], replicated
All inputs are finite; a program needn't handle non-finite values.
Results may differ from a plain program's by a relative error of at most 0.003.
Values sent between devices are 32-bit elements; how exact they have to be, the bound alone decides.
A program may use at most 128 MiB of HBM per device.

v0:
```python
import math

import jax
import jax.numpy as jnp
from jax import lax
from jax.sharding import PartitionSpec as P


def passed_along(value, axis, steps):
    count = lax.axis_size(axis)
    leading, last = (max(0, -steps), min(count, count - steps))
    return lax.ppermute(value, axis, [(source, source + steps) for source in range(leading, last)])


def add_terms(totals, g_a, g_detail, value, shifted, axes):
    return (
        totals[0] + jnp.sum(g_a * value, axis=axes),
        totals[1] + jnp.sum(g_a * shifted, axis=axes),
        totals[2] + jnp.sum(g_detail * value, axis=axes),
        totals[3] + jnp.sum(g_detail * shifted, axis=axes),
    )


def per_device(ids, embed, low_filter, high_filter, level_weights, mix, cotangent):
    tokens = ids.shape[1]
    width = embed.shape[1]
    depth = level_weights.shape[0] - 1
    log_tok = tokens.bit_length() - 1
    onehot = (ids[0][:, None] == jnp.arange(embed.shape[0], dtype=jnp.int32)[None, :]).astype(
        jnp.float32
    )
    x = jnp.dot(onehot, embed, precision=lax.Precision.HIGHEST, preferred_element_type=jnp.float32)
    stored = []
    current = x
    mixed_sum = jnp.zeros_like(x)
    for level in range(log_tok):
        span = 2**level
        received = passed_along(current[tokens - span :], "seq", 1)
        shifted = jnp.concatenate([received, current[: tokens - span]], axis=0)
        stored.append((current, shifted))
        detail = high_filter[0] * current + high_filter[1] * shifted
        mixed_sum = mixed_sum + level_weights[level] * detail
        current = low_filter[0] * current + low_filter[1] * shifted
    deep_stored = []
    for level in range(log_tok, depth):
        shifted = passed_along(current, "seq", 2**level // tokens)
        deep_stored.append((current, shifted))
        detail = high_filter[0] * current + high_filter[1] * shifted
        mixed_sum = mixed_sum + level_weights[level] * detail
        current = low_filter[0] * current + low_filter[1] * shifted
    mixed_sum = mixed_sum + level_weights[depth] * current
    hidden = jax.nn.gelu(mixed_sum).astype(jnp.bfloat16)
    out = x + jnp.dot(hidden, mix, preferred_element_type=jnp.float32)
    cot = cotangent[0]
    g_hidden = lax.dot_general(
        cot, mix, (((1,), (1,)), ((), ())), preferred_element_type=jnp.float32
    )
    g_y = jax.vjp(jax.nn.gelu, mixed_sum)[1](g_hidden)[0]
    mix_term = lax.dot_general(
        hidden, cot, (((0,), (0,)), ((), ())), preferred_element_type=jnp.float32
    )
    level_rows = [None] * (depth + 1)
    zero_row = jnp.zeros((width,), jnp.float32)
    totals = (zero_row, zero_row, zero_row, zero_row)
    level_rows[depth] = jnp.sum(g_y * current, axis=0)
    g_a = level_weights[depth] * g_y
    for level in range(depth - 1, log_tok - 1, -1):
        value, shifted = deep_stored[level - log_tok]
        detail = high_filter[0] * value + high_filter[1] * shifted
        g_detail = level_weights[level] * g_y
        level_rows[level] = jnp.sum(g_y * detail, axis=0)
        totals = add_terms(totals, g_a, g_detail, value, shifted, 0)
        back = low_filter[1] * g_a + high_filter[1] * g_detail
        upward = passed_along(back, "seq", -(2**level // tokens))
        g_a = low_filter[0] * g_a + high_filter[0] * g_detail + upward
    for level in range(log_tok - 1, -1, -1):
        span = 2**level
        value, shifted = stored[level]
        detail = high_filter[0] * value + high_filter[1] * shifted
        g_detail = level_weights[level] * g_y
        level_rows[level] = jnp.sum(g_y * detail, axis=0)
        totals = add_terms(totals, g_a, g_detail, value, shifted, 0)
        back = low_filter[1] * g_a + high_filter[1] * g_detail
        received = passed_along(back[:span], "seq", -1)
        upward = jnp.concatenate([back[span:], received], axis=0)
        g_a = low_filter[0] * g_a + high_filter[0] * g_detail + upward
    g_x = cot.astype(jnp.float32) + g_a
    embed_term = lax.dot_general(
        onehot,
        g_x,
        (((0,), (0,)), ((), ())),
        precision=lax.Precision.HIGHEST,
        preferred_element_type=jnp.float32,
    )
    filter_term = jnp.stack([jnp.stack([totals[0], totals[1]]), jnp.stack([totals[2], totals[3]])])
    levels_term = jnp.stack(level_rows)
    filter_total, levels_total, embed_total, mix_total = lax.psum(
        (filter_term, levels_term, embed_term, mix_term), ("seq", "batch")
    )
    scale = 1.0 / math.sqrt(lax.axis_size("seq") * lax.axis_size("batch") * ids.shape[0] * tokens)
    return (
        out[None],
        scale * filter_total,
        scale * levels_total,
        scale * mix_total,
        scale * embed_total,
    )


def solution(mesh):
    placed = (P("batch", "seq"), P(), P(), P(), P(), P(), P("batch", "seq", None))
    return jax.shard_map(
        per_device,
        mesh=mesh,
        in_specs=placed,
        out_specs=(P("batch", "seq", None), P(), P(), P(), P()),
        check_vma=False,
    )
```

profile of v0, /device:TPU:1, one launch (start us, length us, event | category | flops | bytes accessed | tf_op | source)
XLA Modules:
  0.0 634.4 jit_solution(5356738132445860693)
XLA Ops:
  8.6 3.9 collective-permute-start
  13.5 3.6 collective-permute-start.1
  18.0 3.6 collective-permute-start.2
  22.6 3.6 collective-permute-start.3
  27.2 4.0 collective-permute-start.4
  32.1 5.7 collective-permute-start.5
  39.0 5.7 collective-permute-start.6
  46.2 5.7 collective-permute-start.7
  54.7 5.8 collective-permute-start.8
  60.5 4.6 collective-permute-done.8
  65.4 6.0 collective-permute-start.9
  71.4 8.7 %collective-permute-done.9 = f32[512,256]{1,0:T(8,128)S(1)} collective-permute-done((f32[512,256]{1,0:T(8,128)S(1)}, f32[512,256]{1,0:T(8,128)S(1)}, u32[]{:S(2)}, u32[]{:S(2)}) %collective-permute-start.9) | collective-permute-done | bytes 524320 | tf_op jit(solution)/shard_map/ppermute | solution.py:12
  80.2 6.1 collective-permute-start.10
  86.4 15.6 %collective-permute-done.10 = f32[1024,256]{1,0:T(8,128)S(1)} collective-permute-done((f32[1024,256]{1,0:T(8,128)S(1)}, f32[1024,256]{1,0:T(8,128)S(1)}, u32[]{:S(2)}, u32[]{:S(2)}) %collective-permute-start.10) | collective-permute-done | bytes 1048608 | tf_op jit(solution)/shard_map/ppermute | solution.py:12
  102.2 10.8 %collective-permute-start.11 = (f32[1024,256]{1,0:T(8,128)S(1)}, f32[1024,256]{1,0:T(8,128)S(1)}, u32[]{:S(2)}, u32[]{:S(2)}) collective-permute-start(f32[1024,256]{1,0:T(8,128)S(1)} %multiply_add_fusion.18), channel_id=1, source_target_pairs={{0,8},{4,12},{8,16},{12,20},{16,24},{20,28},{24,32},{28,36},{32,40... | collective-permute-start | bytes 3145736 | tf_op jit(solution)/shard_map/ppermute | solution.py:12
  113.0 11.9 %collective-permute-done.11 = f32[1024,256]{1,0:T(8,128)S(1)} collective-permute-done((f32[1024,256]{1,0:T(8,128)S(1)}, f32[1024,256]{1,0:T(8,128)S(1)}, u32[]{:S(2)}, u32[]{:S(2)}) %collective-permute-start.11) | collective-permute-done | bytes 1048608 | tf_op jit(solution)/shard_map/ppermute | solution.py:12
  125.0 13.1 %collective-permute-start.12 = (f32[1024,256]{1,0:T(8,128)S(1)}, f32[1024,256]{1,0:T(8,128)S(1)}, u32[]{:S(2)}, u32[]{:S(2)}) collective-permute-start(f32[1024,256]{1,0:T(8,128)S(1)} %multiply_add_fusion.16), channel_id=1, source_target_pairs={{0,16},{4,20},{8,24},{12,28},{16,32},{20,36},{24,40},{28,44},{32,4... | collective-permute-start | bytes 3145736 | tf_op jit(solution)/shard_map/ppermute | solution.py:12
  138.2 22.8 %collective-permute-done.12 = f32[1024,256]{1,0:T(8,128)S(1)} collective-permute-done((f32[1024,256]{1,0:T(8,128)S(1)}, f32[1024,256]{1,0:T(8,128)S(1)}, u32[]{:S(2)}, u32[]{:S(2)}) %collective-permute-start.12) | collective-permute-done | bytes 1048608 | tf_op jit(solution)/shard_map/ppermute | solution.py:12
  161.1 3.2 multiply_add_fusion.13
  166.6 14.8 %collective-permute-done.13 = f32[1024,256]{1,0:T(8,128)S(1)} collective-permute-done((f32[1024,256]{1,0:T(8,128)S(1)}, f32[1024,256]{1,0:T(8,128)S(1)}, u32[]{:S(2)}, u32[]{:S(2)}) %collective-permute-start.13) | collective-permute-done | bytes 1048608 | tf_op jit(solution)/shard_map/ppermute | solution.py:12
  183.1 15.7 %collective-permute-done.14 = f32[1024,256]{1,0:T(8,128)S(1)} collective-permute-done((f32[1024,256]{1,0:T(8,128)S(1)}, f32[1024,256]{1,0:T(8,128)S(1)}, u32[]{:S(2)}, u32[]{:S(2)}) %collective-permute-start.14) | collective-permute-done | bytes 1048608 | tf_op jit(solution)/shard_map/ppermute | solution.py:12
  202.4 14.2 %collective-permute-done.15 = f32[1024,256]{1,0:T(8,128)S(1)} collective-permute-done((f32[1024,256]{1,0:T(8,128)S(1)}, f32[1024,256]{1,0:T(8,128)S(1)}, u32[]{:S(2)}, u32[]{:S(2)}) %collective-permute-start.15) | collective-permute-done | bytes 1048608 | tf_op jit(solution)/shard_map/ppermute | solution.py:12
  218.7 19.1 %collective-permute-done.16 = f32[512,256]{1,0:T(8,128)S(1)} collective-permute-done((f32[512,256]{1,0:T(8,128)S(1)}, f32[512,256]{1,0:T(8,128)S(1)}, u32[]{:S(2)}, u32[]{:S(2)}) %collective-permute-start.16) | collective-permute-done | bytes 524320 | tf_op jit(solution)/shard_map/ppermute | solution.py:12
  240.6 8.8 %collective-permute-done.17 = f32[256,256]{1,0:T(8,128)S(1)} collective-permute-done((f32[256,256]{1,0:T(8,128)S(1)}, f32[256,256]{1,0:T(8,128)S(1)}, u32[]{:S(2)}, u32[]{:S(2)}) %collective-permute-start.17) | collective-permute-done | bytes 262176 | tf_op jit(solution)/shard_map/ppermute | solution.py:12
  251.4 13.3 %collective-permute-done.18 = f32[128,256]{1,0:T(8,128)S(1)} collective-permute-done((f32[128,256]{1,0:T(8,128)S(1)}, f32[128,256]{1,0:T(8,128)S(1)}, u32[]{:S(2)}, u32[]{:S(2)}) %collective-permute-start.18) | collective-permute-done | bytes 131104 | tf_op jit(solution)/shard_map/ppermute | solution.py:12
  267.4 8.9 %collective-permute-done.19 = f32[64,256]{1,0:T(8,128)S(1)} collective-permute-done((f32[64,256]{1,0:T(8,128)S(1)}, f32[64,256]{1,0:T(8,128)S(1)}, u32[]{:S(2)}, u32[]{:S(2)}) %collective-permute-start.19) | collective-permute-done | bytes 65568 | tf_op jit(solution)/shard_map/ppermute | solution.py:12
  278.3 21.5 %collective-permute-done.20 = f32[32,256]{1,0:T(8,128)S(1)} collective-permute-done((f32[32,256]{1,0:T(8,128)S(1)}, f32[32,256]{1,0:T(8,128)S(1)}, u32[]{:S(2)}, u32[]{:S(2)}) %collective-permute-start.20) | collective-permute-done | bytes 32800 | tf_op jit(solution)/shard_map/ppermute | solution.py:12
  303.0 7.3 %collective-permute-done.21 = f32[16,256]{1,0:T(8,128)S(1)} collective-permute-done((f32[16,256]{1,0:T(8,128)S(1)}, f32[16,256]{1,0:T(8,128)S(1)}, u32[]{:S(2)}, u32[]{:S(2)}) %collective-permute-start.21) | collective-permute-done | bytes 16416 | tf_op jit(solution)/shard_map/ppermute | solution.py:12
  318.9 3.2 multiply_reduce_fusion.10
  326.0 3.6 collective-permute-done.23
  332.3 211.7 %all-reduce.3.cloned.1.call-done = f32[256,256]{1,0:T(8,128)} async-done(((f32[256,256]{1,0:T(8,128)}), f32[256,256]{1,0:T(8,128)}) %all-reduce.3.cloned.1.call-update) | async-done | bytes 262160 | tf_op jit(solution)/shard_map/psum | solution.py:97
  556.0 69.7 %all-reduce = (f32[2,2,256]{2,1,0:T(2,128)S(1)}, f32[14,256]{1,0:T(8,128)S(1)}, f32[16,256]{1,0:T(8,128)S(1)}) all-reduce(f32[2,2,256]{2,1,0:T(2,128)S(1)} %pad_maximum_fusion.10, f32[14,256]{1,0:T(8,128)S(1)} %stack.83, f32[16,256]{1,0:T(8,128)S(1)} %fusion.8), channel_id=1, replica_groups=mesh['seq'=32,'batch'=4] {'seq','batch'}, use_global_device_ids=true, to_apply=%region_52.0 | all-reduce | flops 8704 | bytes 69632 | tf_op jit(solution)/shard_map/psum | solution.py:97
  (161 shorter events, 63.0 us)
Async XLA Ops:
  7.2 157.1 %copy-start = (bf16[256,256]{1,0:T(8,128)(2,1)S(1)}, bf16[256,256]{1,0:T(8,128)(2,1)}, u32[]{:S(2)}) copy-start(bf16[256,256]{1,0:T(8,128)(2,1)} %param.12) | copy-start | bytes 393220
  7.2 536.9 %all-reduce.3.cloned.1.call-start = ((), (), s32[]{:S(2)}) async-start(), calls=%async_computation | async-start | bytes 524288 | tf_op jit(solution)/shard_map/psum | solution.py:97
  8.6 4.7 collective-permute-start
  13.5 147.6 %copy-start.1 = (f32[1024,256]{1,0:T(8,128)}, f32[1024,256]{1,0:T(8,128)S(1)}, u32[]{:S(2)}) copy-start(f32[1024,256]{1,0:T(8,128)S(1)} %multiply_add_fusion.38) | copy-start | bytes 3145732
  13.5 4.3 collective-permute-start.1
  18.0 4.3 collective-permute-start.2
  22.6 138.5 %copy-start.3 = (f32[1024,256]{1,0:T(8,128)}, f32[1024,256]{1,0:T(8,128)S(1)}, u32[]{:S(2)}) copy-start(f32[1024,256]{1,0:T(8,128)S(1)} %multiply_add_fusion.34) | copy-start | bytes 3145732
  22.6 4.4 collective-permute-start.3
  26.3 284.1 %copy-start.5 = (f32[1016,256]{1,0:T(8,128)}, f32[1016,256]{1,0:T(8,128)S(1)}, u32[]{:S(2)}) copy-start(f32[1016,256]{1,0:T(8,128)S(1)} %slice.181) | copy-start | bytes 3121156
  27.2 4.8 collective-permute-start.4
  32.1 6.7 %collective-permute-start.5 = (f32[32,256]{1,0:T(8,128)S(1)}, f32[32,256]{1,0:T(8,128)S(1)}, u32[]{:S(2)}, u32[]{:S(2)}) collective-permute-start(f32[32,256]{1,0:T(8,128)S(1)} %slice.184), channel_id=1, source_target_pairs={{0,4},{4,8},{8,12},{12,16},{16,20},{20,24},{24,28},{28,32},{32,36}... | collective-permute-start | bytes 98312 | tf_op jit(solution)/shard_map/ppermute | solution.py:12
  39.0 7.0 %collective-permute-start.6 = (f32[64,256]{1,0:T(8,128)S(1)}, f32[64,256]{1,0:T(8,128)S(1)}, u32[]{:S(2)}, u32[]{:S(2)}) collective-permute-start(f32[64,256]{1,0:T(8,128)S(1)} %slice.186), channel_id=1, source_target_pairs={{0,4},{4,8},{8,12},{12,16},{16,20},{20,24},{24,28},{28,32},{32,36}... | collective-permute-start | bytes 196616 | tf_op jit(solution)/shard_map/ppermute | solution.py:12
  46.2 8.3 %collective-permute-start.7 = (f32[128,256]{1,0:T(8,128)S(1)}, f32[128,256]{1,0:T(8,128)S(1)}, u32[]{:S(2)}, u32[]{:S(2)}) collective-permute-start(f32[128,256]{1,0:T(8,128)S(1)} %slice.188), channel_id=1, source_target_pairs={{0,4},{4,8},{8,12},{12,16},{16,20},{20,24},{24,28},{28,32},{32,36}... | collective-permute-start | bytes 393224 | tf_op jit(solution)/shard_map/ppermute | solution.py:12
  54.7 10.5 %collective-permute-start.8 = (f32[256,256]{1,0:T(8,128)S(1)}, f32[256,256]{1,0:T(8,128)S(1)}, u32[]{:S(2)}, u32[]{:S(2)}) collective-permute-start(f32[256,256]{1,0:T(8,128)S(1)} %slice.190), channel_id=1, source_target_pairs={{0,4},{4,8},{8,12},{12,16},{16,20},{20,24},{24,28},{28,32},{32,36}... | collective-permute-start | bytes 786440 | tf_op jit(solution)/shard_map/ppermute | solution.py:12
  65.4 14.7 %collective-permute-start.9 = (f32[512,256]{1,0:T(8,128)S(1)}, f32[512,256]{1,0:T(8,128)S(1)}, u32[]{:S(2)}, u32[]{:S(2)}) collective-permute-start(f32[512,256]{1,0:T(8,128)S(1)} %get-tuple-element.114), channel_id=1, source_target_pairs={{0,4},{4,8},{8,12},{12,16},{16,20},{20,24},{24,28},{28,32},{32,36}... | collective-permute-start | bytes 1572872 | tf_op jit(solution)/shard_map/ppermute | solution.py:12
  80.2 21.8 %collective-permute-start.10 = (f32[1024,256]{1,0:T(8,128)S(1)}, f32[1024,256]{1,0:T(8,128)S(1)}, u32[]{:S(2)}, u32[]{:S(2)}) collective-permute-start(f32[1024,256]{1,0:T(8,128)S(1)} %multiply_add_fusion.20), channel_id=1, source_target_pairs={{0,4},{4,8},{8,12},{12,16},{16,20},{20,24},{24,28},{28,32},{32,36}... | collective-permute-start | bytes 3145736 | tf_op jit(solution)/shard_map/ppermute | solution.py:12
  102.2 22.7 %collective-permute-start.11 = (f32[1024,256]{1,0:T(8,128)S(1)}, f32[1024,256]{1,0:T(8,128)S(1)}, u32[]{:S(2)}, u32[]{:S(2)}) collective-permute-start(f32[1024,256]{1,0:T(8,128)S(1)} %multiply_add_fusion.18), channel_id=1, source_target_pairs={{0,8},{4,12},{8,16},{12,20},{16,24},{20,28},{24,32},{28,36},{32,40... | collective-permute-start | bytes 3145736 | tf_op jit(solution)/shard_map/ppermute | solution.py:12
  125.0 36.0 %collective-permute-start.12 = (f32[1024,256]{1,0:T(8,128)S(1)}, f32[1024,256]{1,0:T(8,128)S(1)}, u32[]{:S(2)}, u32[]{:S(2)}) collective-permute-start(f32[1024,256]{1,0:T(8,128)S(1)} %multiply_add_fusion.16), channel_id=1, source_target_pairs={{0,16},{4,20},{8,24},{12,28},{16,32},{20,36},{24,40},{28,44},{32,4... | collective-permute-start | bytes 3145736 | tf_op jit(solution)/shard_map/ppermute | solution.py:12
  164.3 149.7 %copy-start.10 = (f32[1024,256]{1,0:T(8,128)}, f32[1024,256]{1,0:T(8,128)S(1)}, u32[]{:S(2)}) copy-start(f32[1024,256]{1,0:T(8,128)S(1)} %multiply_add_fusion.13) | copy-start | bytes 3145732
  165.3 16.1 %collective-permute-start.13 = (f32[1024,256]{1,0:T(8,128)S(1)}, f32[1024,256]{1,0:T(8,128)S(1)}, u32[]{:S(2)}, u32[]{:S(2)}) collective-permute-start(f32[1024,256]{1,0:T(8,128)S(1)} %get-tuple-element.134), channel_id=1, source_target_pairs={{16,0},{20,4},{24,8},{28,12},{32,16},{36,20},{40,24},{44,28},{48,3... | collective-permute-start | bytes 3145736 | tf_op jit(solution)/shard_map/ppermute | solution.py:12
  181.8 17.0 %collective-permute-start.14 = (f32[1024,256]{1,0:T(8,128)S(1)}, f32[1024,256]{1,0:T(8,128)S(1)}, u32[]{:S(2)}, u32[]{:S(2)}) collective-permute-start(f32[1024,256]{1,0:T(8,128)S(1)} %multiply_add_fusion.11), channel_id=1, source_target_pairs={{8,0},{12,4},{16,8},{20,12},{24,16},{28,20},{32,24},{36,28},{40,32... | collective-permute-start | bytes 3145736 | tf_op jit(solution)/shard_map/ppermute | solution.py:12
  201.1 15.5 %collective-permute-start.15 = (f32[1024,256]{1,0:T(8,128)S(1)}, f32[1024,256]{1,0:T(8,128)S(1)}, u32[]{:S(2)}, u32[]{:S(2)}) collective-permute-start(f32[1024,256]{1,0:T(8,128)S(1)} %multiply_add_fusion.10), channel_id=1, source_target_pairs={{4,0},{8,4},{12,8},{16,12},{20,16},{24,20},{28,24},{32,28},{36,32}... | collective-permute-start | bytes 3145736 | tf_op jit(solution)/shard_map/ppermute | solution.py:12
  217.4 20.4 %collective-permute-start.16 = (f32[512,256]{1,0:T(8,128)S(1)}, f32[512,256]{1,0:T(8,128)S(1)}, u32[]{:S(2)}, u32[]{:S(2)}) collective-permute-start(f32[512,256]{1,0:T(8,128)S(1)} %get-tuple-element.113), channel_id=1, source_target_pairs={{4,0},{8,4},{12,8},{16,12},{20,16},{24,20},{28,24},{32,28},{36,32}... | collective-permute-start | bytes 1572872 | tf_op jit(solution)/shard_map/ppermute | solution.py:12
  239.1 10.3 %collective-permute-start.17 = (f32[256,256]{1,0:T(8,128)S(1)}, f32[256,256]{1,0:T(8,128)S(1)}, u32[]{:S(2)}, u32[]{:S(2)}) collective-permute-start(f32[256,256]{1,0:T(8,128)S(1)} %slice.197), channel_id=1, source_target_pairs={{4,0},{8,4},{12,8},{16,12},{20,16},{24,20},{28,24},{32,28},{36,32}... | collective-permute-start | bytes 786440 | tf_op jit(solution)/shard_map/ppermute | solution.py:12
  250.1 14.6 %collective-permute-start.18 = (f32[128,256]{1,0:T(8,128)S(1)}, f32[128,256]{1,0:T(8,128)S(1)}, u32[]{:S(2)}, u32[]{:S(2)}) collective-permute-start(f32[128,256]{1,0:T(8,128)S(1)} %slice.397), channel_id=1, source_target_pairs={{4,0},{8,4},{12,8},{16,12},{20,16},{24,20},{28,24},{32,28},{36,32}... | collective-permute-start | bytes 393224 | tf_op jit(solution)/shard_map/ppermute | solution.py:12
  266.0 10.3 %collective-permute-start.19 = (f32[64,256]{1,0:T(8,128)S(1)}, f32[64,256]{1,0:T(8,128)S(1)}, u32[]{:S(2)}, u32[]{:S(2)}) collective-permute-start(f32[64,256]{1,0:T(8,128)S(1)} %slice.399), channel_id=1, source_target_pairs={{4,0},{8,4},{12,8},{16,12},{20,16},{24,20},{28,24},{32,28},{36,32}... | collective-permute-start | bytes 196616 | tf_op jit(solution)/shard_map/ppermute | solution.py:12
  277.0 22.8 %collective-permute-start.20 = (f32[32,256]{1,0:T(8,128)S(1)}, f32[32,256]{1,0:T(8,128)S(1)}, u32[]{:S(2)}, u32[]{:S(2)}) collective-permute-start(f32[32,256]{1,0:T(8,128)S(1)} %slice.401), channel_id=1, source_target_pairs={{4,0},{8,4},{12,8},{16,12},{20,16},{24,20},{28,24},{32,28},{36,32}... | collective-permute-start | bytes 98312 | tf_op jit(solution)/shard_map/ppermute | solution.py:12
  301.7 8.7 %collective-permute-start.21 = (f32[16,256]{1,0:T(8,128)S(1)}, f32[16,256]{1,0:T(8,128)S(1)}, u32[]{:S(2)}, u32[]{:S(2)}) collective-permute-start(f32[16,256]{1,0:T(8,128)S(1)} %slice.403), channel_id=1, source_target_pairs={{4,0},{8,4},{12,8},{16,12},{20,16},{24,20},{28,24},{32,28},{36,32}... | collective-permute-start | bytes 49160 | tf_op jit(solution)/shard_map/ppermute | solution.py:12
  312.7 6.1 collective-permute-start.22
  323.1 6.4 %collective-permute-start.23 = (f32[4,256]{1,0:T(4,128)S(1)}, f32[4,256]{1,0:T(4,128)S(1)}, u32[]{:S(2)}, u32[]{:S(2)}) collective-permute-start(f32[4,256]{1,0:T(4,128)S(1)} %slice.407), channel_id=1, source_target_pairs={{4,0},{8,4},{12,8},{16,12},{20,16},{24,20},{28,24},{32,28},{36,32}... | collective-permute-start | bytes 12296 | tf_op jit(solution)/shard_map/ppermute | solution.py:12
  331.0 214.8 %collective-permute-start.24 = (f32[2,256]{1,0:T(2,128)S(1)}, f32[2,256]{1,0:T(2,128)S(1)}, u32[]{:S(2)}, u32[]{:S(2)}) collective-permute-start(f32[2,256]{1,0:T(2,128)S(1)} %slice.409), channel_id=1, source_target_pairs={{4,0},{8,4},{12,8},{16,12},{20,16},{24,20},{28,24},{32,28},{36,32}... | collective-permute-start | bytes 6152 | tf_op jit(solution)/shard_map/ppermute | solution.py:12
  549.0 4.6 collective-permute-start.25
  (19 other events, 105.8 us)
Sparse Core Ops, SparseCore 0:
  326.0 217.9 all-reduce.2
where the time goes:
time: 636 us; the launch traced here: 634 us
  waiting for transfers between devices  414 us (65%)
  starting transfers between devices  94.7 us (15%)
  blocking collectives  69.7 us (11%)
  other arithmetic  25.1 us (4%)
  between operations  14.9 us (2%)
  local copies, waits for them, and re-layouts  8.72 us (1%)
  matrix products  7.44 us (1%)
    psum x1, waiting for transfers between devices, per_device(): lax.psum((filter_term, levels_term, embed_term, mix_term), ('seq', 'batch'))  212 us
    ppermute x26, waiting for transfers between devices, passed_along(): lax.ppermute(value, axis, [(source, source + steps) for source in range(l...  202 us
    ppermute x26, starting transfers between devices, passed_along(): lax.ppermute(value, axis, [(source, source + steps) for source in range(l...  94.7 us
    psum x1, blocking collectives, per_device(): lax.psum((filter_term, levels_term, embed_term, mix_term), ('seq', 'batch'))  69.7 us
  transfers between devices with their start and end apart: 27, of which 26 were waited for; matrix products, arithmetic and copies ran while one was open for 2% of the time, Pallas kernels for 0%

commit v1 on v0

v1 whole, which is shorter than its diff:
```python
import functools
import math

import jax
import jax.numpy as jnp
from jax import lax
from jax.experimental import pallas as pl
from jax.experimental.pallas import tpu as pltpu
from jax.sharding import PartitionSpec as P

MESH = pl.DeviceIdType.MESH
F32, BF16 = jnp.float32, jnp.bfloat16
LEVELS = 13
VOCAB = 16
WIDTH = 256
LANES = 128
TOKENS = 1024
BACK = 8
TILES = (BACK + 1) * TOKENS // LANES
NEAR = 56
CLASSES = 136
ROWS = CLASSES * VOCAB


def near_class(level, ones):
    return 1 + level * (level + 1) // 2 + ones


def far_class(shard, ones):
    return NEAR + (shard - 1) * 11 + ones


def far_level(shard):
    return 9 + shard.bit_length()


def dot(a, b):
    return jnp.dot(a, b, preferred_element_type=F32)


def halves(value):
    high = value.astype(BF16)
    return high, (value - high.astype(F32)).astype(BF16)


def ids_kernel(count, ids_ref, out_ref, held, send_sem, recv_sem):
    me = lax.axis_index("seq")
    barrier = pltpu.get_barrier_semaphore()
    for step in range(1, BACK + 1):
        pl.semaphore_signal(
            barrier, inc=1, device_id={"seq": lax.rem(me + count - step, count)}, device_id_type=MESH
        )
    pl.semaphore_wait(barrier, BACK)
    copies = []
    for step in range(1, BACK + 1):
        copy = pltpu.make_async_remote_copy(
            src_ref=ids_ref,
            dst_ref=held.at[step - 1],
            send_sem=send_sem.at[step - 1],
            recv_sem=recv_sem.at[step - 1],
            device_id={"seq": lax.rem(me + step, count)},
            device_id_type=MESH,
        )
        copy.start()
        copies.append(copy)
    out_ref[BACK] = ids_ref[...]
    for step in range(1, BACK + 1):
        copies[step - 1].wait()
        out_ref[BACK - step] = jnp.where(me >= step, held[step - 1], -1)


def window_of_ids(ids, count):
    return pl.pallas_call(
        functools.partial(ids_kernel, count),
        out_shape=jax.ShapeDtypeStruct((BACK + 1, 8, LANES), jnp.int32),
        in_specs=[pl.BlockSpec(memory_space=pltpu.VMEM)],
        out_specs=pl.BlockSpec(memory_space=pltpu.VMEM),
        scratch_shapes=[
            pltpu.VMEM((BACK, 8, LANES), jnp.int32),
            pltpu.SemaphoreType.DMA((BACK,)),
            pltpu.SemaphoreType.DMA((BACK,)),
        ],
        compiler_params=pltpu.CompilerParams(collective_id=0, has_side_effects=True),
    )(ids)


def level_factors(low, high, weights):
    folded = [None] * (LEVELS + 1)
    kappa = [None] * LEVELS
    folded[LEVELS] = weights[LEVELS]
    for level in range(LEVELS - 1, -1, -1):
        kappa[level] = weights[level] * high[1] + low[1] * folded[level + 1]
        folded[level] = weights[level] * high[0] + low[0] * folded[level + 1]
    return folded, kappa


def rows_of(ref):
    return [ref[row : row + 1, :] for row in range(ref.shape[0])]


def make_weights(low, folded, kappa, embed, weights_ref):
    powers = []
    for row in low:
        chain = [jnp.ones_like(row)]
        for _ in range(10):
            chain.append(chain[-1] * row)
        powers.append(chain)

    def passed(level, ones):
        return powers[0][level - ones] * powers[1][ones]

    def put(place, factor):
        high, low_part = halves(factor * embed)
        rows = slice(place * VOCAB, (place + 1) * VOCAB)
        weights_ref[rows, 0:WIDTH] = high
        weights_ref[rows, WIDTH:] = low_part

    put(0, folded[0])
    for level in range(10):
        for ones in range(level + 1):
            put(near_class(level, ones), kappa[level] * passed(level, ones))
    for shard in range(1, 8):
        level = far_level(shard)
        extra = shard.bit_count() - 1
        factor = kappa[level] * powers[0][level - 10 - extra] * powers[1][extra]
        for ones in range(11):
            put(far_class(shard, ones), factor * passed(10, ones))
    weights_ref[(NEAR + 77) * VOCAB :, :] = jnp.zeros(
        ((CLASSES - NEAR - 77) * VOCAB, 2 * WIDTH), BF16
    )
    return powers, passed


def lag_tables():
    place = lax.broadcasted_iota(jnp.int32, (2 * LANES, LANES), 0)
    lag = lax.broadcasted_iota(jnp.int32, (2 * LANES, LANES), 1) - place
    lag = jnp.where(place >= LANES, lag + 2 * LANES, lag)
    inside = (lag >= 0) & (lag < LANES)
    ones = jnp.zeros_like(lag)
    offset = jnp.zeros_like(lag)
    for bit in range(7):
        ones = ones + ((lag >> bit) & 1)
        offset = offset + jnp.where(lag >= 2**bit, bit, 0)
    ones = jnp.where(inside, ones, -1)
    klass = jnp.where(inside, jnp.where(lag == 0, 0, offset + ones), -1)
    return ones, klass


def where_is(table, value):
    return jnp.where(table == value, 1.0, 0.0).astype(BF16)


def make_features(window_ref, tokens_ref, s7, s8, s9, features_ref):
    names = lax.broadcasted_iota(jnp.int32, (VOCAB, LANES), 0)
    tokens_ref[0:VOCAB, LANES:] = jnp.zeros((VOCAB, LANES), BF16)
    for tile in range(TILES):
        row = window_ref[tile // 8, tile % 8 : tile % 8 + 1, :]
        hot = where_is(names, jnp.broadcast_to(row, (VOCAB, LANES)))
        tokens_ref[tile * VOCAB : (tile + 1) * VOCAB, 0:LANES] = hot
        if tile + 1 < TILES:
            tokens_ref[(tile + 1) * VOCAB : (tile + 2) * VOCAB, LANES:] = hot
    ones, klass = lag_tables()
    for pair in range(4):
        table = jnp.concatenate([where_is(ones, 2 * pair), where_is(ones, 2 * pair + 1)], axis=1)
        result = dot(tokens_ref[VOCAB : 71 * VOCAB, :], table).astype(BF16)
        for tile in range(1, 71):
            for half in range(2):
                s7[(2 * pair + half) * VOCAB : (2 * pair + half + 1) * VOCAB, tile * LANES : (tile + 1) * LANES] = (
                    result[(tile - 1) * VOCAB : tile * VOCAB, half * LANES : (half + 1) * LANES]
                )
    own = tokens_ref[64 * VOCAB : 72 * VOCAB, :]
    for first in range(0, 29, 2):
        members = list(range(first, min(first + 2, 29)))
        table = jnp.concatenate([where_is(klass, member) for member in members], axis=1)
        result = dot(own, table).astype(BF16)
        for tile in range(8):
            for half, member in enumerate(members):
                features_ref[member * VOCAB : (member + 1) * VOCAB, tile * LANES : (tile + 1) * LANES] = result[
                    tile * VOCAB : (tile + 1) * VOCAB, half * LANES : (half + 1) * LANES
                ]

    def step(source, level, ones, begin, end):
        span = 2**level
        total = None
        if ones <= level:
            total = source[ones * VOCAB : (ones + 1) * VOCAB, begin:end]
        if ones >= 1:
            late = source[(ones - 1) * VOCAB : ones * VOCAB, begin - span : end - span]
            total = late if total is None else total + late
        return total

    for ones in range(9):
        s8[ones * VOCAB : (ones + 1) * VOCAB, 2 * LANES : 70 * LANES] = step(s7, 7, ones, 2 * LANES, 70 * LANES)
    for ones in range(10):
        s9[ones * VOCAB : (ones + 1) * VOCAB, 4 * LANES : 68 * LANES] = step(s8, 8, ones, 4 * LANES, 68 * LANES)
    for shard in range(1, 8):
        begin = (BACK - shard) * TOKENS
        for ones in range(11):
            place = far_class(shard, ones) * VOCAB
            features_ref[place : place + VOCAB, :] = step(s9, 9, ones, begin, begin + TOKENS)
    home = BACK * TOKENS
    for level, source in ((7, s7), (8, s8), (9, s9)):
        place = near_class(level, 0) * VOCAB
        span = 2**level
        features_ref[place : place + (level + 1) * VOCAB, :] = source[:, home - span : home - span + TOKENS]
    features_ref[(NEAR + 77) * VOCAB :, :] = jnp.zeros(((CLASSES - NEAR - 77) * VOCAB, TOKENS), BF16)


def gelu_parts(y):
    root = math.sqrt(2.0 / math.pi)
    square = y * y
    bend = jnp.tanh(root * (y + 0.044715 * square * y))
    half = 0.5 * (1.0 + bend)
    slope = half + 0.5 * y * (1.0 - bend * bend) * (root * (1.0 + 3 * 0.044715 * square))
    return y * half, slope


def layer_kernel(
    window_ref, embed_ref, low_ref, high_ref, levels_ref, mix_ref, cot_ref,
    out_ref, part_ref,
    tokens_ref, s7, s8, s9, features_ref, weights_ref, turned_ref, g_ref, z_ref,
):
    embed = embed_ref[...]
    low, high, levels = rows_of(low_ref), rows_of(high_ref), rows_of(levels_ref)
    folded, kappa = level_factors(low, high, levels)
    powers, passed = make_weights(low, folded, kappa, embed, weights_ref)
    turned_ref[...] = weights_ref[...].T
    make_features(window_ref, tokens_ref, s7, s8, s9, features_ref)

    first, second = halves(embed)
    third = (embed - first.astype(F32) - second.astype(F32)).astype(BF16)
    table = jnp.concatenate([first, second, third], axis=0)
    mix = mix_ref[...]
    mix_sum = None
    block = 256
    for start in range(0, TOKENS, block):
        span = slice(start, start + block)
        both = dot(turned_ref[...], features_ref[:, span])
        y = (both[:WIDTH] + both[WIDTH:]).T
        active, slope = gelu_parts(y)
        hidden = active.astype(BF16)
        cot = cot_ref[span, :]
        hot = features_ref[0:VOCAB, span]
        x = lax.dot_general(
            jnp.concatenate([hot, hot, hot], axis=0), table, (((0,), (0,)), ((), ())), preferred_element_type=F32
        )
        out_ref[span, :] = x + dot(hidden, mix)
        g_hidden = lax.dot_general(cot, mix, (((1,), (1,)), ((), ())), preferred_element_type=F32)
        g_high, g_low = halves(g_hidden * slope)
        g_ref[span, 0:WIDTH] = g_high
        g_ref[span, WIDTH:] = g_low
        term = lax.dot_general(hidden, cot, (((0,), (0,)), ((), ())), preferred_element_type=F32)
        mix_sum = term if mix_sum is None else mix_sum + term

    for chunk in range(8):
        for tile in range(8):
            row = 32 * chunk + 8 * (tile // 2)
            column = LANES * (tile % 2)
            part_ref[chunk, tile] = mix_sum[row : row + 8, column : column + LANES]

    both = dot(features_ref[...], g_ref[...])
    z_ref[...] = both[:, :WIDTH] + both[:, WIDTH:]

    def z_of(place):
        return z_ref[place * VOCAB : (place + 1) * VOCAB, :]

    def group(terms):
        total = counted = None
        for ones, factor, place in terms:
            term = factor * z_of(place)
            total = term if total is None else total + term
            if ones:
                more = term * float(ones)
                counted = more if counted is None else counted + more
        return total, jnp.zeros_like(total) if counted is None else counted

    totals = []
    for level in range(10):
        totals.append(group([(n, passed(level, n), near_class(level, n)) for n in range(level + 1)]))
    for level in range(10, LEVELS):
        total = counted = None
        for shard in range(2 ** (level - 10), 2 ** (level - 9)):
            extra = shard.bit_count() - 1
            factor = powers[0][level - 10 - extra] * powers[1][extra]
            part, part_counted = group([(n, passed(10, n), far_class(shard, n)) for n in range(11)])
            part_counted = factor * (part_counted + float(extra) * part)
            part = factor * part
            total = part if total is None else total + part
            counted = part_counted if counted is None else counted + part_counted
        totals.append((total, counted))

    def over_names(value):
        return jnp.sum(embed * value, axis=0, keepdims=True)

    z0 = z_of(0)
    rows = [over_names(z0)]
    embed_sum = folded[0] * z0 + dot(features_ref[0:VOCAB, :], cot_ref[...])
    zero_sum = one_sum = jnp.zeros_like(z0)
    for level, (total, counted) in enumerate(totals):
        rows.append(over_names(total))
        embed_sum = embed_sum + kappa[level] * total
        one_sum = one_sum + kappa[level] * counted
        zero_sum = zero_sum + kappa[level] * (float(level) * total - counted)
    rows += [over_names(zero_sum), over_names(one_sum)]
    small = jnp.concatenate(rows + [embed_sum], axis=0)
    for chunk in range(8):
        row, column = 8 * (chunk // 2), LANES * (chunk % 2)
        part_ref[chunk, 8] = small[row : row + 8, column : column + LANES]


def layer(window, embed, low, high, levels, mix, cot):
    vmem = pl.BlockSpec(memory_space=pltpu.VMEM)
    return pl.pallas_call(
        layer_kernel,
        out_shape=(
            jax.ShapeDtypeStruct((TOKENS, WIDTH), F32),
            jax.ShapeDtypeStruct((8, 9, 8, LANES), F32),
        ),
        in_specs=[vmem] * 7,
        out_specs=(vmem, vmem),
        scratch_shapes=[
            pltpu.VMEM((TILES * VOCAB, 2 * LANES), BF16),
            pltpu.VMEM((8 * VOCAB, TILES * LANES), BF16),
            pltpu.VMEM((9 * VOCAB, TILES * LANES), BF16),
            pltpu.VMEM((10 * VOCAB, TILES * LANES), BF16),
            pltpu.VMEM((ROWS, TOKENS), BF16),
            pltpu.VMEM((ROWS, 2 * WIDTH), BF16),
            pltpu.VMEM((2 * WIDTH, ROWS), BF16),
            pltpu.VMEM((TOKENS, 2 * WIDTH), BF16),
            pltpu.VMEM((ROWS, WIDTH), F32),
        ],
        compiler_params=pltpu.CompilerParams(vmem_limit_bytes=56 * 2**20),
    )(window, embed, low, high, levels, mix, cot)


def sum_kernel(
    scale, part_ref, low_ref, high_ref, levels_ref,
    mix_ref, filters_ref, grad_levels_ref, embed_ref,
    near, mine, far, gathered, whole, sends, recvs,
):
    seq, batch = lax.axis_index("seq"), lax.axis_index("batch")
    column, core = lax.rem(seq, 4), lax.rem(batch, 2)
    outer_seq, outer_batch = lax.div(seq, 4), lax.div(batch, 2)
    near_rank = column * 2 + core
    far_rank = outer_seq * 2 + outer_batch

    def near_peer(step):
        rank = lax.rem(near_rank + step, 8)
        return rank, (outer_seq * 4 + lax.div(rank, 2), outer_batch * 2 + lax.rem(rank, 2))

    def far_peer(step):
        rank = lax.rem(far_rank + step, 16)
        return rank, (lax.div(rank, 2) * 4 + column, lax.rem(rank, 2) * 2 + core)

    barrier = pltpu.get_barrier_semaphore()
    for step in range(1, 8):
        pl.semaphore_signal(barrier, inc=1, device_id=near_peer(step)[1], device_id_type=MESH)
    for step in range(1, 16):
        pl.semaphore_signal(barrier, inc=1, device_id=far_peer(step)[1], device_id_type=MESH)
    pl.semaphore_wait(barrier, 22)

    def send(source, target, phase, step, peer):
        copy = pltpu.make_async_remote_copy(
            src_ref=source,
            dst_ref=target,
            send_sem=sends.at[phase, step],
            recv_sem=recvs.at[phase, step],
            device_id=peer,
            device_id_type=MESH,
        )
        copy.start()
        return copy

    copies = []
    for step in range(1, 8):
        rank, peer = near_peer(step)
        copies.append(send(part_ref.at[rank], near.at[step - 1], 0, step, peer))
    total = part_ref[near_rank]
    for step in range(1, 8):
        copies[step - 1].wait()
        total = total + near[step - 1]

    for half in range(16):
        mine[half, 0] = total[half // 2, 4 * (half % 2) : 4 * (half % 2) + 4]
        mine[half, 1] = total[8, 0:4]
        mine[half, 2] = total[8, 4:8]
    copies = []
    for step in range(1, 16):
        rank, peer = far_peer(step)
        copies.append(send(mine.at[rank], far.at[step - 1], 1, step, peer))
    total = mine[far_rank]
    for step in range(1, 16):
        copies[step - 1].wait()
        total = total + far[step - 1]

    gathered[far_rank] = total[0]
    copies = []
    for step in range(1, 16):
        copies.append(send(gathered.at[far_rank], gathered.at[far_rank], 2, step, far_peer(step)[1]))
    whole[near_rank, 8] = jnp.concatenate([total[1], total[2]], axis=0)
    for copy in copies:
        copy.wait()
    for tile in range(8):
        whole[near_rank, tile] = jnp.concatenate([gathered[2 * tile], gathered[2 * tile + 1]], axis=0)
    copies = []
    for step in range(1, 8):
        copies.append(send(whole.at[near_rank], whole.at[near_rank], 3, step, near_peer(step)[1]))
    for copy in copies:
        copy.wait()

    for chunk in range(8):
        for tile in range(8):
            row = 32 * chunk + 8 * (tile // 2)
            start = LANES * (tile % 2)
            mix_ref[row : row + 8, start : start + LANES] = scale * whole[chunk, tile]
    quarters = [
        scale * jnp.concatenate([whole[2 * quarter, 8], whole[2 * quarter + 1, 8]], axis=1)
        for quarter in range(4)
    ]
    embed_ref[0:8, :] = quarters[2]
    embed_ref[8:16, :] = quarters[3]
    shifted = [quarters[row // 8][row % 8 : row % 8 + 1] for row in range(1, 14)]
    zero_inner, one_inner = quarters[1][6:7], quarters[1][7:8]
    low, high, levels = rows_of(low_ref), rows_of(high_ref), rows_of(levels_ref)
    folded, _ = level_factors(low, high, levels)
    current = quarters[0][0:1]
    low_zero, low_one = zero_inner / low[0], one_inner / low[1]
    high_zero = high_one = jnp.zeros_like(current)
    for level in range(LEVELS):
        late = shifted[level]
        grad_levels_ref[level : level + 1, :] = high[0] * current + high[1] * late
        low_zero = low_zero + folded[level + 1] * current
        low_one = low_one + folded[level + 1] * late
        high_zero = high_zero + levels[level] * current
        high_one = high_one + levels[level] * late
        current = low[0] * current + low[1] * late
    grad_levels_ref[LEVELS : LEVELS + 1, :] = current
    filters_ref[0, 0:1, :] = low_zero
    filters_ref[0, 1:2, :] = low_one
    filters_ref[1, 0:1, :] = high_zero
    filters_ref[1, 1:2, :] = high_one


def summed(scale, part, low, high, levels):
    vmem = pl.BlockSpec(memory_space=pltpu.VMEM)
    return pl.pallas_call(
        functools.partial(sum_kernel, scale),
        out_shape=(
            jax.ShapeDtypeStruct((WIDTH, WIDTH), F32),
            jax.ShapeDtypeStruct((2, 2, WIDTH), F32),
            jax.ShapeDtypeStruct((LEVELS + 1, WIDTH), F32),
            jax.ShapeDtypeStruct((VOCAB, WIDTH), F32),
        ),
        in_specs=[vmem] * 4,
        out_specs=(vmem,) * 4,
        scratch_shapes=[
            pltpu.VMEM((7, 9, 8, LANES), F32),
            pltpu.VMEM((16, 3, 4, LANES), F32),
            pltpu.VMEM((15, 3, 4, LANES), F32),
            pltpu.VMEM((16, 4, LANES), F32),
            pltpu.VMEM((8, 9, 8, LANES), F32),
            pltpu.SemaphoreType.DMA((4, 16)),
            pltpu.SemaphoreType.DMA((4, 16)),
        ],
        compiler_params=pltpu.CompilerParams(collective_id=1, has_side_effects=True),
    )(part, low, high, levels)


def per_device(ids, embed, low_filter, high_filter, level_weights, mix, cotangent):
    count = lax.axis_size("seq")
    window = window_of_ids(ids.reshape(8, LANES), count)
    out, part = layer(window, embed, low_filter, high_filter, level_weights, mix, cotangent[0])
    scale = 1.0 / math.sqrt(count * lax.axis_size("batch") * TOKENS)
    grad_mix, grad_filters, grad_levels, grad_embed = summed(
        scale, part, low_filter, high_filter, level_weights
    )
    return out[None], grad_filters, grad_levels, grad_mix, grad_embed


def solution(mesh):
    placed = (P("batch", "seq"), P(), P(), P(), P(), P(), P("batch", "seq", None))
    return jax.shard_map(
        per_device,
        mesh=mesh,
        in_specs=placed,
        out_specs=(P("batch", "seq", None), P(), P(), P(), P()),
        check_vma=False,
    )
```

time: 636 us -> 58.9 us (0.09)
  waiting for transfers between devices: 414 us -> 0 us
  starting transfers between devices: 94.7 us -> 0 us
  blocking collectives: 69.7 us -> 0 us
  Pallas kernels: 0 us -> 53 us
  other arithmetic: 25.1 us -> 0 us
  between operations: 14.9 us -> 0.66 us
  matrix products: 7.44 us -> 0 us
    psum x1 -> x0, waiting for transfers between devices: 212 us -> none  [per_device(): lax.psum((filter_term, levels_term, embed_term, mix_term), ('seq', 'batch'))]
    ppermute x26 -> x0, waiting for transfers between devices: 202 us -> none  [passed_along(): lax.ppermute(value, axis, [(source, source + steps) for source in range(l...]
    ppermute x26 -> x0, starting transfers between devices: 94.7 us -> none  [passed_along(): lax.ppermute(value, axis, [(source, source + steps) for source in range(l...]
    psum x1 -> x0, blocking collectives: 69.7 us -> none  [per_device(): lax.psum((filter_term, levels_term, embed_term, mix_term), ('seq', 'batch'))]
    pallas_call x0 -> x3, Pallas kernels: none -> 53 us  [the longest x1 26.7 us: summed(): pl.pallas_call(functools.partial(sum_kernel, scale), out_shape=(jax.Shape...]
    reduce_sum x10 -> x0, other arithmetic: 12.4 us -> none  [the longest x5 8.75 us: per_device(): level_rows[level] = jnp.sum(g_y * detail, axis=0)]
    add x29 -> x0, other arithmetic: 9.17 us -> none  [the longest x12 4.06 us: per_device(): back = low_filter[1] * g_a + high_filter[1] * g_detail]
    dot_general x5 -> x0, matrix products: 7.44 us -> none  [the longest x1 2.33 us: per_device(): lax.dot_general(onehot, g_x, (((0,), (0,)), ((), ())), precision=lax.Prec...]
  transfers between devices with their start and end apart: 27 -> 0, of which waited for: 26 -> 0; matrix products, arithmetic and copies ran while one was open for 2% -> 0% of each run, Pallas kernels for 0% -> 0%
where the time goes in v1:
time: 58.9 us; the launch traced here: 58.6 us
  Pallas kernels  53 us (90%)
  local copies, waits for them, and re-layouts  4.86 us (8%)
  between operations  0.66 us (1%)
    pallas_call x1, Pallas kernels, summed(): pl.pallas_call(functools.partial(sum_kernel, scale), out_shape=(jax.Shape...  26.7 us
    pallas_call x1, Pallas kernels, window_of_ids(): pl.pallas_call(functools.partial(ids_kernel, count), out_shape=jax.ShapeD...  13.8 us
    pallas_call x1, Pallas kernels, layer(): pl.pallas_call(layer_kernel, out_shape=(jax.ShapeDtypeStruct((TOKENS, WID...  12.6 us
    unnamed x8, local copies, waits for them, and re-layouts  4.86 us

profile of v1, /device:TPU:1, one launch (start us, length us, event | category | flops | bytes accessed | tf_op | source)
XLA Modules:
  0.0 58.6 jit_solution(764207791870071087)
XLA Ops:
  0.6 13.8 %shard_map.110.window_ref = s32[9,8,128]{2,1,0:T(8,128)} custom-call(s32[8,128]{1,0:T(8,128)} %bitcast.4), custom_call_target="tpu_custom_call" | custom-call | tf_op jit(solution)/shard_map/pallas_call | solution.py:73
  14.4 12.6 %shard_map.111 = (f32[1024,256]{1,0:T(8,128)}, f32[8,9,8,128]{3,2,1,0:T(8,128)}) custom-call(s32[9,8,128]{2,1,0:T(8,128)} %shard_map.110.window_ref, f32[16,256]{1,0:T(8,128)} %embed_ref.1, f32[2,256]{1,0:T(2,128)} %low_ref.3, f32[2,256]{1,0:T(2,128)} %high_ref.3, f32[14,256]{1,0:T(8,128)} %levels_ref.3, bf16[256,256]{1,0:T(8,128)(2,1)} %mix_ref.1, ...), custom_call_target="tpu_custom_call" | custom-call | tf_op jit(solution)/shard_map/pallas_call | solution.py:313
  27.0 26.7 %shard_map.112 = (f32[256,256]{1,0:T(8,128)}, f32[2,2,256]{2,1,0:T(2,128)}, f32[14,256]{1,0:T(8,128)}, f32[16,256]{1,0:T(8,128)}) custom-call(f32[8,9,8,128]{3,2,1,0:T(8,128)} %get-tuple-element.12.part_ref, f32[2,256]{1,0:T(2,128)} %low_ref.3, f32[2,256]{1,0:T(2,128)} %high_ref.3, f32[14,256]{1,0:T(8,128)} %levels_ref.3), custom_call_target="tpu_custom_call" | custom-call | tf_op jit(solution)/shard_map/pallas_call | solution.py:446
  53.7 0.0 copy-start.1
  53.7 0.7 %copy-done.1 = f32[2,2,256]{2,1,0:T(2,128)S(1)} copy-done((f32[2,2,256]{2,1,0:T(2,128)S(1)}, f32[2,2,256]{2,1,0:T(2,128)}, u32[]{:S(2)}) %copy-start.1) | copy-done | bytes 4120
  54.4 0.6 %copy.16 = f32[2,2,256]{2,1,0:T(2,128)} copy(f32[2,2,256]{2,1,0:T(2,128)S(1)} %copy-done.1) | data formatting | bytes 8192
  54.9 1.3 %copy.17 = f32[14,256]{1,0:T(8,128)} copy(f32[14,256]{1,0:T(8,128)} %get-tuple-element.24) | data formatting | bytes 28672
  56.3 0.0 copy-start
  56.3 1.7 %copy.18 = f32[256,256]{1,0:T(8,128)} copy(f32[256,256]{1,0:T(8,128)} %get-tuple-element.25) | data formatting | bytes 524288
  58.0 0.0 copy-done
  58.0 0.6 %copy.19 = f32[16,256]{1,0:T(8,128)} copy(f32[16,256]{1,0:T(8,128)S(1)} %copy-done) | data formatting | bytes 32768
Async XLA Ops:
  53.7 0.7 %copy-start.1 = (f32[2,2,256]{2,1,0:T(2,128)S(1)}, f32[2,2,256]{2,1,0:T(2,128)}, u32[]{:S(2)}) copy-start(f32[2,2,256]{2,1,0:T(2,128)} %get-tuple-element.23) | copy-start | bytes 12292
  56.3 1.7 %copy-start = (f32[16,256]{1,0:T(8,128)S(1)}, f32[16,256]{1,0:T(8,128)}, u32[]{:S(2)}) copy-start(f32[16,256]{1,0:T(8,128)} %get-tuple-element.26) | copy-start | bytes 49156

commit v2 on v0

v2 whole, which is shorter than its diff:
```python
import functools
import math

import jax
import jax.numpy as jnp
from jax import lax
from jax.experimental import pallas as pl
from jax.experimental.pallas import tpu as pltpu
from jax.sharding import PartitionSpec as P

MESH = pl.DeviceIdType.MESH
F32, BF16 = jnp.float32, jnp.bfloat16
LEVELS = 13
VOCAB = 16
WIDTH = 256
LANES = 128
TOKENS = 1024
BACK = 8
TILES = (BACK + 1) * TOKENS // LANES
CLASSES = 1 + LEVELS * (LEVELS + 1) // 2
ROWS = 96 * VOCAB


def class_of(level, ones):
    return 1 + level * (level + 1) // 2 + ones


def block_of(level, ones):
    return slice(class_of(level, ones) * VOCAB, (class_of(level, ones) + 1) * VOCAB)


def dot(a, b):
    return jnp.dot(a, b, preferred_element_type=F32)


def halves(value):
    high = value.astype(BF16)
    return high, (value - high.astype(F32)).astype(BF16)


def level_factors(low, high, weights):
    folded = [None] * (LEVELS + 1)
    kappa = [None] * LEVELS
    folded[LEVELS] = weights[LEVELS]
    for level in range(LEVELS - 1, -1, -1):
        kappa[level] = weights[level] * high[1] + low[1] * folded[level + 1]
        folded[level] = weights[level] * high[0] + low[0] * folded[level + 1]
    return folded, kappa


def rows_of(ref):
    return [ref[row : row + 1, :] for row in range(ref.shape[0])]


def lag_weights(low):
    chains = []
    for row in low:
        chain = [jnp.ones_like(row)]
        for _ in range(LEVELS - 1):
            chain.append(chain[-1] * row)
        chains.append(chain)
    return lambda level, ones: chains[0][level - ones] * chains[1][ones]


def make_weights(passed, folded, kappa, embed, weights_ref):
    def put(rows, factor):
        high, rest = halves(factor * embed)
        weights_ref[rows, 0:WIDTH] = high
        weights_ref[rows, WIDTH:] = rest

    put(slice(0, VOCAB), folded[0])
    for level in range(LEVELS):
        for ones in range(level + 1):
            put(block_of(level, ones), kappa[level] * passed(level, ones))
    weights_ref[CLASSES * VOCAB :, :] = jnp.zeros((ROWS - CLASSES * VOCAB, 2 * WIDTH), BF16)


def where_is(table, value):
    return jnp.where(table == value, 1.0, 0.0).astype(BF16)


def make_tables(ones_ref, class_ref):
    place = lax.broadcasted_iota(jnp.int32, (2 * LANES, LANES), 0)
    lag = lax.broadcasted_iota(jnp.int32, (2 * LANES, LANES), 1) - place
    lag = jnp.where(place >= LANES, lag + 2 * LANES, lag)
    inside = (lag >= 0) & (lag < LANES)
    ones = jnp.zeros_like(lag)
    offset = jnp.zeros_like(lag)
    for bit in range(7):
        ones = ones + ((lag >> bit) & 1)
        offset = offset + jnp.where(lag >= 2**bit, bit, 0)
    klass = jnp.where(inside, jnp.where(lag == 0, 0, offset + ones), -1)
    ones = jnp.where(inside, ones, -1)
    for value in range(8):
        ones_ref[:, value * LANES : (value + 1) * LANES] = where_is(ones, value)
    for value in range(29):
        class_ref[:, value * LANES : (value + 1) * LANES] = where_is(klass, value)


def make_hot(tokens_ref, first, ids):
    names = lax.broadcasted_iota(jnp.int32, (VOCAB, LANES), 0)
    for row in range(8):
        tile = first + row
        hot = where_is(names, jnp.broadcast_to(ids[row : row + 1, :], (VOCAB, LANES)))
        tokens_ref[tile * VOCAB : (tile + 1) * VOCAB, 0:LANES] = hot
        if tile + 1 < TILES:
            tokens_ref[(tile + 1) * VOCAB : (tile + 2) * VOCAB, LANES:] = hot


def make_near(tokens_ref, class_ref, features_ref):
    own = tokens_ref[64 * VOCAB : 72 * VOCAB, :]
    for first in range(0, 29, 2):
        members = range(first, min(first + 2, 29))
        result = dot(own, class_ref[:, first * LANES : (first + len(members)) * LANES]).astype(BF16)
        for tile in range(8):
            for half, member in enumerate(members):
                features_ref[member * VOCAB : (member + 1) * VOCAB, tile * LANES : (tile + 1) * LANES] = result[
                    tile * VOCAB : (tile + 1) * VOCAB, half * LANES : (half + 1) * LANES
                ]


def make_far(tokens_ref, ones_ref, s7, s8, s9, s10, features_ref):
    for pair in range(4):
        result = dot(
            tokens_ref[VOCAB : 71 * VOCAB, :], ones_ref[:, 2 * pair * LANES : 2 * (pair + 1) * LANES]
        ).astype(BF16)
        for tile in range(1, 71):
            for half in range(2):
                value = 2 * pair + half
                s7[value * VOCAB : (value + 1) * VOCAB, tile * LANES : (tile + 1) * LANES] = result[
                    (tile - 1) * VOCAB : tile * VOCAB, half * LANES : (half + 1) * LANES
                ]

    def step(source, level, ones, begin, end):
        span = 2**level
        total = None
        if 0 <= ones <= level:
            total = source[ones * VOCAB : (ones + 1) * VOCAB, begin:end]
        if 1 <= ones <= level + 1:
            late = source[(ones - 1) * VOCAB : ones * VOCAB, begin - span : end - span]
            total = late if total is None else total + late
        return total

    def both(one, other):
        if one is None or other is None:
            return other if one is None else one
        return one + other

    for ones in range(9):
        s8[ones * VOCAB : (ones + 1) * VOCAB, 2 * LANES : 70 * LANES] = step(s7, 7, ones, 2 * LANES, 70 * LANES)
    for ones in range(10):
        s9[ones * VOCAB : (ones + 1) * VOCAB, 4 * LANES : 68 * LANES] = step(s8, 8, ones, 4 * LANES, 68 * LANES)
    for ones in range(11):
        s10[ones * VOCAB : (ones + 1) * VOCAB, 8 * LANES : 64 * LANES] = step(s9, 9, ones, 8 * LANES, 64 * LANES)
    home = BACK * TOKENS
    for level, source in ((7, s7), (8, s8), (9, s9), (10, s10)):
        rows = slice(class_of(level, 0) * VOCAB, class_of(level + 1, 0) * VOCAB)
        begin = home - 2**level
        features_ref[rows, :] = source[:, begin : begin + TOKENS]
    for ones in range(12):
        begin = home - 2048
        features_ref[block_of(11, ones), :] = step(s10, 10, ones, begin, begin + TOKENS)
    for ones in range(13):
        begin = home - 4096
        near = step(s10, 10, ones, begin, begin + TOKENS)
        late = step(s10, 10, ones - 1, begin - 2048, begin - 2048 + TOKENS)
        features_ref[block_of(12, ones), :] = both(near, late)
    features_ref[CLASSES * VOCAB :, :] = jnp.zeros((ROWS - CLASSES * VOCAB, TOKENS), BF16)


def gelu_parts(y):
    root = math.sqrt(2.0 / math.pi)
    square = y * y
    bend = jnp.tanh(root * (y + 0.044715 * square * y))
    half = 0.5 * (1.0 + bend)
    slope = half + 0.5 * y * (1.0 - bend * bend) * (root * (1.0 + 3 * 0.044715 * square))
    return y * half, slope


def forward(turned_ref, features_ref, mix_ref, cot_ref, hidden_ref, g_ref):
    mix = mix_ref[...]
    mix_sum = None
    block = 256
    for start in range(0, TOKENS, block):
        span = slice(start, start + block)
        both = dot(turned_ref[...], features_ref[:, span])
        y = (both[:WIDTH] + both[WIDTH:]).T
        active, slope = gelu_parts(y)
        hidden = active.astype(BF16)
        hidden_ref[span, :] = hidden
        cot = cot_ref[span, :]
        g_hidden = lax.dot_general(cot, mix, (((1,), (1,)), ((), ())), preferred_element_type=F32)
        g_high, g_rest = halves(g_hidden * slope)
        g_ref[span, 0:WIDTH] = g_high
        g_ref[span, WIDTH:] = g_rest
        term = lax.dot_general(hidden, cot, (((0,), (0,)), ((), ())), preferred_element_type=F32)
        mix_sum = term if mix_sum is None else mix_sum + term
    return mix_sum


def backward(passed, folded, kappa, embed, features_ref, g_ref, cot_ref, z_ref):
    both = dot(features_ref[0 : CLASSES * VOCAB, :], g_ref[...])
    z_ref[...] = both[:, :WIDTH] + both[:, WIDTH:]

    def over_names(value):
        return jnp.sum(embed * value, axis=0, keepdims=True)

    z0 = z_ref[0:VOCAB, :]
    rows = [over_names(z0)]
    embed_sum = folded[0] * z0 + dot(features_ref[0:VOCAB, :], cot_ref[...])
    zero_sum = one_sum = jnp.zeros_like(z0)
    for level in range(LEVELS):
        total = passed(level, 0) * z_ref[block_of(level, 0), :]
        counted = jnp.zeros_like(total)
        for ones in range(1, level + 1):
            term = passed(level, ones) * z_ref[block_of(level, ones), :]
            total = total + term
            counted = counted + float(ones) * term
        rows.append(over_names(total))
        embed_sum = embed_sum + kappa[level] * total
        one_sum = one_sum + kappa[level] * counted
        zero_sum = zero_sum + kappa[level] * (float(level) * total - counted)
    rows += [over_names(zero_sum), over_names(one_sum)]
    return jnp.concatenate(rows + [embed_sum], axis=0)


def layer_kernel(
    count, ids_ref, embed_ref, low_ref, high_ref, levels_ref, mix_ref, cot_ref,
    hidden_ref, whole,
    held, ids_send, ids_recv, ones_ref, class_ref, tokens_ref, s7, s8, s9, s10, features_ref, weights_ref, turned_ref,
    g_ref, z_ref, part, sibling, halved, first, second, third, sends, recvs,
):
    seq, batch = lax.axis_index("seq"), lax.axis_index("batch")
    x, y = lax.rem(seq, 4), lax.rem(lax.div(seq, 4), 4)
    core = lax.rem(batch, 2)
    z = lax.div(seq, 16) * 2 + lax.div(batch, 2)

    def device(x, y, z, core):
        return lax.div(z, 2) * 16 + y * 4 + x, lax.rem(z, 2) * 2 + core

    spots = (x + core * (y - x), y + core * (z - y), z + core * (x - z))

    def peer_of(axis, step):
        spot = list(spots)
        spot[axis] = lax.rem(spots[axis] + step, 4)
        a, b, c = spot
        return device(a + core * (c - a), b + core * (a - b), c + core * (b - c), core)

    other = device(x, y, z, 1 - core)
    barrier = pltpu.get_barrier_semaphore()

    def greet(peer):
        pl.semaphore_signal(barrier, inc=1, device_id=peer, device_id_type=MESH)

    for step in range(1, BACK + 1):
        greet((lax.rem(seq + count - step, count), batch))
    greet(other)
    for axis in range(3):
        for step in range(1, 4):
            greet(peer_of(axis, step))
    pl.semaphore_wait(barrier, BACK + 10)

    def copy_to(source, target, sent, received, peer):
        copy = pltpu.make_async_remote_copy(
            src_ref=source, dst_ref=target, send_sem=sent, recv_sem=received, device_id=peer, device_id_type=MESH
        )
        copy.start()
        return copy

    id_copies = [
        copy_to(
            ids_ref, held.at[step], ids_send.at[step], ids_recv.at[step], (lax.rem(seq + step + 1, count), batch)
        )
        for step in range(BACK)
    ]

    embed = embed_ref[...]
    low, high, levels = rows_of(low_ref), rows_of(high_ref), rows_of(levels_ref)
    folded, kappa = level_factors(low, high, levels)
    passed = lag_weights(low)
    make_weights(passed, folded, kappa, embed, weights_ref)
    turned_ref[...] = weights_ref[...].T
    make_tables(ones_ref, class_ref)
    tokens_ref[0:VOCAB, LANES:] = jnp.zeros((VOCAB, LANES), BF16)
    make_hot(tokens_ref, 8 * BACK, ids_ref[...])
    for step in range(BACK):
        id_copies[step].wait()
        make_hot(tokens_ref, 8 * (BACK - 1 - step), jnp.where(seq > step, held[step], -1))
    make_near(tokens_ref, class_ref, features_ref)
    make_far(tokens_ref, ones_ref, s7, s8, s9, s10, features_ref)
    mix_sum = forward(turned_ref, features_ref, mix_ref, cot_ref, hidden_ref, g_ref)
    small = backward(passed, folded, kappa, embed, features_ref, g_ref, cot_ref, z_ref)

    for chunk in range(8):
        for tile in range(8):
            row = 32 * chunk + 8 * (tile // 2)
            column = LANES * (tile % 2)
            part[chunk, tile] = mix_sum[row : row + 8, column : column + LANES]
        row, column = 8 * (chunk // 2), LANES * (chunk % 2)
        part[chunk, 8] = small[row : row + 8, column : column + LANES]

    copy_to(
        part.at[pl.ds(4 * (1 - core), 4)], sibling, sends.at[0, 0], recvs.at[0, 0], other
    ).wait()
    for chunk in range(4):
        halved[chunk] = part[4 * core + chunk] + sibling[chunk]

    def exchange(phase, axis, source_of, target):
        copies = [
            copy_to(source_of(step), target.at[spots[axis]], sends.at[phase, step], recvs.at[phase, step], peer_of(axis, step))
            for step in range(1, 4)
        ]
        for copy in copies:
            copy.wait()

    first[spots[0]] = halved[spots[0]]
    exchange(1, 0, lambda step: halved.at[lax.rem(spots[0] + step, 4)], first)
    second[spots[1]] = (first[0] + first[1]) + (first[2] + first[3])
    exchange(2, 1, lambda step: second.at[spots[1]], second)
    third[spots[2]] = (second[0] + second[1]) + (second[2] + second[3])
    exchange(3, 2, lambda step: third.at[spots[2]], third)
    mine = 4 * core + spots[0]
    whole[mine] = (third[0] + third[1]) + (third[2] + third[3])
    copies = [
        copy_to(whole.at[mine], whole.at[mine], sends.at[4, step], recvs.at[4, step], peer_of(0, step))
        for step in range(1, 4)
    ]
    for copy in copies:
        copy.wait()
    ours = whole.at[pl.ds(4 * core, 4)]
    copy_to(ours, ours, sends.at[5, 0], recvs.at[5, 0], other).wait()


def layer(count, ids, embed, low, high, levels, mix, cot):
    vmem = pl.BlockSpec(memory_space=pltpu.VMEM)
    chunk = (9, 8, LANES)
    return pl.pallas_call(
        functools.partial(layer_kernel, count),
        out_shape=(
            jax.ShapeDtypeStruct((TOKENS, WIDTH), BF16),
            jax.ShapeDtypeStruct((8,) + chunk, F32),
        ),
        in_specs=[vmem] * 7,
        out_specs=(vmem, vmem),
        scratch_shapes=[
            pltpu.VMEM((BACK, 8, LANES), jnp.int32),
            pltpu.SemaphoreType.DMA((BACK,)),
            pltpu.SemaphoreType.DMA((BACK,)),
            pltpu.VMEM((2 * LANES, 8 * LANES), BF16),
            pltpu.VMEM((2 * LANES, 29 * LANES), BF16),
            pltpu.VMEM((TILES * VOCAB, 2 * LANES), BF16),
            pltpu.VMEM((8 * VOCAB, TILES * LANES), BF16),
            pltpu.VMEM((9 * VOCAB, TILES * LANES), BF16),
            pltpu.VMEM((10 * VOCAB, TILES * LANES), BF16),
            pltpu.VMEM((11 * VOCAB, TILES * LANES), BF16),
            pltpu.VMEM((ROWS, TOKENS), BF16),
            pltpu.VMEM((ROWS, 2 * WIDTH), BF16),
            pltpu.VMEM((2 * WIDTH, ROWS), BF16),
            pltpu.VMEM((TOKENS, 2 * WIDTH), BF16),
            pltpu.VMEM((CLASSES * VOCAB, WIDTH), F32),
            pltpu.VMEM((8,) + chunk, F32),
            pltpu.VMEM((4,) + chunk, F32),
            pltpu.VMEM((4,) + chunk, F32),
            pltpu.VMEM((4,) + chunk, F32),
            pltpu.VMEM((4,) + chunk, F32),
            pltpu.VMEM((4,) + chunk, F32),
            pltpu.SemaphoreType.DMA((6, 4)),
            pltpu.SemaphoreType.DMA((6, 4)),
        ],
        compiler_params=pltpu.CompilerParams(
            collective_id=0, has_side_effects=True, vmem_limit_bytes=56 * 2**20
        ),
    )(ids, embed, low, high, levels, mix, cot)


def finish_kernel(
    scale, ids_ref, hidden_ref, whole, embed_in_ref, mix_in_ref, low_ref, high_ref, levels_ref,
    out_ref, filters_ref, grad_levels_ref, mix_ref, embed_ref,
):
    embed = embed_in_ref[...]
    high_part, middle = halves(embed)
    rest = (embed - high_part.astype(F32) - middle.astype(F32)).astype(BF16)
    table = jnp.concatenate([high_part, middle, rest], axis=0)
    names = lax.broadcasted_iota(jnp.int32, (VOCAB, LANES), 0)
    for tile in range(8):
        rows = slice(tile * LANES, (tile + 1) * LANES)
        hot = where_is(names, jnp.broadcast_to(ids_ref[tile : tile + 1, :], (VOCAB, LANES)))
        hot = jnp.concatenate([hot, hot, hot], axis=0)
        x = lax.dot_general(hot, table, (((0,), (0,)), ((), ())), preferred_element_type=F32)
        out_ref[rows, :] = x + dot(hidden_ref[rows, :], mix_in_ref[...])
    for chunk in range(8):
        for tile in range(8):
            row = 32 * chunk + 8 * (tile // 2)
            start = LANES * (tile % 2)
            mix_ref[row : row + 8, start : start + LANES] = scale * whole[chunk, tile]
    quarters = [
        scale * jnp.concatenate([whole[2 * quarter, 8], whole[2 * quarter + 1, 8]], axis=1)
        for quarter in range(4)
    ]
    embed_ref[0:8, :] = quarters[2]
    embed_ref[8:16, :] = quarters[3]
    shifted = [quarters[row // 8][row % 8 : row % 8 + 1] for row in range(1, 14)]
    zero_inner, one_inner = quarters[1][6:7], quarters[1][7:8]
    low, high, levels = rows_of(low_ref), rows_of(high_ref), rows_of(levels_ref)
    folded, _ = level_factors(low, high, levels)
    current = quarters[0][0:1]
    low_zero, low_one = zero_inner / low[0], one_inner / low[1]
    high_zero = high_one = jnp.zeros_like(current)
    for level in range(LEVELS):
        late = shifted[level]
        grad_levels_ref[level : level + 1, :] = high[0] * current + high[1] * late
        low_zero = low_zero + folded[level + 1] * current
        low_one = low_one + folded[level + 1] * late
        high_zero = high_zero + levels[level] * current
        high_one = high_one + levels[level] * late
        current = low[0] * current + low[1] * late
    grad_levels_ref[LEVELS : LEVELS + 1, :] = current
    filters_ref[0, 0:1, :] = low_zero
    filters_ref[0, 1:2, :] = low_one
    filters_ref[1, 0:1, :] = high_zero
    filters_ref[1, 1:2, :] = high_one


def finish(scale, ids, hidden, whole, embed, mix, low, high, levels):
    vmem = pl.BlockSpec(memory_space=pltpu.VMEM)
    return pl.pallas_call(
        functools.partial(finish_kernel, scale),
        out_shape=(
            jax.ShapeDtypeStruct((TOKENS, WIDTH), F32),
            jax.ShapeDtypeStruct((2, 2, WIDTH), F32),
            jax.ShapeDtypeStruct((LEVELS + 1, WIDTH), F32),
            jax.ShapeDtypeStruct((WIDTH, WIDTH), F32),
            jax.ShapeDtypeStruct((VOCAB, WIDTH), F32),
        ),
        in_specs=[vmem] * 8,
        out_specs=(vmem,) * 5,
        compiler_params=pltpu.CompilerParams(vmem_limit_bytes=56 * 2**20),
    )(ids, hidden, whole, embed, mix, low, high, levels)


def per_device(ids, embed, low_filter, high_filter, level_weights, mix, cotangent):
    count = lax.axis_size("seq")
    ids = ids.reshape(8, LANES)
    hidden, whole = layer(count, ids, embed, low_filter, high_filter, level_weights, mix, cotangent[0])
    scale = 1.0 / math.sqrt(count * lax.axis_size("batch") * TOKENS)
    out, grad_filters, grad_levels, grad_mix, grad_embed = finish(
        scale, ids, hidden, whole, embed, mix, low_filter, high_filter, level_weights
    )
    return out[None], grad_filters, grad_levels, grad_mix, grad_embed


def solution(mesh):
    placed = (P("batch", "seq"), P(), P(), P(), P(), P(), P("batch", "seq", None))
    return jax.shard_map(
        per_device,
        mesh=mesh,
        in_specs=placed,
        out_specs=(P("batch", "seq", None), P(), P(), P(), P()),
        check_vma=False,
    )
```

time: 636 us -> 45.2 us (0.07)
  waiting for transfers between devices: 414 us -> 0 us
  starting transfers between devices: 94.7 us -> 0 us
  blocking collectives: 69.7 us -> 0 us
  Pallas kernels: 0 us -> 44.4 us
  other arithmetic: 25.1 us -> 0 us
  between operations: 14.9 us -> 0.64 us
  local copies, waits for them, and re-layouts: 8.72 us -> 0 us
  matrix products: 7.44 us -> 0 us
    psum x1 -> x0, waiting for transfers between devices: 212 us -> none  [per_device(): lax.psum((filter_term, levels_term, embed_term, mix_term), ('seq', 'batch'))]
    ppermute x26 -> x0, waiting for transfers between devices: 202 us -> none  [passed_along(): lax.ppermute(value, axis, [(source, source + steps) for source in range(l...]
    ppermute x26 -> x0, starting transfers between devices: 94.7 us -> none  [passed_along(): lax.ppermute(value, axis, [(source, source + steps) for source in range(l...]
    psum x1 -> x0, blocking collectives: 69.7 us -> none  [per_device(): lax.psum((filter_term, levels_term, embed_term, mix_term), ('seq', 'batch'))]
    pallas_call x0 -> x2, Pallas kernels: none -> 44.4 us  [the longest x1 41.7 us: layer(): pl.pallas_call(functools.partial(layer_kernel, count), out_shape=(jax.Sha...]
    reduce_sum x10 -> x0, other arithmetic: 12.4 us -> none  [the longest x5 8.75 us: per_device(): level_rows[level] = jnp.sum(g_y * detail, axis=0)]
    add x29 -> x0, other arithmetic: 9.17 us -> none  [the longest x12 4.06 us: per_device(): back = low_filter[1] * g_a + high_filter[1] * g_detail]
    dot_general x5 -> x0, matrix products: 7.44 us -> none  [the longest x1 2.33 us: per_device(): lax.dot_general(onehot, g_x, (((0,), (0,)), ((), ())), precision=lax.Prec...]
  transfers between devices with their start and end apart: 27 -> 0, of which waited for: 26 -> 0; matrix products, arithmetic and copies ran while one was open for 2% -> 0% of each run, Pallas kernels for 0% -> 0%
where the time goes in v2:
time: 45.2 us; the launch traced here: 45 us
  Pallas kernels  44.4 us (98%)
  between operations  0.64 us (1%)
    pallas_call x1, Pallas kernels, layer(): pl.pallas_call(functools.partial(layer_kernel, count), out_shape=(jax.Sha...  41.7 us
    pallas_call x1, Pallas kernels, finish(): pl.pallas_call(functools.partial(finish_kernel, scale), out_shape=(jax.Sh...  2.68 us

profile of v2, /device:TPU:1, one launch (start us, length us, event | category | flops | bytes accessed | tf_op | source)
XLA Modules:
  0.0 45.0 jit_solution(17965443424451239839)
XLA Ops:
  0.6 41.7 %shard_map.110 = (bf16[1024,256]{1,0:T(8,128)(2,1)}, f32[8,9,8,128]{3,2,1,0:T(8,128)}) custom-call(s32[8,128]{1,0:T(8,128)} %bitcast.4, f32[16,256]{1,0:T(8,128)} %embed_in_ref.1, f32[2,256]{1,0:T(2,128)} %low_ref.3, f32[2,256]{1,0:T(2,128)} %high_ref.3, f32[14,256]{1,0:T(8,128)} %levels_ref.3, bf16[256,256]{1,0:T(8,128)(2,1)} %mix_in_ref.1, ...), custom_call_target="tpu_custom_call" | custom-call | tf_op jit(solution)/shard_map/pallas_call | solution.py:337
  42.4 2.7 %shard_map.111 = (f32[1024,256]{1,0:T(8,128)}, f32[2,2,256]{2,1,0:T(2,128)}, f32[14,256]{1,0:T(8,128)}, f32[256,256]{1,0:T(8,128)}, f32[16,256]{1,0:T(8,128)}) custom-call(s32[8,128]{1,0:T(8,128)} %bitcast.5, bf16[1024,256]{1,0:T(8,128)(2,1)} %get-tuple-element.12.hidden_ref, f32[8,9,8,128]{3,2,1,0:T(8,128)} %get-tuple-element.13.whole, ...), custom_call_target="tpu_custom_call" | custom-call | tf_op jit(solution)/shard_map/pallas_call | solution.py:426

commit v3 on v2

--- a/solution.py
+++ b/solution.py
@@ -225,28 +225,35 @@
 
 
 def layer_kernel(
-    count, ids_ref, embed_ref, low_ref, high_ref, levels_ref, mix_ref, cot_ref,
-    hidden_ref, whole,
+    count, ids_ref, embed_ref, low_ref, high_ref, levels_ref, mix_ref, cot_hbm,
+    hidden_hbm, whole_hbm,
     held, ids_send, ids_recv, ones_ref, class_ref, tokens_ref, s7, s8, s9, s10, features_ref, weights_ref, turned_ref,
-    g_ref, z_ref, part, sibling, halved, first, second, third, sends, recvs,
+    cot_ref, hidden_ref, g_ref, z_ref, local_sem, mix_part, small_part, mix_in, small_in, second, third, total,
+    sends, recvs,
 ):
     seq, batch = lax.axis_index("seq"), lax.axis_index("batch")
     x, y = lax.rem(seq, 4), lax.rem(lax.div(seq, 4), 4)
     core = lax.rem(batch, 2)
     z = lax.div(seq, 16) * 2 + lax.div(batch, 2)
 
-    def device(x, y, z, core):
+    def along(order):
+        return [x + order * (y - x), y + order * (z - y), z + order * (x - z)]
+
+    def device(order, spots, core):
+        a, b, c = spots
+        x, y, z = a + order * (c - a), b + order * (a - b), c + order * (b - c)
         return lax.div(z, 2) * 16 + y * 4 + x, lax.rem(z, 2) * 2 + core
 
-    spots = (x + core * (y - x), y + core * (z - y), z + core * (x - z))
-
-    def peer_of(axis, step):
-        spot = list(spots)
-        spot[axis] = lax.rem(spots[axis] + step, 4)
-        a, b, c = spot
-        return device(a + core * (c - a), b + core * (a - b), c + core * (b - c), core)
-
-    other = device(x, y, z, 1 - core)
+    def moved(spots, axis, step):
+        return [lax.rem(spot + step, 4) if place == axis else spot for place, spot in enumerate(spots)]
+
+    mine, theirs = along(core), along(1 - core)
+    own_peer = lambda axis, step: device(core, moved(mine, axis, step), core)
+    their_peer = lambda step: device(1 - core, moved(theirs, 0, step), 1 - core)
+    cross_peer = lambda step: device(core, moved(mine, 0, step), 1 - core)
+
+    cot_copy = pltpu.make_async_copy(cot_hbm, cot_ref, local_sem.at[0])
+    cot_copy.start()
     barrier = pltpu.get_barrier_semaphore()
 
     def greet(peer):
@@ -254,11 +261,13 @@
 
     for step in range(1, BACK + 1):
         greet((lax.rem(seq + count - step, count), batch))
-    greet(other)
-    for axis in range(3):
-        for step in range(1, 4):
-            greet(peer_of(axis, step))
-    pl.semaphore_wait(barrier, BACK + 10)
+    for step in range(4):
+        greet(their_peer(step))
+    for step in range(1, 4):
+        greet(cross_peer(step))
+        for axis in range(3):
+            greet(own_peer(axis, step))
+    pl.semaphore_wait(barrier, BACK + 16)
 
     def copy_to(source, target, sent, received, peer):
         copy = pltpu.make_async_remote_copy(
@@ -283,67 +292,104 @@
     make_tables(ones_ref, class_ref)
     tokens_ref[0:VOCAB, LANES:] = jnp.zeros((VOCAB, LANES), BF16)
     make_hot(tokens_ref, 8 * BACK, ids_ref[...])
-    for step in range(BACK):
+
+    def receive(step):
         id_copies[step].wait()
         make_hot(tokens_ref, 8 * (BACK - 1 - step), jnp.where(seq > step, held[step], -1))
+
+    receive(0)
     make_near(tokens_ref, class_ref, features_ref)
+    for step in range(1, BACK):
+        receive(step)
     make_far(tokens_ref, ones_ref, s7, s8, s9, s10, features_ref)
+    cot_copy.wait()
     mix_sum = forward(turned_ref, features_ref, mix_ref, cot_ref, hidden_ref, g_ref)
-    small = backward(passed, folded, kappa, embed, features_ref, g_ref, cot_ref, z_ref)
-
+    hidden_copy = pltpu.make_async_copy(hidden_ref, hidden_hbm, local_sem.at[1])
+    hidden_copy.start()
+
+    def spread(phase, part, target):
+        copies = []
+        for step in range(1, 4):
+            place = 4 * core + lax.rem(mine[0] + step, 4)
+            copies.append(
+                copy_to(part.at[place], target.at[step - 1], sends.at[phase, step - 1], recvs.at[phase, step - 1], own_peer(0, step))
+            )
+        for step in range(4):
+            place = 4 * (1 - core) + lax.rem(theirs[0] + step, 4)
+            copies.append(
+                copy_to(part.at[place], target.at[step + 3], sends.at[phase, step + 3], recvs.at[phase, step + 3], their_peer(step))
+            )
+        return copies
+
+    home = 4 * core + mine[0]
     for chunk in range(8):
         for tile in range(8):
             row = 32 * chunk + 8 * (tile // 2)
             column = LANES * (tile % 2)
-            part[chunk, tile] = mix_sum[row : row + 8, column : column + LANES]
+            mix_part[chunk, tile] = mix_sum[row : row + 8, column : column + LANES]
+    mix_copies = spread(0, mix_part, mix_in)
+    small = backward(passed, folded, kappa, embed, features_ref, g_ref, cot_ref, z_ref)
+    for chunk in range(8):
         row, column = 8 * (chunk // 2), LANES * (chunk % 2)
-        part[chunk, 8] = small[row : row + 8, column : column + LANES]
-
-    copy_to(
-        part.at[pl.ds(4 * (1 - core), 4)], sibling, sends.at[0, 0], recvs.at[0, 0], other
-    ).wait()
-    for chunk in range(4):
-        halved[chunk] = part[4 * core + chunk] + sibling[chunk]
-
-    def exchange(phase, axis, source_of, target):
+        small_part[chunk] = small[row : row + 8, column : column + LANES]
+    small_copies = spread(1, small_part, small_in)
+    for copy in mix_copies:
+        copy.wait()
+    mixed = mix_part[home]
+    for slot in range(7):
+        mixed = mixed + mix_in[slot]
+    second[mine[1], 0:8] = mixed
+    for copy in small_copies:
+        copy.wait()
+    rows = small_part[home]
+    for slot in range(7):
+        rows = rows + small_in[slot]
+    second[mine[1], 8] = rows
+
+    def exchange(phase, axis, target):
+        spot = target.at[mine[axis]]
         copies = [
-            copy_to(source_of(step), target.at[spots[axis]], sends.at[phase, step], recvs.at[phase, step], peer_of(axis, step))
+            copy_to(spot, spot, sends.at[phase, step], recvs.at[phase, step], own_peer(axis, step))
             for step in range(1, 4)
         ]
         for copy in copies:
             copy.wait()
 
-    first[spots[0]] = halved[spots[0]]
-    exchange(1, 0, lambda step: halved.at[lax.rem(spots[0] + step, 4)], first)
-    second[spots[1]] = (first[0] + first[1]) + (first[2] + first[3])
-    exchange(2, 1, lambda step: second.at[spots[1]], second)
-    third[spots[2]] = (second[0] + second[1]) + (second[2] + second[3])
-    exchange(3, 2, lambda step: third.at[spots[2]], third)
-    mine = 4 * core + spots[0]
-    whole[mine] = (third[0] + third[1]) + (third[2] + third[3])
-    copies = [
-        copy_to(whole.at[mine], whole.at[mine], sends.at[4, step], recvs.at[4, step], peer_of(0, step))
-        for step in range(1, 4)
-    ]
+    exchange(2, 1, second)
+    third[mine[2]] = (second[0] + second[1]) + (second[2] + second[3])
+    exchange(3, 2, third)
+    total[...] = (third[0] + third[1]) + (third[2] + third[3])
+    local = pltpu.make_async_copy(total, whole_hbm.at[home], local_sem.at[2])
+    local.start()
+    copies = []
+    for step in range(1, 4):
+        copies.append(
+            copy_to(total, whole_hbm.at[home], sends.at[4, step - 1], recvs.at[4, step - 1], own_peer(0, step))
+        )
+    for step in range(4):
+        copies.append(
+            copy_to(total, whole_hbm.at[home], sends.at[4, step + 3], recvs.at[4, step + 3], cross_peer(step))
+        )
+    hidden_copy.wait()
+    local.wait()
     for copy in copies:
         copy.wait()
-    ours = whole.at[pl.ds(4 * core, 4)]
-    copy_to(ours, ours, sends.at[5, 0], recvs.at[5, 0], other).wait()
 
 
 def layer(count, ids, embed, low, high, levels, mix, cot):
     vmem = pl.BlockSpec(memory_space=pltpu.VMEM)
-    chunk = (9, 8, LANES)
+    anywhere = pl.BlockSpec(memory_space=pl.ANY)
+    tile = (8, LANES)
     return pl.pallas_call(
         functools.partial(layer_kernel, count),
         out_shape=(
             jax.ShapeDtypeStruct((TOKENS, WIDTH), BF16),
-            jax.ShapeDtypeStruct((8,) + chunk, F32),
+            jax.ShapeDtypeStruct((8, 9) + tile, F32),
         ),
-        in_specs=[vmem] * 7,
-        out_specs=(vmem, vmem),
+        in_specs=[vmem] * 6 + [anywhere],
+        out_specs=(anywhere, anywhere),
         scratch_shapes=[
-            pltpu.VMEM((BACK, 8, LANES), jnp.int32),
+            pltpu.VMEM((BACK,) + tile, jnp.int32),
             pltpu.SemaphoreType.DMA((BACK,)),
             pltpu.SemaphoreType.DMA((BACK,)),
             pltpu.VMEM((2 * LANES, 8 * LANES), BF16),
@@ -356,16 +402,20 @@
             pltpu.VMEM((ROWS, TOKENS), BF16),
             pltpu.VMEM((ROWS, 2 * WIDTH), BF16),
             pltpu.VMEM((2 * WIDTH, ROWS), BF16),
+            pltpu.VMEM((TOKENS, WIDTH), BF16),
+            pltpu.VMEM((TOKENS, WIDTH), BF16),
             pltpu.VMEM((TOKENS, 2 * WIDTH), BF16),
             pltpu.VMEM((CLASSES * VOCAB, WIDTH), F32),
-            pltpu.VMEM((8,) + chunk, F32),
-            pltpu.VMEM((4,) + chunk, F32),
-            pltpu.VMEM((4,) + chunk, F32),
-            pltpu.VMEM((4,) + chunk, F32),
-            pltpu.VMEM((4,) + chunk, F32),
-            pltpu.VMEM((4,) + chunk, F32),
-            pltpu.SemaphoreType.DMA((6, 4)),
-            pltpu.SemaphoreType.DMA((6, 4)),
+            pltpu.SemaphoreType.DMA((3,)),
+            pltpu.VMEM((8, 8) + tile, F32),
+            pltpu.VMEM((8,) + tile, F32),
+            pltpu.VMEM((7, 8) + tile, F32),
+            pltpu.VMEM((7,) + tile, F32),
+            pltpu.VMEM((4, 9) + tile, F32),
+            pltpu.VMEM((4, 9) + tile, F32),
+            pltpu.VMEM((9,) + tile, F32),
+            pltpu.SemaphoreType.DMA((5, 8)),
+            pltpu.SemaphoreType.DMA((5, 8)),
         ],
         compiler_params=pltpu.CompilerParams(
             collective_id=0, has_side_effects=True, vmem_limit_bytes=56 * 2**20
@@ -374,25 +424,49 @@
 
 
 def finish_kernel(
-    scale, ids_ref, hidden_ref, whole, embed_in_ref, mix_in_ref, low_ref, high_ref, levels_ref,
-    out_ref, filters_ref, grad_levels_ref, mix_ref, embed_ref,
+    scale, ids_ref, hidden_hbm, whole_hbm, embed_in_ref, mix_in_ref, low_ref, high_ref, levels_ref,
+    out_hbm, filters_ref, grad_levels_ref, mix_hbm, embed_ref,
+    hidden, whole, out, mix, sems,
 ):
+    parts = 4
+    length = TOKENS // parts
+    spans = [pl.ds(part * length, length) for part in range(parts)]
+    loads = [pltpu.make_async_copy(hidden_hbm.at[span], hidden.at[span], sems.at[0, part]) for part, span in enumerate(spans)]
+    for load in loads:
+        load.start()
+    whole_load = pltpu.make_async_copy(whole_hbm, whole, sems.at[2, 0])
+    whole_load.start()
+    stores = []
     embed = embed_in_ref[...]
     high_part, middle = halves(embed)
     rest = (embed - high_part.astype(F32) - middle.astype(F32)).astype(BF16)
     table = jnp.concatenate([high_part, middle, rest], axis=0)
     names = lax.broadcasted_iota(jnp.int32, (VOCAB, LANES), 0)
-    for tile in range(8):
-        rows = slice(tile * LANES, (tile + 1) * LANES)
-        hot = where_is(names, jnp.broadcast_to(ids_ref[tile : tile + 1, :], (VOCAB, LANES)))
+    for part in range(parts):
+        hot = jnp.concatenate(
+            [
+                where_is(names, jnp.broadcast_to(ids_ref[tile : tile + 1, :], (VOCAB, LANES)))
+                for tile in range(2 * part, 2 * part + 2)
+            ],
+            axis=1,
+        )
         hot = jnp.concatenate([hot, hot, hot], axis=0)
         x = lax.dot_general(hot, table, (((0,), (0,)), ((), ())), preferred_element_type=F32)
-        out_ref[rows, :] = x + dot(hidden_ref[rows, :], mix_in_ref[...])
+        loads[part].wait()
+        rows = slice(part * length, (part + 1) * length)
+        out[rows, :] = x + dot(hidden[rows, :], mix_in_ref[...])
+        store = pltpu.make_async_copy(out.at[spans[part]], out_hbm.at[spans[part]], sems.at[1, part])
+        store.start()
+        stores.append(store)
+    whole_load.wait()
     for chunk in range(8):
         for tile in range(8):
             row = 32 * chunk + 8 * (tile // 2)
             start = LANES * (tile % 2)
-            mix_ref[row : row + 8, start : start + LANES] = scale * whole[chunk, tile]
+            mix[row : row + 8, start : start + LANES] = scale * whole[chunk, tile]
+    store = pltpu.make_async_copy(mix, mix_hbm, sems.at[2, 1])
+    store.start()
+    stores.append(store)
     quarters = [
         scale * jnp.concatenate([whole[2 * quarter, 8], whole[2 * quarter + 1, 8]], axis=1)
         for quarter in range(4)
@@ -419,10 +493,13 @@
     filters_ref[0, 1:2, :] = low_one
     filters_ref[1, 0:1, :] = high_zero
     filters_ref[1, 1:2, :] = high_one
+    for store in stores:
+        store.wait()
 
 
 def finish(scale, ids, hidden, whole, embed, mix, low, high, levels):
     vmem = pl.BlockSpec(memory_space=pltpu.VMEM)
+    anywhere = pl.BlockSpec(memory_space=pl.ANY)
     return pl.pallas_call(
         functools.partial(finish_kernel, scale),
         out_shape=(
@@ -432,8 +509,15 @@
             jax.ShapeDtypeStruct((WIDTH, WIDTH), F32),
             jax.ShapeDtypeStruct((VOCAB, WIDTH), F32),
         ),
-        in_specs=[vmem] * 8,
-        out_specs=(vmem,) * 5,
+        in_specs=[vmem, anywhere, anywhere] + [vmem] * 5,
+        out_specs=(anywhere, vmem, vmem, anywhere, vmem),
+        scratch_shapes=[
+            pltpu.VMEM((TOKENS, WIDTH), BF16),
+            pltpu.VMEM((8, 9, 8, LANES), F32),
+            pltpu.VMEM((TOKENS, WIDTH), F32),
+            pltpu.VMEM((WIDTH, WIDTH), F32),
+            pltpu.SemaphoreType.DMA((3, 4)),
+        ],
         compiler_params=pltpu.CompilerParams(vmem_limit_bytes=56 * 2**20),
     )(ids, hidden, whole, embed, mix, low, high, levels)
 

time: 45.2 us -> 44.3 us (0.980)
  Pallas kernels: 44.4 us -> 43.5 us
    pallas_call x1, Pallas kernels: 41.7 us -> 39 us  [layer(): pl.pallas_call(functools.partial(layer_kernel, count), out_shape=(jax.Sha...]
    pallas_call x1, Pallas kernels: 2.68 us -> 4.52 us  [finish(): pl.pallas_call(functools.partial(finish_kernel, scale), out_shape=(jax.Sh...]
where the time goes in v3:
time: 44.3 us; the launch traced here: 44.1 us
  Pallas kernels  43.5 us (98%)
  between operations  0.64 us (1%)
    pallas_call x1, Pallas kernels, layer(): pl.pallas_call(functools.partial(layer_kernel, count), out_shape=(jax.Sha...  39 us
    pallas_call x1, Pallas kernels, finish(): pl.pallas_call(functools.partial(finish_kernel, scale), out_shape=(jax.Sh...  4.52 us

profile of v3, /device:TPU:1, one launch (start us, length us, event | category | flops | bytes accessed | tf_op | source)
XLA Modules:
  0.0 44.1 jit_solution(10357555697793922072)
XLA Ops:
  0.6 39.0 %shard_map.110 = (bf16[1024,256]{1,0:T(8,128)(2,1)}, f32[8,9,8,128]{3,2,1,0:T(8,128)}) custom-call(s32[8,128]{1,0:T(8,128)} %bitcast.4, f32[16,256]{1,0:T(8,128)} %embed_in_ref.1, f32[2,256]{1,0:T(2,128)} %low_ref.3, f32[2,256]{1,0:T(2,128)} %high_ref.3, f32[14,256]{1,0:T(8,128)} %levels_ref.3, bf16[256,256]{1,0:T(8,128)(2,1)} %mix_in_ref.1, ...), custom_call_target="tpu_custom_call" | custom-call | tf_op jit(solution)/shard_map/pallas_call | solution.py:383
  39.6 4.5 %shard_map.111 = (f32[1024,256]{1,0:T(8,128)}, f32[2,2,256]{2,1,0:T(2,128)}, f32[14,256]{1,0:T(8,128)}, f32[256,256]{1,0:T(8,128)}, f32[16,256]{1,0:T(8,128)}) custom-call(s32[8,128]{1,0:T(8,128)} %bitcast.5, bf16[1024,256]{1,0:T(8,128)(2,1)} %get-tuple-element.12.hidden_hbm, f32[8,9,8,128]{3,2,1,0:T(8,128)} %get-tuple-element.13.whole_hbm, ...), custom_call_target="tpu_custom_call" | custom-call | tf_op jit(solution)/shard_map/pallas_call | solution.py:503

commit v4 on v2

--- a/solution.py
+++ b/solution.py
@@ -19,6 +19,8 @@
 TILES = (BACK + 1) * TOKENS // LANES
 CLASSES = 1 + LEVELS * (LEVELS + 1) // 2
 ROWS = 96 * VOCAB
+NEAR = 56 * VOCAB
+CHUNKS = 32
 
 
 def class_of(level, ones):
@@ -107,7 +109,47 @@
             tokens_ref[(tile + 1) * VOCAB : (tile + 2) * VOCAB, LANES:] = hot
 
 
-def make_near(tokens_ref, class_ref, features_ref):
+def put_counts(result, s7, first, last, pair):
+    for tile in range(first, last):
+        for half in range(2):
+            value = 2 * pair + half
+            s7[value * VOCAB : (value + 1) * VOCAB, tile * LANES : (tile + 1) * LANES] = result[
+                (tile - first) * VOCAB : (tile - first + 1) * VOCAB, half * LANES : (half + 1) * LANES
+            ]
+
+
+def count_tiles(tokens_ref, ones_ref, s7, first, last):
+    for pair in range(4):
+        table = ones_ref[:, 2 * pair * LANES : 2 * (pair + 1) * LANES]
+        result = dot(tokens_ref[first * VOCAB : last * VOCAB, :], table).astype(BF16)
+        put_counts(result, s7, first, last, pair)
+
+
+def widened(source, level, ones, first, last):
+    begin, end, span = first * LANES, last * LANES, 2**level
+    total = None
+    if 0 <= ones <= level:
+        total = source[ones * VOCAB : (ones + 1) * VOCAB, begin:end]
+    if 1 <= ones <= level + 1:
+        late = source[(ones - 1) * VOCAB : ones * VOCAB, begin - span : end - span]
+        total = late if total is None else total + late
+    return total
+
+
+def widen(source, target, level, first, last):
+    for ones in range(level + 2):
+        target[ones * VOCAB : (ones + 1) * VOCAB, first * LANES : last * LANES] = widened(
+            source, level, ones, first, last
+        )
+
+
+def place_level(source, level, features_ref):
+    rows = slice(class_of(level, 0) * VOCAB, class_of(level + 1, 0) * VOCAB)
+    begin = BACK * TOKENS - 2**level
+    features_ref[rows, :] = source[:, begin : begin + TOKENS]
+
+
+def make_near(tokens_ref, class_ref, ones_ref, s7, s8, s9, features_ref):
     own = tokens_ref[64 * VOCAB : 72 * VOCAB, :]
     for first in range(0, 29, 2):
         members = range(first, min(first + 2, 29))
@@ -117,55 +159,25 @@
                 features_ref[member * VOCAB : (member + 1) * VOCAB, tile * LANES : (tile + 1) * LANES] = result[
                     tile * VOCAB : (tile + 1) * VOCAB, half * LANES : (half + 1) * LANES
                 ]
+    count_tiles(tokens_ref, ones_ref, s7, 57, 71)
+    widen(s7, s8, 7, 58, 70)
+    widen(s8, s9, 8, 60, 68)
+    place_level(s7, 7, features_ref)
+    place_level(s8, 8, features_ref)
+    place_level(s9, 9, features_ref)
 
 
 def make_far(tokens_ref, ones_ref, s7, s8, s9, s10, features_ref):
-    for pair in range(4):
-        result = dot(
-            tokens_ref[VOCAB : 71 * VOCAB, :], ones_ref[:, 2 * pair * LANES : 2 * (pair + 1) * LANES]
-        ).astype(BF16)
-        for tile in range(1, 71):
-            for half in range(2):
-                value = 2 * pair + half
-                s7[value * VOCAB : (value + 1) * VOCAB, tile * LANES : (tile + 1) * LANES] = result[
-                    (tile - 1) * VOCAB : tile * VOCAB, half * LANES : (half + 1) * LANES
-                ]
-
-    def step(source, level, ones, begin, end):
-        span = 2**level
-        total = None
-        if 0 <= ones <= level:
-            total = source[ones * VOCAB : (ones + 1) * VOCAB, begin:end]
-        if 1 <= ones <= level + 1:
-            late = source[(ones - 1) * VOCAB : ones * VOCAB, begin - span : end - span]
-            total = late if total is None else total + late
-        return total
-
-    def both(one, other):
-        if one is None or other is None:
-            return other if one is None else one
-        return one + other
-
-    for ones in range(9):
-        s8[ones * VOCAB : (ones + 1) * VOCAB, 2 * LANES : 70 * LANES] = step(s7, 7, ones, 2 * LANES, 70 * LANES)
-    for ones in range(10):
-        s9[ones * VOCAB : (ones + 1) * VOCAB, 4 * LANES : 68 * LANES] = step(s8, 8, ones, 4 * LANES, 68 * LANES)
-    for ones in range(11):
-        s10[ones * VOCAB : (ones + 1) * VOCAB, 8 * LANES : 64 * LANES] = step(s9, 9, ones, 8 * LANES, 64 * LANES)
-    home = BACK * TOKENS
-    for level, source in ((7, s7), (8, s8), (9, s9), (10, s10)):
-        rows = slice(class_of(level, 0) * VOCAB, class_of(level + 1, 0) * VOCAB)
-        begin = home - 2**level
-        features_ref[rows, :] = source[:, begin : begin + TOKENS]
+    count_tiles(tokens_ref, ones_ref, s7, 1, 57)
+    widen(s7, s8, 7, 2, 58)
+    widen(s8, s9, 8, 4, 60)
+    widen(s9, s10, 9, 8, 64)
+    place_level(s10, 10, features_ref)
     for ones in range(12):
-        begin = home - 2048
-        features_ref[block_of(11, ones), :] = step(s10, 10, ones, begin, begin + TOKENS)
+        features_ref[block_of(11, ones), :] = widened(s10, 10, ones, 48, 56)
     for ones in range(13):
-        begin = home - 4096
-        near = step(s10, 10, ones, begin, begin + TOKENS)
-        late = step(s10, 10, ones - 1, begin - 2048, begin - 2048 + TOKENS)
-        features_ref[block_of(12, ones), :] = both(near, late)
-    features_ref[CLASSES * VOCAB :, :] = jnp.zeros((ROWS - CLASSES * VOCAB, TOKENS), BF16)
+        near, late = widened(s10, 10, ones, 32, 40), widened(s10, 10, ones - 1, 16, 24)
+        features_ref[block_of(12, ones), :] = late if near is None else near if late is None else near + late
 
 
 def gelu_parts(y):
@@ -177,14 +189,21 @@
     return y * half, slope
 
 
-def forward(turned_ref, features_ref, mix_ref, cot_ref, hidden_ref, g_ref):
+def near_part(turned_ref, features_ref, y_ref):
+    for start in range(0, TOKENS, 256):
+        span = slice(start, start + 256)
+        both = dot(turned_ref[:, 0:NEAR], features_ref[0:NEAR, span])
+        y_ref[:, span] = both[:WIDTH] + both[WIDTH:]
+
+
+def forward(turned_ref, features_ref, y_ref, mix_ref, cot_ref, hidden_ref, g_ref):
     mix = mix_ref[...]
     mix_sum = None
     block = 256
     for start in range(0, TOKENS, block):
         span = slice(start, start + block)
-        both = dot(turned_ref[...], features_ref[:, span])
-        y = (both[:WIDTH] + both[WIDTH:]).T
+        both = dot(turned_ref[:, NEAR:], features_ref[NEAR:, span])
+        y = (y_ref[:, span] + both[:WIDTH] + both[WIDTH:]).T
         active, slope = gelu_parts(y)
         hidden = active.astype(BF16)
         hidden_ref[span, :] = hidden
@@ -225,28 +244,36 @@
 
 
 def layer_kernel(
-    count, ids_ref, embed_ref, low_ref, high_ref, levels_ref, mix_ref, cot_ref,
+    count, ids_hbm, embed_hbm, low_hbm, high_hbm, levels_hbm, mix_hbm, cot_hbm,
     hidden_ref, whole,
     held, ids_send, ids_recv, ones_ref, class_ref, tokens_ref, s7, s8, s9, s10, features_ref, weights_ref, turned_ref,
-    g_ref, z_ref, part, sibling, halved, first, second, third, sends, recvs,
+    y_ref, g_ref, z_ref, ids_ref, embed_ref, low_ref, high_ref, levels_ref, mix_ref, cot_ref, local_sem,
+    mix_part, small_part, mix_in, small_in, second, third, sends, recvs,
 ):
     seq, batch = lax.axis_index("seq"), lax.axis_index("batch")
     x, y = lax.rem(seq, 4), lax.rem(lax.div(seq, 4), 4)
     core = lax.rem(batch, 2)
     z = lax.div(seq, 16) * 2 + lax.div(batch, 2)
 
-    def device(x, y, z, core):
+    def along(order):
+        return x + order * (y - x), y + order * (z - y), z + order * (x - z)
+
+    def device(order, spots, core):
+        a, b, c = spots
+        x, y, z = a + order * (c - a), b + order * (a - b), c + order * (b - c)
         return lax.div(z, 2) * 16 + y * 4 + x, lax.rem(z, 2) * 2 + core
 
-    spots = (x + core * (y - x), y + core * (z - y), z + core * (x - z))
-
-    def peer_of(axis, step):
-        spot = list(spots)
-        spot[axis] = lax.rem(spots[axis] + step, 4)
-        a, b, c = spot
-        return device(a + core * (c - a), b + core * (a - b), c + core * (b - c), core)
-
-    other = device(x, y, z, 1 - core)
+    def moved(spots, i, j, k):
+        return lax.rem(spots[0] + i, 4), lax.rem(spots[1] + j, 4), lax.rem(spots[2] + k, 4)
+
+    mine, theirs = along(core), along(1 - core)
+    plane = [(i, j) for i in range(4) for j in range(4)]
+    others = plane[1:]
+    own_peer = lambda i, j, k: device(core, moved(mine, i, j, k), core)
+    their_peer = lambda i, j: device(1 - core, moved(theirs, i, j, 0), 1 - core)
+    cross_peer = lambda i, j: device(core, moved(mine, i, j, 0), 1 - core)
+    chunk_of = lambda core, spots: 16 * core + 4 * spots[0] + spots[1]
+
     barrier = pltpu.get_barrier_semaphore()
 
     def greet(peer):
@@ -254,11 +281,31 @@
 
     for step in range(1, BACK + 1):
         greet((lax.rem(seq + count - step, count), batch))
-    greet(other)
-    for axis in range(3):
-        for step in range(1, 4):
-            greet(peer_of(axis, step))
-    pl.semaphore_wait(barrier, BACK + 10)
+    for i, j in others:
+        greet(own_peer(i, j, 0))
+    for k in range(1, 4):
+        greet(own_peer(0, 0, k))
+    for i, j in plane:
+        greet(their_peer(i, j))
+        if i:
+            greet(cross_peer(i + core * (j - i), j + core * (i - j)))
+    loads = [
+        pltpu.make_async_copy(source, target, local_sem.at[place])
+        for place, (source, target) in enumerate(
+            [
+                (ids_hbm, ids_ref),
+                (embed_hbm, embed_ref),
+                (low_hbm, low_ref),
+                (high_hbm, high_ref),
+                (levels_hbm, levels_ref),
+                (mix_hbm, mix_ref),
+                (cot_hbm, cot_ref),
+            ]
+        )
+    ]
+    for load in loads:
+        load.start()
+    pl.semaphore_wait(barrier, BACK + 46)
 
     def copy_to(source, target, sent, received, peer):
         copy = pltpu.make_async_remote_copy(
@@ -269,11 +316,13 @@
 
     id_copies = [
         copy_to(
-            ids_ref, held.at[step], ids_send.at[step], ids_recv.at[step], (lax.rem(seq + step + 1, count), batch)
+            ids_hbm, held.at[step], ids_send.at[step], ids_recv.at[step], (lax.rem(seq + step + 1, count), batch)
         )
         for step in range(BACK)
     ]
 
+    for load in loads:
+        load.wait()
     embed = embed_ref[...]
     low, high, levels = rows_of(low_ref), rows_of(high_ref), rows_of(levels_ref)
     folded, kappa = level_factors(low, high, levels)
@@ -282,65 +331,85 @@
     turned_ref[...] = weights_ref[...].T
     make_tables(ones_ref, class_ref)
     tokens_ref[0:VOCAB, LANES:] = jnp.zeros((VOCAB, LANES), BF16)
+    features_ref[CLASSES * VOCAB :, :] = jnp.zeros((ROWS - CLASSES * VOCAB, TOKENS), BF16)
     make_hot(tokens_ref, 8 * BACK, ids_ref[...])
-    for step in range(BACK):
+
+    def receive(step):
         id_copies[step].wait()
         make_hot(tokens_ref, 8 * (BACK - 1 - step), jnp.where(seq > step, held[step], -1))
-    make_near(tokens_ref, class_ref, features_ref)
+
+    receive(0)
+    make_near(tokens_ref, class_ref, ones_ref, s7, s8, s9, features_ref)
+    near_part(turned_ref, features_ref, y_ref)
+    for step in range(1, BACK):
+        receive(step)
     make_far(tokens_ref, ones_ref, s7, s8, s9, s10, features_ref)
-    mix_sum = forward(turned_ref, features_ref, mix_ref, cot_ref, hidden_ref, g_ref)
+    mix_sum = forward(turned_ref, features_ref, y_ref, mix_ref, cot_ref, hidden_ref, g_ref)
+
+    def spread(phase, part, target):
+        copies = []
+        for slot, (i, j) in enumerate(others):
+            place = chunk_of(core, moved(mine, i, j, 0))
+            copies.append(
+                copy_to(part.at[place], target.at[slot], sends.at[phase, slot], recvs.at[phase, slot], own_peer(i, j, 0))
+            )
+        for slot, (i, j) in enumerate(plane, 15):
+            place = chunk_of(1 - core, moved(theirs, i, j, 0))
+            copies.append(
+                copy_to(part.at[place], target.at[slot], sends.at[phase, slot], recvs.at[phase, slot], their_peer(i, j))
+            )
+        return copies
+
+    home = chunk_of(core, mine)
+    for chunk in range(CHUNKS):
+        mix_part[chunk] = mix_sum[8 * chunk : 8 * chunk + 8]
+    mix_copies = spread(0, mix_part, mix_in)
     small = backward(passed, folded, kappa, embed, features_ref, g_ref, cot_ref, z_ref)
-
-    for chunk in range(8):
-        for tile in range(8):
-            row = 32 * chunk + 8 * (tile // 2)
-            column = LANES * (tile % 2)
-            part[chunk, tile] = mix_sum[row : row + 8, column : column + LANES]
-        row, column = 8 * (chunk // 2), LANES * (chunk % 2)
-        part[chunk, 8] = small[row : row + 8, column : column + LANES]
-
-    copy_to(
-        part.at[pl.ds(4 * (1 - core), 4)], sibling, sends.at[0, 0], recvs.at[0, 0], other
-    ).wait()
-    for chunk in range(4):
-        halved[chunk] = part[4 * core + chunk] + sibling[chunk]
-
-    def exchange(phase, axis, source_of, target):
-        copies = [
-            copy_to(source_of(step), target.at[spots[axis]], sends.at[phase, step], recvs.at[phase, step], peer_of(axis, step))
-            for step in range(1, 4)
-        ]
-        for copy in copies:
-            copy.wait()
-
-    first[spots[0]] = halved[spots[0]]
-    exchange(1, 0, lambda step: halved.at[lax.rem(spots[0] + step, 4)], first)
-    second[spots[1]] = (first[0] + first[1]) + (first[2] + first[3])
-    exchange(2, 1, lambda step: second.at[spots[1]], second)
-    third[spots[2]] = (second[0] + second[1]) + (second[2] + second[3])
-    exchange(3, 2, lambda step: third.at[spots[2]], third)
-    mine = 4 * core + spots[0]
-    whole[mine] = (third[0] + third[1]) + (third[2] + third[3])
+    for chunk in range(CHUNKS):
+        small_part[chunk] = small[chunk : chunk + 1]
+    small_copies = spread(1, small_part, small_in)
+    for copy in mix_copies:
+        copy.wait()
+    mixed = mix_part[home]
+    for slot in range(CHUNKS - 1):
+        mixed = mixed + mix_in[slot]
+    for row in range(8):
+        second[mine[2], row] = mixed[row : row + 1]
+    for copy in small_copies:
+        copy.wait()
+    row = small_part[home]
+    for slot in range(CHUNKS - 1):
+        row = row + small_in[slot]
+    second[mine[2], 8] = row
+    spot = second.at[mine[2]]
     copies = [
-        copy_to(whole.at[mine], whole.at[mine], sends.at[4, step], recvs.at[4, step], peer_of(0, step))
-        for step in range(1, 4)
+        copy_to(spot, spot, sends.at[2, k], recvs.at[2, k], own_peer(0, 0, k)) for k in range(1, 4)
     ]
     for copy in copies:
         copy.wait()
-    ours = whole.at[pl.ds(4 * core, 4)]
-    copy_to(ours, ours, sends.at[5, 0], recvs.at[5, 0], other).wait()
+    third[...] = (second[0] + second[1]) + (second[2] + second[3])
+    landing = whole.at[pl.ds(9 * home, 9)]
+    copies = []
+    for slot, (i, j) in enumerate(others):
+        copies.append(copy_to(third, landing, sends.at[3, slot], recvs.at[3, slot], own_peer(i, j, 0)))
+    for slot, (i, j) in enumerate(plane, 15):
+        copies.append(copy_to(third, landing, sends.at[3, slot], recvs.at[3, slot], cross_peer(i, j)))
+    whole[pl.ds(9 * home, 9)] = third[...]
+    for copy in copies:
+        copy.wait()
 
 
 def layer(count, ids, embed, low, high, levels, mix, cot):
     vmem = pl.BlockSpec(memory_space=pltpu.VMEM)
-    chunk = (9, 8, LANES)
+    far = pl.BlockSpec(memory_space=pltpu.HBM)
+    arguments = (ids, embed, low, high, levels, mix, cot)
     return pl.pallas_call(
         functools.partial(layer_kernel, count),
         out_shape=(
             jax.ShapeDtypeStruct((TOKENS, WIDTH), BF16),
-            jax.ShapeDtypeStruct((8,) + chunk, F32),
+            jax.ShapeDtypeStruct((9 * CHUNKS, 1, WIDTH), F32),
         ),
-        in_specs=[vmem] * 7,
+        in_specs=[far] * 7,
         out_specs=(vmem, vmem),
         scratch_shapes=[
             pltpu.VMEM((BACK, 8, LANES), jnp.int32),
@@ -356,21 +425,24 @@
             pltpu.VMEM((ROWS, TOKENS), BF16),
             pltpu.VMEM((ROWS, 2 * WIDTH), BF16),
             pltpu.VMEM((2 * WIDTH, ROWS), BF16),
+            pltpu.VMEM((WIDTH, TOKENS), F32),
             pltpu.VMEM((TOKENS, 2 * WIDTH), BF16),
             pltpu.VMEM((CLASSES * VOCAB, WIDTH), F32),
-            pltpu.VMEM((8,) + chunk, F32),
-            pltpu.VMEM((4,) + chunk, F32),
-            pltpu.VMEM((4,) + chunk, F32),
-            pltpu.VMEM((4,) + chunk, F32),
-            pltpu.VMEM((4,) + chunk, F32),
-            pltpu.VMEM((4,) + chunk, F32),
-            pltpu.SemaphoreType.DMA((6, 4)),
-            pltpu.SemaphoreType.DMA((6, 4)),
+            *[pltpu.VMEM(array.shape, array.dtype) for array in arguments],
+            pltpu.SemaphoreType.DMA((7,)),
+            pltpu.VMEM((CHUNKS, 8, WIDTH), F32),
+            pltpu.VMEM((CHUNKS, 1, WIDTH), F32),
+            pltpu.VMEM((CHUNKS - 1, 8, WIDTH), F32),
+            pltpu.VMEM((CHUNKS - 1, 1, WIDTH), F32),
+            pltpu.VMEM((4, 9, 1, WIDTH), F32),
+            pltpu.VMEM((9, 1, WIDTH), F32),
+            pltpu.SemaphoreType.DMA((4, CHUNKS)),
+            pltpu.SemaphoreType.DMA((4, CHUNKS)),
         ],
         compiler_params=pltpu.CompilerParams(
-            collective_id=0, has_side_effects=True, vmem_limit_bytes=56 * 2**20
+            collective_id=0, has_side_effects=True, vmem_limit_bytes=44 * 2**20
         ),
-    )(ids, embed, low, high, levels, mix, cot)
+    )(*arguments)
 
 
 def finish_kernel(
@@ -388,22 +460,17 @@
         hot = jnp.concatenate([hot, hot, hot], axis=0)
         x = lax.dot_general(hot, table, (((0,), (0,)), ((), ())), preferred_element_type=F32)
         out_ref[rows, :] = x + dot(hidden_ref[rows, :], mix_in_ref[...])
-    for chunk in range(8):
-        for tile in range(8):
-            row = 32 * chunk + 8 * (tile // 2)
-            start = LANES * (tile % 2)
-            mix_ref[row : row + 8, start : start + LANES] = scale * whole[chunk, tile]
-    quarters = [
-        scale * jnp.concatenate([whole[2 * quarter, 8], whole[2 * quarter + 1, 8]], axis=1)
-        for quarter in range(4)
-    ]
-    embed_ref[0:8, :] = quarters[2]
-    embed_ref[8:16, :] = quarters[3]
-    shifted = [quarters[row // 8][row % 8 : row % 8 + 1] for row in range(1, 14)]
-    zero_inner, one_inner = quarters[1][6:7], quarters[1][7:8]
+    for chunk in range(CHUNKS):
+        for row in range(8):
+            mix_ref[8 * chunk + row : 8 * chunk + row + 1, :] = scale * whole[9 * chunk + row]
+    summed = [scale * whole[9 * chunk + 8] for chunk in range(CHUNKS)]
+    for name in range(VOCAB):
+        embed_ref[name : name + 1, :] = summed[16 + name]
+    shifted = summed[1:14]
+    zero_inner, one_inner = summed[14], summed[15]
     low, high, levels = rows_of(low_ref), rows_of(high_ref), rows_of(levels_ref)
     folded, _ = level_factors(low, high, levels)
-    current = quarters[0][0:1]
+    current = summed[0]
     low_zero, low_one = zero_inner / low[0], one_inner / low[1]
     high_zero = high_one = jnp.zeros_like(current)
     for level in range(LEVELS):
@@ -434,7 +501,7 @@
         ),
         in_specs=[vmem] * 8,
         out_specs=(vmem,) * 5,
-        compiler_params=pltpu.CompilerParams(vmem_limit_bytes=56 * 2**20),
+        compiler_params=pltpu.CompilerParams(vmem_limit_bytes=16 * 2**20),
     )(ids, hidden, whole, embed, mix, low, high, levels)
 
 

time: 45.2 us -> 45.9 us (1.015)
  local copies, waits for them, and re-layouts: 0 us -> 5.42 us
  Pallas kernels: 44.4 us -> 39.4 us
    unnamed x0 -> x14, local copies, waits for them, and re-layouts: none -> 5.42 us
    pallas_call x1, Pallas kernels: 41.7 us -> 37.8 us  [layer(): pl.pallas_call(functools.partial(layer_kernel, count), out_shape=(jax.Sha...]
    pallas_call x1, Pallas kernels: 2.68 us -> 1.6 us  [finish(): pl.pallas_call(functools.partial(finish_kernel, scale), out_shape=(jax.Sh...]
where the time goes in v4:
time: 45.9 us; the launch traced here: 45.5 us
  Pallas kernels  39.4 us (86%)
  local copies, waits for them, and re-layouts  5.42 us (12%)
  between operations  0.66 us (1%)
    pallas_call x1, Pallas kernels, layer(): pl.pallas_call(functools.partial(layer_kernel, count), out_shape=(jax.Sha...  37.8 us
    unnamed x14, local copies, waits for them, and re-layouts  5.42 us
    pallas_call x1, Pallas kernels, finish(): pl.pallas_call(functools.partial(finish_kernel, scale), out_shape=(jax.Sh...  1.6 us

profile of v4, /device:TPU:1, one launch (start us, length us, event | category | flops | bytes accessed | tf_op | source)
XLA Modules:
  0.0 45.5 jit_solution(14530471031238855699)
XLA Ops:
  0.6 0.0 copy-start.5
  0.6 0.7 %copy-done.5 = f32[2,256]{1,0:T(2,128)S(1)} copy-done((f32[2,256]{1,0:T(2,128)S(1)}, f32[2,256]{1,0:T(2,128)}, u32[]{:S(2)}) %copy-start.5) | copy-done | bytes 2072
  1.3 0.0 copy-start
  1.3 1.0 %copy-done = bf16[1,1024,256]{2,1,0:T(8,128)(2,1)S(1)} copy-done((bf16[1,1024,256]{2,1,0:T(8,128)(2,1)S(1)}, bf16[1,1024,256]{2,1,0:T(8,128)(2,1)}, u32[]{:S(2)}) %copy-start) | copy-done | bytes 524312
  2.4 0.0 copy-start.1
  2.4 0.9 %copy-done.1 = bf16[256,256]{1,0:T(8,128)(2,1)S(1)} copy-done((bf16[256,256]{1,0:T(8,128)(2,1)S(1)}, bf16[256,256]{1,0:T(8,128)(2,1)}, u32[]{:S(2)}) %copy-start.1) | copy-done | bytes 131096
  3.3 0.0 copy-start.2
  3.3 0.7 %copy-done.2 = f32[16,256]{1,0:T(8,128)S(1)} copy-done((f32[16,256]{1,0:T(8,128)S(1)}, f32[16,256]{1,0:T(8,128)}, u32[]{:S(2)}) %copy-start.2) | copy-done | bytes 16408
  4.0 0.0 copy-start.3
  4.0 0.7 %copy-done.3 = f32[14,256]{1,0:T(8,128)S(1)} copy-done((f32[14,256]{1,0:T(8,128)S(1)}, f32[14,256]{1,0:T(8,128)}, u32[]{:S(2)}) %copy-start.3) | copy-done | bytes 14360
  4.7 0.0 copy-start.4
  4.7 0.7 %copy-done.4 = s32[1,1024]{1,0:T(1,128)S(1)} copy-done((s32[1,1024]{1,0:T(1,128)S(1)}, s32[1,1024]{1,0:T(1,128)}, u32[]{:S(2)}) %copy-start.4) | copy-done | bytes 4120
  5.4 0.0 copy-start.6
  5.4 0.7 %copy-done.6 = f32[2,256]{1,0:T(2,128)S(1)} copy-done((f32[2,256]{1,0:T(2,128)S(1)}, f32[2,256]{1,0:T(2,128)}, u32[]{:S(2)}) %copy-start.6) | copy-done | bytes 2072
  6.1 37.8 %shard_map.110 = (bf16[1024,256]{1,0:T(8,128)(2,1)S(1)}, f32[288,1,256]{2,1,0:T(1,128)S(1)}) custom-call(s32[8,128]{1,0:T(8,128)S(1)} %bitcast.4, f32[16,256]{1,0:T(8,128)S(1)} %copy-done.2, f32[2,256]{1,0:T(2,128)S(1)} %copy-done.5, f32[2,256]{1,0:T(2,128)S(1)} %copy-done.6, f32[14,256]{1,0:T(8,128)S(1)} %copy-done.3, bf16[256,256]{1,0:T(8,128)(2,1)S(1)} %copy-done.1, ...), custom_call_target="tpu_custom_call" | custom-call | tf_op jit(solution)/shard_map/pallas_call | solution.py:406
  43.9 1.6 %shard_map.111 = (f32[1024,256]{1,0:T(8,128)}, f32[2,2,256]{2,1,0:T(2,128)}, f32[14,256]{1,0:T(8,128)}, f32[256,256]{1,0:T(8,128)}, f32[16,256]{1,0:T(8,128)}) custom-call(s32[8,128]{1,0:T(8,128)S(1)} %bitcast.5, bf16[1024,256]{1,0:T(8,128)(2,1)S(1)} %get-tuple-element.12.hidden_ref, f32[288,1,256]{2,1,0:T(1,128)S(1)} %get-tuple-element.13.whole, ...), custom_call_target="tpu_custom_call" | custom-call | tf_op jit(solution)/shard_map/pallas_call | solution.py:493
Async XLA Ops:
  0.6 0.7 %copy-start.5 = (f32[2,256]{1,0:T(2,128)S(1)}, f32[2,256]{1,0:T(2,128)}, u32[]{:S(2)}) copy-start(f32[2,256]{1,0:T(2,128)} %low_ref.1) | copy-start | bytes 6148
  1.3 1.0 %copy-start = (bf16[1,1024,256]{2,1,0:T(8,128)(2,1)S(1)}, bf16[1,1024,256]{2,1,0:T(8,128)(2,1)}, u32[]{:S(2)}) copy-start(bf16[1,1024,256]{2,1,0:T(8,128)(2,1)} %param.13) | copy-start | bytes 1572868
  2.4 0.9 %copy-start.1 = (bf16[256,256]{1,0:T(8,128)(2,1)S(1)}, bf16[256,256]{1,0:T(8,128)(2,1)}, u32[]{:S(2)}) copy-start(bf16[256,256]{1,0:T(8,128)(2,1)} %mix_in_ref.1) | copy-start | bytes 393220
  3.3 0.7 %copy-start.2 = (f32[16,256]{1,0:T(8,128)S(1)}, f32[16,256]{1,0:T(8,128)}, u32[]{:S(2)}) copy-start(f32[16,256]{1,0:T(8,128)} %embed_in_ref.1) | copy-start | bytes 49156
  4.0 0.7 %copy-start.3 = (f32[14,256]{1,0:T(8,128)S(1)}, f32[14,256]{1,0:T(8,128)}, u32[]{:S(2)}) copy-start(f32[14,256]{1,0:T(8,128)} %levels_ref.1) | copy-start | bytes 43012
  4.7 0.7 %copy-start.4 = (s32[1,1024]{1,0:T(1,128)S(1)}, s32[1,1024]{1,0:T(1,128)}, u32[]{:S(2)}) copy-start(s32[1,1024]{1,0:T(1,128)} %param.7) | copy-start | bytes 12292
  5.4 0.7 %copy-start.6 = (f32[2,256]{1,0:T(2,128)S(1)}, f32[2,256]{1,0:T(2,128)}, u32[]{:S(2)}) copy-start(f32[2,256]{1,0:T(2,128)} %high_ref.1) | copy-start | bytes 6148

commit v5 on v4

--- a/solution.py
+++ b/solution.py
@@ -217,6 +217,18 @@
     return mix_sum
 
 
+def outputs(embed, features_ref, hidden_ref, mix_ref, out_ref):
+    high, middle = halves(embed)
+    rest = (embed - high.astype(F32) - middle.astype(F32)).astype(BF16)
+    table = jnp.concatenate([high, middle, rest], axis=0)
+    for start in range(0, TOKENS, 256):
+        span = slice(start, start + 256)
+        hot = features_ref[0:VOCAB, span]
+        hot = jnp.concatenate([hot, hot, hot], axis=0)
+        x = lax.dot_general(hot, table, (((0,), (0,)), ((), ())), preferred_element_type=F32)
+        out_ref[span, :] = x + dot(hidden_ref[span, :], mix_ref[...])
+
+
 def backward(passed, folded, kappa, embed, features_ref, g_ref, cot_ref, z_ref):
     both = dot(features_ref[0 : CLASSES * VOCAB, :], g_ref[...])
     z_ref[...] = both[:, :WIDTH] + both[:, WIDTH:]
@@ -244,10 +256,10 @@
 
 
 def layer_kernel(
-    count, ids_hbm, embed_hbm, low_hbm, high_hbm, levels_hbm, mix_hbm, cot_hbm,
-    hidden_ref, whole,
-    held, ids_send, ids_recv, ones_ref, class_ref, tokens_ref, s7, s8, s9, s10, features_ref, weights_ref, turned_ref,
-    y_ref, g_ref, z_ref, ids_ref, embed_ref, low_ref, high_ref, levels_ref, mix_ref, cot_ref, local_sem,
+    count, scale, ids_hbm, embed_hbm, low_hbm, high_hbm, levels_hbm, mix_hbm, cot_hbm,
+    out_ref, whole, factors_ref,
+    held, ids_sems, ones_ref, class_ref, tokens_ref, s7, s8, s9, s10, features_ref, weights_ref, turned_ref,
+    y_ref, hidden_ref, g_ref, z_ref, ids_ref, embed_ref, low_ref, high_ref, levels_ref, mix_ref, cot_ref, local_sem,
     mix_part, small_part, mix_in, small_in, second, third, sends, recvs,
 ):
     seq, batch = lax.axis_index("seq"), lax.axis_index("batch")
@@ -267,8 +279,9 @@
         return lax.rem(spots[0] + i, 4), lax.rem(spots[1] + j, 4), lax.rem(spots[2] + k, 4)
 
     mine, theirs = along(core), along(1 - core)
-    plane = [(i, j) for i in range(4) for j in range(4)]
-    others = plane[1:]
+    hops = lambda spot: sum(min(step, 4 - step) for step in spot)
+    plane = sorted([(i, j) for i in range(4) for j in range(4)], key=hops, reverse=True)
+    others = plane[:-1]
     own_peer = lambda i, j, k: device(core, moved(mine, i, j, k), core)
     their_peer = lambda i, j: device(1 - core, moved(theirs, i, j, 0), 1 - core)
     cross_peer = lambda i, j: device(core, moved(mine, i, j, 0), 1 - core)
@@ -314,12 +327,12 @@
         copy.start()
         return copy
 
-    id_copies = [
-        copy_to(
-            ids_hbm, held.at[step], ids_send.at[step], ids_recv.at[step], (lax.rem(seq + step + 1, count), batch)
-        )
-        for step in range(BACK)
-    ]
+    def drain(ref, sem):
+        pltpu.make_async_copy(ref, ref, sem).wait()
+
+    for step in reversed(range(BACK)):
+        received = ids_sems.at[1 if step else 0]
+        copy_to(ids_hbm, held.at[step], ids_sems.at[2], received, (lax.rem(seq + step + 1, count), batch))
 
     for load in loads:
         load.wait()
@@ -335,86 +348,90 @@
     make_hot(tokens_ref, 8 * BACK, ids_ref[...])
 
     def receive(step):
-        id_copies[step].wait()
         make_hot(tokens_ref, 8 * (BACK - 1 - step), jnp.where(seq > step, held[step], -1))
 
+    drain(held.at[0], ids_sems.at[0])
     receive(0)
     make_near(tokens_ref, class_ref, ones_ref, s7, s8, s9, features_ref)
     near_part(turned_ref, features_ref, y_ref)
+    factors_ref[0:2, :] = low_ref[...]
+    factors_ref[2:4, :] = high_ref[...]
+    factors_ref[4:18, :] = levels_ref[...]
+    for level in range(LEVELS + 1):
+        factors_ref[18 + level : 19 + level, :] = folded[level]
+    drain(held.at[pl.ds(1, BACK - 1)], ids_sems.at[1])
     for step in range(1, BACK):
         receive(step)
     make_far(tokens_ref, ones_ref, s7, s8, s9, s10, features_ref)
     mix_sum = forward(turned_ref, features_ref, y_ref, mix_ref, cot_ref, hidden_ref, g_ref)
 
+    home = chunk_of(core, mine)
+
     def spread(phase, part, target):
-        copies = []
-        for slot, (i, j) in enumerate(others):
-            place = chunk_of(core, moved(mine, i, j, 0))
-            copies.append(
-                copy_to(part.at[place], target.at[slot], sends.at[phase, slot], recvs.at[phase, slot], own_peer(i, j, 0))
-            )
-        for slot, (i, j) in enumerate(plane, 15):
+        for slot, (i, j) in enumerate(plane):
             place = chunk_of(1 - core, moved(theirs, i, j, 0))
-            copies.append(
-                copy_to(part.at[place], target.at[slot], sends.at[phase, slot], recvs.at[phase, slot], their_peer(i, j))
-            )
-        return copies
-
-    home = chunk_of(core, mine)
+            copy_to(part.at[place], target.at[slot + 15], sends.at[phase], recvs.at[phase], their_peer(i, j))
+            if (i, j) in others:
+                place = chunk_of(core, moved(mine, i, j, 0))
+                copy_to(part.at[place], target.at[slot], sends.at[phase], recvs.at[phase], own_peer(i, j, 0))
+
     for chunk in range(CHUNKS):
-        mix_part[chunk] = mix_sum[8 * chunk : 8 * chunk + 8]
-    mix_copies = spread(0, mix_part, mix_in)
-    small = backward(passed, folded, kappa, embed, features_ref, g_ref, cot_ref, z_ref)
+        mix_part[chunk] = scale * mix_sum[8 * chunk : 8 * chunk + 8]
+    spread(0, mix_part, mix_in)
+    small = scale * backward(passed, folded, kappa, embed, features_ref, g_ref, cot_ref, z_ref)
     for chunk in range(CHUNKS):
         small_part[chunk] = small[chunk : chunk + 1]
-    small_copies = spread(1, small_part, small_in)
-    for copy in mix_copies:
-        copy.wait()
+    spread(1, small_part, small_in)
+    drain(mix_in, recvs.at[0])
     mixed = mix_part[home]
     for slot in range(CHUNKS - 1):
         mixed = mixed + mix_in[slot]
     for row in range(8):
         second[mine[2], row] = mixed[row : row + 1]
-    for copy in small_copies:
-        copy.wait()
+    drain(small_in, recvs.at[1])
     row = small_part[home]
     for slot in range(CHUNKS - 1):
         row = row + small_in[slot]
     second[mine[2], 8] = row
     spot = second.at[mine[2]]
-    copies = [
-        copy_to(spot, spot, sends.at[2, k], recvs.at[2, k], own_peer(0, 0, k)) for k in range(1, 4)
-    ]
-    for copy in copies:
-        copy.wait()
+    for k in (2, 1, 3):
+        copy_to(spot, spot, sends.at[2], recvs.at[2], own_peer(0, 0, k))
+    outputs(embed, features_ref, hidden_ref, mix_ref, out_ref)
+    drain(second.at[pl.ds(0, 3)], recvs.at[2])
     third[...] = (second[0] + second[1]) + (second[2] + second[3])
     landing = whole.at[pl.ds(9 * home, 9)]
-    copies = []
-    for slot, (i, j) in enumerate(others):
-        copies.append(copy_to(third, landing, sends.at[3, slot], recvs.at[3, slot], own_peer(i, j, 0)))
-    for slot, (i, j) in enumerate(plane, 15):
-        copies.append(copy_to(third, landing, sends.at[3, slot], recvs.at[3, slot], cross_peer(i, j)))
+    for i, j in plane:
+        copy_to(third, landing, sends.at[3], recvs.at[3], cross_peer(i, j))
+        if (i, j) in others:
+            copy_to(third, landing, sends.at[3], recvs.at[3], own_peer(i, j, 0))
     whole[pl.ds(9 * home, 9)] = third[...]
-    for copy in copies:
-        copy.wait()
-
-
-def layer(count, ids, embed, low, high, levels, mix, cot):
+    drain(held, ids_sems.at[2])
+    drain(mix_in, sends.at[0])
+    drain(small_in, sends.at[1])
+    drain(second.at[pl.ds(0, 3)], sends.at[2])
+    gathered = whole.at[pl.ds(0, 9 * (CHUNKS - 1))]
+    drain(gathered, recvs.at[3])
+    drain(gathered, sends.at[3])
+
+
+def layer(count, scale, ids, embed, low, high, levels, mix, cot):
     vmem = pl.BlockSpec(memory_space=pltpu.VMEM)
     far = pl.BlockSpec(memory_space=pltpu.HBM)
-    arguments = (ids, embed, low, high, levels, mix, cot)
+    arguments = tuple(
+        pltpu.with_memory_space_constraint(array, pltpu.HBM) for array in (ids, embed, low, high, levels, mix, cot)
+    )
     return pl.pallas_call(
-        functools.partial(layer_kernel, count),
+        functools.partial(layer_kernel, count, scale),
         out_shape=(
-            jax.ShapeDtypeStruct((TOKENS, WIDTH), BF16),
+            jax.ShapeDtypeStruct((TOKENS, WIDTH), F32),
             jax.ShapeDtypeStruct((9 * CHUNKS, 1, WIDTH), F32),
+            jax.ShapeDtypeStruct((32, WIDTH), F32),
         ),
         in_specs=[far] * 7,
-        out_specs=(vmem, vmem),
+        out_specs=(vmem,) * 3,
         scratch_shapes=[
             pltpu.VMEM((BACK, 8, LANES), jnp.int32),
-            pltpu.SemaphoreType.DMA((BACK,)),
-            pltpu.SemaphoreType.DMA((BACK,)),
+            pltpu.SemaphoreType.DMA((3,)),
             pltpu.VMEM((2 * LANES, 8 * LANES), BF16),
             pltpu.VMEM((2 * LANES, 29 * LANES), BF16),
             pltpu.VMEM((TILES * VOCAB, 2 * LANES), BF16),
@@ -426,6 +443,7 @@
             pltpu.VMEM((ROWS, 2 * WIDTH), BF16),
             pltpu.VMEM((2 * WIDTH, ROWS), BF16),
             pltpu.VMEM((WIDTH, TOKENS), F32),
+            pltpu.VMEM((TOKENS, WIDTH), BF16),
             pltpu.VMEM((TOKENS, 2 * WIDTH), BF16),
             pltpu.VMEM((CLASSES * VOCAB, WIDTH), F32),
             *[pltpu.VMEM(array.shape, array.dtype) for array in arguments],
@@ -436,8 +454,8 @@
             pltpu.VMEM((CHUNKS - 1, 1, WIDTH), F32),
             pltpu.VMEM((4, 9, 1, WIDTH), F32),
             pltpu.VMEM((9, 1, WIDTH), F32),
-            pltpu.SemaphoreType.DMA((4, CHUNKS)),
-            pltpu.SemaphoreType.DMA((4, CHUNKS)),
+            pltpu.SemaphoreType.DMA((4,)),
+            pltpu.SemaphoreType.DMA((4,)),
         ],
         compiler_params=pltpu.CompilerParams(
             collective_id=0, has_side_effects=True, vmem_limit_bytes=44 * 2**20
@@ -446,32 +464,21 @@
 
 
 def finish_kernel(
-    scale, ids_ref, hidden_ref, whole, embed_in_ref, mix_in_ref, low_ref, high_ref, levels_ref,
-    out_ref, filters_ref, grad_levels_ref, mix_ref, embed_ref,
+    out_ref, whole, factors_ref, out_hbm, filters_ref, grad_levels_ref, mix_ref, embed_ref, sem
 ):
-    embed = embed_in_ref[...]
-    high_part, middle = halves(embed)
-    rest = (embed - high_part.astype(F32) - middle.astype(F32)).astype(BF16)
-    table = jnp.concatenate([high_part, middle, rest], axis=0)
-    names = lax.broadcasted_iota(jnp.int32, (VOCAB, LANES), 0)
-    for tile in range(8):
-        rows = slice(tile * LANES, (tile + 1) * LANES)
-        hot = where_is(names, jnp.broadcast_to(ids_ref[tile : tile + 1, :], (VOCAB, LANES)))
-        hot = jnp.concatenate([hot, hot, hot], axis=0)
-        x = lax.dot_general(hot, table, (((0,), (0,)), ((), ())), preferred_element_type=F32)
-        out_ref[rows, :] = x + dot(hidden_ref[rows, :], mix_in_ref[...])
+    store = pltpu.make_async_copy(out_ref, out_hbm, sem)
+    store.start()
     for chunk in range(CHUNKS):
         for row in range(8):
-            mix_ref[8 * chunk + row : 8 * chunk + row + 1, :] = scale * whole[9 * chunk + row]
-    summed = [scale * whole[9 * chunk + 8] for chunk in range(CHUNKS)]
+            mix_ref[8 * chunk + row : 8 * chunk + row + 1, :] = whole[9 * chunk + row]
+    summed = [whole[9 * chunk + 8] for chunk in range(CHUNKS)]
     for name in range(VOCAB):
         embed_ref[name : name + 1, :] = summed[16 + name]
     shifted = summed[1:14]
-    zero_inner, one_inner = summed[14], summed[15]
-    low, high, levels = rows_of(low_ref), rows_of(high_ref), rows_of(levels_ref)
-    folded, _ = level_factors(low, high, levels)
+    factors = rows_of(factors_ref)
+    low, high, levels, folded = factors[0:2], factors[2:4], factors[4:18], factors[18:32]
     current = summed[0]
-    low_zero, low_one = zero_inner / low[0], one_inner / low[1]
+    low_zero, low_one = summed[14] / low[0], summed[15] / low[1]
     high_zero = high_one = jnp.zeros_like(current)
     for level in range(LEVELS):
         late = shifted[level]
@@ -486,12 +493,13 @@
     filters_ref[0, 1:2, :] = low_one
     filters_ref[1, 0:1, :] = high_zero
     filters_ref[1, 1:2, :] = high_one
-
-
-def finish(scale, ids, hidden, whole, embed, mix, low, high, levels):
+    store.wait()
+
+
+def finish(out, whole, factors):
     vmem = pl.BlockSpec(memory_space=pltpu.VMEM)
     return pl.pallas_call(
-        functools.partial(finish_kernel, scale),
+        finish_kernel,
         out_shape=(
             jax.ShapeDtypeStruct((TOKENS, WIDTH), F32),
             jax.ShapeDtypeStruct((2, 2, WIDTH), F32),
@@ -499,20 +507,20 @@
             jax.ShapeDtypeStruct((WIDTH, WIDTH), F32),
             jax.ShapeDtypeStruct((VOCAB, WIDTH), F32),
         ),
-        in_specs=[vmem] * 8,
-        out_specs=(vmem,) * 5,
+        in_specs=[vmem] * 3,
+        out_specs=(pl.BlockSpec(memory_space=pl.ANY),) + (vmem,) * 4,
+        scratch_shapes=[pltpu.SemaphoreType.DMA],
         compiler_params=pltpu.CompilerParams(vmem_limit_bytes=16 * 2**20),
-    )(ids, hidden, whole, embed, mix, low, high, levels)
+    )(out, whole, factors)
 
 
 def per_device(ids, embed, low_filter, high_filter, level_weights, mix, cotangent):
     count = lax.axis_size("seq")
-    ids = ids.reshape(8, LANES)
-    hidden, whole = layer(count, ids, embed, low_filter, high_filter, level_weights, mix, cotangent[0])
     scale = 1.0 / math.sqrt(count * lax.axis_size("batch") * TOKENS)
-    out, grad_filters, grad_levels, grad_mix, grad_embed = finish(
-        scale, ids, hidden, whole, embed, mix, low_filter, high_filter, level_weights
+    out, whole, factors = layer(
+        count, scale, ids.reshape(8, LANES), embed, low_filter, high_filter, level_weights, mix, cotangent[0]
     )
+    out, grad_filters, grad_levels, grad_mix, grad_embed = finish(out, whole, factors)
     return out[None], grad_filters, grad_levels, grad_mix, grad_embed
 
 

time: 45.9 us -> 37.5 us (0.82)
  local copies, waits for them, and re-layouts: 5.42 us -> 0 us
  Pallas kernels: 39.4 us -> 36.8 us
    unnamed x14 -> x0, local copies, waits for them, and re-layouts: 5.42 us -> none
    pallas_call x2, Pallas kernels: 39.4 us -> 36.8 us  [the longest x1 35.1 us: layer(): pl.pallas_call(functools.partial(layer_kernel, count, scale), out_shape=(...]
where the time goes in v5:
time: 37.5 us; the launch traced here: 37.4 us
  Pallas kernels  36.8 us (98%)
  between operations  0.64 us (2%)
    pallas_call x1, Pallas kernels, layer(): pl.pallas_call(functools.partial(layer_kernel, count, scale), out_shape=(...  35.1 us
    pallas_call x1, Pallas kernels, finish(): pl.pallas_call(finish_kernel, out_shape=(jax.ShapeDtypeStruct((TOKENS, WI...  1.69 us

profile of v5, /device:TPU:1, one launch (start us, length us, event | category | flops | bytes accessed | tf_op | source)
XLA Modules:
  0.0 37.4 jit_solution(5968453455595516325)
XLA Ops:
  0.6 35.1 %shard_map.110 = (f32[1024,256]{1,0:T(8,128)S(1)}, f32[288,1,256]{2,1,0:T(1,128)S(1)}, f32[32,256]{1,0:T(8,128)S(1)}) custom-call(s32[8,128]{1,0:T(8,128)} %bitcast.4, f32[16,256]{1,0:T(8,128)} %embed_hbm.1, f32[2,256]{1,0:T(2,128)} %low_hbm.1, f32[2,256]{1,0:T(2,128)} %high_hbm.1, f32[14,256]{1,0:T(8,128)} %levels_hbm.1, bf16[256,256]{1,0:T(8,128)(2,1)} %mix_hbm.1, ...), custom_call_target="tpu_custom_call" | custom-call | tf_op jit(solution)/shard_map/pallas_call | solution.py:423
  35.7 1.7 %shard_map.111 = (f32[1024,256]{1,0:T(8,128)}, f32[2,2,256]{2,1,0:T(2,128)}, f32[14,256]{1,0:T(8,128)}, f32[256,256]{1,0:T(8,128)}, f32[16,256]{1,0:T(8,128)}) custom-call(f32[1024,256]{1,0:T(8,128)S(1)} %get-tuple-element.13.out_ref, f32[288,1,256]{2,1,0:T(1,128)S(1)} %get-tuple-element.14.whole, f32[32,256]{1,0:T(8,128)S(1)} %get-tuple-element.15.factors_ref), custom_call_target="tpu_custom_call" | custom-call | tf_op jit(solution)/shard_map/pallas_call | solution.py:501

commit v6 on v5

--- a/solution.py
+++ b/solution.py
@@ -17,14 +17,15 @@
 TOKENS = 1024
 BACK = 8
 TILES = (BACK + 1) * TOKENS // LANES
-CLASSES = 1 + LEVELS * (LEVELS + 1) // 2
+CLASSES = 93
 ROWS = 96 * VOCAB
 NEAR = 56 * VOCAB
+LAST = 80 * VOCAB
 CHUNKS = 32
 
 
 def class_of(level, ones):
-    return 1 + level * (level + 1) // 2 + ones
+    return 1 + level * (level + 1) // 2 + ones + level // 12
 
 
 def block_of(level, ones):
@@ -64,6 +65,11 @@
     return lambda level, ones: chains[0][level - ones] * chains[1][ones]
 
 
+def clear_padding(ref):
+    for rows in (slice(LAST - VOCAB, LAST), slice(CLASSES * VOCAB, ROWS)):
+        ref[rows, :] = jnp.zeros((rows.stop - rows.start, ref.shape[1]), BF16)
+
+
 def make_weights(passed, folded, kappa, embed, weights_ref):
     def put(rows, factor):
         high, rest = halves(factor * embed)
@@ -74,7 +80,7 @@
     for level in range(LEVELS):
         for ones in range(level + 1):
             put(block_of(level, ones), kappa[level] * passed(level, ones))
-    weights_ref[CLASSES * VOCAB :, :] = jnp.zeros((ROWS - CLASSES * VOCAB, 2 * WIDTH), BF16)
+    clear_padding(weights_ref)
 
 
 def where_is(table, value):
@@ -167,14 +173,21 @@
     place_level(s9, 9, features_ref)
 
 
-def make_far(tokens_ref, ones_ref, s7, s8, s9, s10, features_ref):
-    count_tiles(tokens_ref, ones_ref, s7, 1, 57)
-    widen(s7, s8, 7, 2, 58)
-    widen(s8, s9, 8, 4, 60)
-    widen(s9, s10, 9, 8, 64)
+def make_middle(tokens_ref, ones_ref, s7, s8, s9, s10, features_ref):
+    count_tiles(tokens_ref, ones_ref, s7, 33, 57)
+    widen(s7, s8, 7, 34, 58)
+    widen(s8, s9, 8, 36, 60)
+    widen(s9, s10, 9, 40, 64)
     place_level(s10, 10, features_ref)
     for ones in range(12):
         features_ref[block_of(11, ones), :] = widened(s10, 10, ones, 48, 56)
+
+
+def make_last(tokens_ref, ones_ref, s7, s8, s9, s10, features_ref):
+    count_tiles(tokens_ref, ones_ref, s7, 1, 33)
+    widen(s7, s8, 7, 2, 34)
+    widen(s8, s9, 8, 4, 36)
+    widen(s9, s10, 9, 8, 40)
     for ones in range(13):
         near, late = widened(s10, 10, ones, 32, 40), widened(s10, 10, ones - 1, 16, 24)
         features_ref[block_of(12, ones), :] = late if near is None else near if late is None else near + late
@@ -189,30 +202,34 @@
     return y * half, slope
 
 
-def near_part(turned_ref, features_ref, y_ref):
+def add_part(turned_ref, features_ref, y_ref, first, last):
     for start in range(0, TOKENS, 256):
         span = slice(start, start + 256)
-        both = dot(turned_ref[:, 0:NEAR], features_ref[0:NEAR, span])
-        y_ref[:, span] = both[:WIDTH] + both[WIDTH:]
-
-
-def forward(turned_ref, features_ref, y_ref, mix_ref, cot_ref, hidden_ref, g_ref):
-    mix = mix_ref[...]
+        both = dot(turned_ref[:, first:last], features_ref[first:last, span])
+        part = both[:WIDTH] + both[WIDTH:]
+        y_ref[:, span] = part if first == 0 else y_ref[:, span] + part
+
+
+def before_gelu(mix_ref, cot_ref, g_hidden_ref):
+    g_hidden_ref[...] = lax.dot_general(
+        cot_ref[...], mix_ref[...], (((1,), (1,)), ((), ())), preferred_element_type=F32
+    )
+
+
+def forward(turned_ref, features_ref, y_ref, g_hidden_ref, cot_ref, hidden_ref, g_ref):
     mix_sum = None
     block = 256
     for start in range(0, TOKENS, block):
         span = slice(start, start + block)
-        both = dot(turned_ref[:, NEAR:], features_ref[NEAR:, span])
+        both = dot(turned_ref[:, LAST:], features_ref[LAST:, span])
         y = (y_ref[:, span] + both[:WIDTH] + both[WIDTH:]).T
         active, slope = gelu_parts(y)
         hidden = active.astype(BF16)
         hidden_ref[span, :] = hidden
-        cot = cot_ref[span, :]
-        g_hidden = lax.dot_general(cot, mix, (((1,), (1,)), ((), ())), preferred_element_type=F32)
-        g_high, g_rest = halves(g_hidden * slope)
+        g_high, g_rest = halves(g_hidden_ref[span, :] * slope)
         g_ref[span, 0:WIDTH] = g_high
         g_ref[span, WIDTH:] = g_rest
-        term = lax.dot_general(hidden, cot, (((0,), (0,)), ((), ())), preferred_element_type=F32)
+        term = lax.dot_general(hidden, cot_ref[span, :], (((0,), (0,)), ((), ())), preferred_element_type=F32)
         mix_sum = term if mix_sum is None else mix_sum + term
     return mix_sum
 
@@ -230,17 +247,25 @@
 
 
 def backward(passed, folded, kappa, embed, features_ref, g_ref, cot_ref, z_ref):
-    both = dot(features_ref[0 : CLASSES * VOCAB, :], g_ref[...])
-    z_ref[...] = both[:, :WIDTH] + both[:, WIDTH:]
-
     def over_names(value):
         return jnp.sum(embed * value, axis=0, keepdims=True)
 
-    z0 = z_ref[0:VOCAB, :]
-    rows = [over_names(z0)]
-    embed_sum = folded[0] * z0 + dot(features_ref[0:VOCAB, :], cot_ref[...])
-    zero_sum = one_sum = jnp.zeros_like(z0)
+    def products(first, last):
+        both = dot(features_ref[first:last, :], g_ref[...])
+        z_ref[first:last, :] = both[:, :WIDTH] + both[:, WIDTH:]
+
+    ends = {0: class_of(8, 0) * VOCAB, 8: class_of(11, 0) * VOCAB, 11: CLASSES * VOCAB}
+    begin = 0
+    rows = []
     for level in range(LEVELS):
+        if level in ends:
+            products(begin, ends[level])
+            begin = ends[level]
+        if level == 0:
+            z0 = z_ref[0:VOCAB, :]
+            rows.append(over_names(z0))
+            embed_sum = folded[0] * z0 + dot(features_ref[0:VOCAB, :], cot_ref[...])
+            zero_sum = one_sum = jnp.zeros_like(z0)
         total = passed(level, 0) * z_ref[block_of(level, 0), :]
         counted = jnp.zeros_like(total)
         for ones in range(1, level + 1):
@@ -259,7 +284,7 @@
     count, scale, ids_hbm, embed_hbm, low_hbm, high_hbm, levels_hbm, mix_hbm, cot_hbm,
     out_ref, whole, factors_ref,
     held, ids_sems, ones_ref, class_ref, tokens_ref, s7, s8, s9, s10, features_ref, weights_ref, turned_ref,
-    y_ref, hidden_ref, g_ref, z_ref, ids_ref, embed_ref, low_ref, high_ref, levels_ref, mix_ref, cot_ref, local_sem,
+    y_ref, g_hidden_ref, hidden_ref, g_ref, z_ref, ids_ref, embed_ref, low_ref, high_ref, levels_ref, mix_ref, cot_ref, local_sem,
     mix_part, small_part, mix_in, small_in, second, third, sends, recvs,
 ):
     seq, batch = lax.axis_index("seq"), lax.axis_index("batch")
@@ -330,9 +355,11 @@
     def drain(ref, sem):
         pltpu.make_async_copy(ref, ref, sem).wait()
 
-    for step in reversed(range(BACK)):
-        received = ids_sems.at[1 if step else 0]
-        copy_to(ids_hbm, held.at[step], ids_sems.at[2], received, (lax.rem(seq + step + 1, count), batch))
+    arrivals = [(0, 1), (1, 4), (4, BACK)]
+    for group, (first, last) in reversed(list(enumerate(arrivals))):
+        for step in range(first, last):
+            peer = lax.rem(seq + step + 1, count), batch
+            copy_to(ids_hbm, held.at[step], ids_sems.at[3], ids_sems.at[group], peer)
 
     for load in loads:
         load.wait()
@@ -344,26 +371,31 @@
     turned_ref[...] = weights_ref[...].T
     make_tables(ones_ref, class_ref)
     tokens_ref[0:VOCAB, LANES:] = jnp.zeros((VOCAB, LANES), BF16)
-    features_ref[CLASSES * VOCAB :, :] = jnp.zeros((ROWS - CLASSES * VOCAB, TOKENS), BF16)
+    clear_padding(features_ref)
+    before_gelu(mix_ref, cot_ref, g_hidden_ref)
     make_hot(tokens_ref, 8 * BACK, ids_ref[...])
 
-    def receive(step):
-        make_hot(tokens_ref, 8 * (BACK - 1 - step), jnp.where(seq > step, held[step], -1))
-
-    drain(held.at[0], ids_sems.at[0])
-    receive(0)
-    make_near(tokens_ref, class_ref, ones_ref, s7, s8, s9, features_ref)
-    near_part(turned_ref, features_ref, y_ref)
     factors_ref[0:2, :] = low_ref[...]
     factors_ref[2:4, :] = high_ref[...]
     factors_ref[4:18, :] = levels_ref[...]
     for level in range(LEVELS + 1):
         factors_ref[18 + level : 19 + level, :] = folded[level]
-    drain(held.at[pl.ds(1, BACK - 1)], ids_sems.at[1])
-    for step in range(1, BACK):
-        receive(step)
-    make_far(tokens_ref, ones_ref, s7, s8, s9, s10, features_ref)
-    mix_sum = forward(turned_ref, features_ref, y_ref, mix_ref, cot_ref, hidden_ref, g_ref)
+
+    def receive(group):
+        first, last = arrivals[group]
+        drain(held.at[pl.ds(first, last - first)], ids_sems.at[group])
+        for step in range(first, last):
+            make_hot(tokens_ref, 8 * (BACK - 1 - step), jnp.where(seq > step, held[step], -1))
+
+    receive(0)
+    make_near(tokens_ref, class_ref, ones_ref, s7, s8, s9, features_ref)
+    add_part(turned_ref, features_ref, y_ref, 0, NEAR)
+    receive(1)
+    make_middle(tokens_ref, ones_ref, s7, s8, s9, s10, features_ref)
+    add_part(turned_ref, features_ref, y_ref, NEAR, LAST)
+    receive(2)
+    make_last(tokens_ref, ones_ref, s7, s8, s9, s10, features_ref)
+    mix_sum = forward(turned_ref, features_ref, y_ref, g_hidden_ref, cot_ref, hidden_ref, g_ref)
 
     home = chunk_of(core, mine)
 
@@ -405,7 +437,7 @@
         if (i, j) in others:
             copy_to(third, landing, sends.at[3], recvs.at[3], own_peer(i, j, 0))
     whole[pl.ds(9 * home, 9)] = third[...]
-    drain(held, ids_sems.at[2])
+    drain(held, ids_sems.at[3])
     drain(mix_in, sends.at[0])
     drain(small_in, sends.at[1])
     drain(second.at[pl.ds(0, 3)], sends.at[2])
@@ -431,7 +463,7 @@
         out_specs=(vmem,) * 3,
         scratch_shapes=[
             pltpu.VMEM((BACK, 8, LANES), jnp.int32),
-            pltpu.SemaphoreType.DMA((3,)),
+            pltpu.SemaphoreType.DMA((4,)),
             pltpu.VMEM((2 * LANES, 8 * LANES), BF16),
             pltpu.VMEM((2 * LANES, 29 * LANES), BF16),
             pltpu.VMEM((TILES * VOCAB, 2 * LANES), BF16),
@@ -443,6 +475,7 @@
             pltpu.VMEM((ROWS, 2 * WIDTH), BF16),
             pltpu.VMEM((2 * WIDTH, ROWS), BF16),
             pltpu.VMEM((WIDTH, TOKENS), F32),
+            pltpu.VMEM((TOKENS, WIDTH), F32),
             pltpu.VMEM((TOKENS, WIDTH), BF16),
             pltpu.VMEM((TOKENS, 2 * WIDTH), BF16),
             pltpu.VMEM((CLASSES * VOCAB, WIDTH), F32),
@@ -464,16 +497,26 @@
 
 
 def finish_kernel(
-    out_ref, whole, factors_ref, out_hbm, filters_ref, grad_levels_ref, mix_ref, embed_ref, sem
+    out_ref, whole, factors_ref,
+    out_hbm, filters_hbm, levels_hbm, mix_hbm, embed_hbm,
+    filters_ref, grad_levels_ref, mix_ref, embed_ref, sems,
 ):
-    store = pltpu.make_async_copy(out_ref, out_hbm, sem)
-    store.start()
+    stores = []
+
+    def store(source, target):
+        copy = pltpu.make_async_copy(source, target, sems.at[len(stores)])
+        copy.start()
+        stores.append(copy)
+
+    store(out_ref, out_hbm)
     for chunk in range(CHUNKS):
         for row in range(8):
             mix_ref[8 * chunk + row : 8 * chunk + row + 1, :] = whole[9 * chunk + row]
+    store(mix_ref, mix_hbm)
     summed = [whole[9 * chunk + 8] for chunk in range(CHUNKS)]
     for name in range(VOCAB):
         embed_ref[name : name + 1, :] = summed[16 + name]
+    store(embed_ref, embed_hbm)
     shifted = summed[1:14]
     factors = rows_of(factors_ref)
     low, high, levels, folded = factors[0:2], factors[2:4], factors[4:18], factors[18:32]
@@ -493,23 +536,20 @@
     filters_ref[0, 1:2, :] = low_one
     filters_ref[1, 0:1, :] = high_zero
     filters_ref[1, 1:2, :] = high_one
-    store.wait()
+    store(filters_ref, filters_hbm)
+    store(grad_levels_ref, levels_hbm)
+    for copy in stores:
+        copy.wait()
 
 
 def finish(out, whole, factors):
-    vmem = pl.BlockSpec(memory_space=pltpu.VMEM)
+    shapes = [(TOKENS, WIDTH), (2, 2, WIDTH), (LEVELS + 1, WIDTH), (WIDTH, WIDTH), (VOCAB, WIDTH)]
     return pl.pallas_call(
         finish_kernel,
-        out_shape=(
-            jax.ShapeDtypeStruct((TOKENS, WIDTH), F32),
-            jax.ShapeDtypeStruct((2, 2, WIDTH), F32),
-            jax.ShapeDtypeStruct((LEVELS + 1, WIDTH), F32),
-            jax.ShapeDtypeStruct((WIDTH, WIDTH), F32),
-            jax.ShapeDtypeStruct((VOCAB, WIDTH), F32),
-        ),
-        in_specs=[vmem] * 3,
-        out_specs=(pl.BlockSpec(memory_space=pl.ANY),) + (vmem,) * 4,
-        scratch_shapes=[pltpu.SemaphoreType.DMA],
+        out_shape=tuple(jax.ShapeDtypeStruct(shape, F32) for shape in shapes),
+        in_specs=[pl.BlockSpec(memory_space=pltpu.VMEM)] * 3,
+        out_specs=(pl.BlockSpec(memory_space=pl.ANY),) * 5,
+        scratch_shapes=[pltpu.VMEM(shape, F32) for shape in shapes[1:]] + [pltpu.SemaphoreType.DMA((5,))],
         compiler_params=pltpu.CompilerParams(vmem_limit_bytes=16 * 2**20),
     )(out, whole, factors)
 

time: 37.5 us -> 37.5 us (level)
    pallas_call x1, Pallas kernels: 1.69 us -> 1.1 us  [finish(): pl.pallas_call(finish_kernel, out_shape=tuple((jax.ShapeDtypeStruct(shape...]
    pallas_call x1, Pallas kernels: 35.1 us -> 35.7 us  [layer(): pl.pallas_call(functools.partial(layer_kernel, count, scale), out_shape=(...]
where the time goes in v6:
time: 37.5 us; the launch traced here: 37.4 us
  Pallas kernels  36.8 us (98%)
  between operations  0.64 us (2%)
    pallas_call x1, Pallas kernels, layer(): pl.pallas_call(functools.partial(layer_kernel, count, scale), out_shape=(...  35.7 us
    pallas_call x1, Pallas kernels, finish(): pl.pallas_call(finish_kernel, out_shape=tuple((jax.ShapeDtypeStruct(shape...  1.1 us

profile of v6, /device:TPU:1, one launch (start us, length us, event | category | flops | bytes accessed | tf_op | source)
XLA Modules:
  0.0 37.4 jit_solution(6460380309798940480)
XLA Ops:
  0.6 35.7 %shard_map.110 = (f32[1024,256]{1,0:T(8,128)S(1)}, f32[288,1,256]{2,1,0:T(1,128)S(1)}, f32[32,256]{1,0:T(8,128)S(1)}) custom-call(s32[8,128]{1,0:T(8,128)} %bitcast.4, f32[16,256]{1,0:T(8,128)} %embed_hbm.1, f32[2,256]{1,0:T(2,128)} %low_hbm.1, f32[2,256]{1,0:T(2,128)} %high_hbm.1, f32[14,256]{1,0:T(8,128)} %levels_hbm.1, bf16[256,256]{1,0:T(8,128)(2,1)} %mix_hbm.1, ...), custom_call_target="tpu_custom_call" | custom-call | tf_op jit(solution)/shard_map/pallas_call | solution.py:455
  36.3 1.1 %shard_map.111 = (f32[1024,256]{1,0:T(8,128)}, f32[2,2,256]{2,1,0:T(2,128)}, f32[14,256]{1,0:T(8,128)}, f32[256,256]{1,0:T(8,128)}, f32[16,256]{1,0:T(8,128)}) custom-call(f32[1024,256]{1,0:T(8,128)S(1)} %get-tuple-element.13.out_ref, f32[288,1,256]{2,1,0:T(1,128)S(1)} %get-tuple-element.14.whole, f32[32,256]{1,0:T(8,128)S(1)} %get-tuple-element.15.factors_ref), custom_call_target="tpu_custom_call" | custom-call | tf_op jit(solution)/shard_map/pallas_call | solution.py:547

commit v7 on v6

--- a/solution.py
+++ b/solution.py
@@ -21,7 +21,9 @@
 ROWS = 96 * VOCAB
 NEAR = 56 * VOCAB
 LAST = 80 * VOCAB
-CHUNKS = 32
+OWNERS = 16
+SHARE = WIDTH // OWNERS
+PART = SHARE + 2
 
 
 def class_of(level, ones):
@@ -292,26 +294,14 @@
     core = lax.rem(batch, 2)
     z = lax.div(seq, 16) * 2 + lax.div(batch, 2)
 
-    def along(order):
-        return x + order * (y - x), y + order * (z - y), z + order * (x - z)
-
-    def device(order, spots, core):
-        a, b, c = spots
-        x, y, z = a + order * (c - a), b + order * (a - b), c + order * (b - c)
-        return lax.div(z, 2) * 16 + y * 4 + x, lax.rem(z, 2) * 2 + core
-
-    def moved(spots, i, j, k):
-        return lax.rem(spots[0] + i, 4), lax.rem(spots[1] + j, 4), lax.rem(spots[2] + k, 4)
-
-    mine, theirs = along(core), along(1 - core)
+    def chip(i, j, k, core):
+        x_to, y_to, z_to = lax.rem(x + i, 4), lax.rem(y + j, 4), lax.rem(z + k, 4)
+        return lax.div(z_to, 2) * 16 + y_to * 4 + x_to, lax.rem(z_to, 2) * 2 + core
+
+    part_of = lambda i, j: 4 * lax.rem(x + i, 4) + lax.rem(y + j, 4)
     hops = lambda spot: sum(min(step, 4 - step) for step in spot)
     plane = sorted([(i, j) for i in range(4) for j in range(4)], key=hops, reverse=True)
     others = plane[:-1]
-    own_peer = lambda i, j, k: device(core, moved(mine, i, j, k), core)
-    their_peer = lambda i, j: device(1 - core, moved(theirs, i, j, 0), 1 - core)
-    cross_peer = lambda i, j: device(core, moved(mine, i, j, 0), 1 - core)
-    chunk_of = lambda core, spots: 16 * core + 4 * spots[0] + spots[1]
-
     barrier = pltpu.get_barrier_semaphore()
 
     def greet(peer):
@@ -320,13 +310,19 @@
     for step in range(1, BACK + 1):
         greet((lax.rem(seq + count - step, count), batch))
     for i, j in others:
-        greet(own_peer(i, j, 0))
-    for k in range(1, 4):
-        greet(own_peer(0, 0, k))
-    for i, j in plane:
-        greet(their_peer(i, j))
-        if i:
-            greet(cross_peer(i + core * (j - i), j + core * (i - j)))
+        greet(chip(i, j, 0, 1))
+
+    @pl.when(core == 0)
+    def _():
+        greet(chip(0, 0, 0, 1))
+
+    @pl.when(core == 1)
+    def _():
+        for i, j in plane:
+            greet(chip(i, j, 0, 0))
+        for k in range(1, 4):
+            greet(chip(0, 0, k, 1))
+
     loads = [
         pltpu.make_async_copy(source, target, local_sem.at[place])
         for place, (source, target) in enumerate(
@@ -343,7 +339,7 @@
     ]
     for load in loads:
         load.start()
-    pl.semaphore_wait(barrier, BACK + 46)
+    pl.semaphore_wait(barrier, BACK + 16 + 18 * core)
 
     def copy_to(source, target, sent, received, peer):
         copy = pltpu.make_async_remote_copy(
@@ -397,53 +393,67 @@
     make_last(tokens_ref, ones_ref, s7, s8, s9, s10, features_ref)
     mix_sum = forward(turned_ref, features_ref, y_ref, g_hidden_ref, cot_ref, hidden_ref, g_ref)
 
-    home = chunk_of(core, mine)
-
-    def spread(phase, part, target):
-        for slot, (i, j) in enumerate(plane):
-            place = chunk_of(1 - core, moved(theirs, i, j, 0))
-            copy_to(part.at[place], target.at[slot + 15], sends.at[phase], recvs.at[phase], their_peer(i, j))
+    home = part_of(0, 0)
+
+    def spread(phase, source_of, target):
+        for slot, (i, j) in enumerate(others):
+            copy_to(
+                source_of(part_of(i, j)), target.at[slot + 15 * (1 - core)], sends.at[phase], recvs.at[phase], chip(i, j, 0, 1)
+            )
+
+        @pl.when(core == 0)
+        def _():
+            copy_to(source_of(home), target.at[30], sends.at[phase], recvs.at[phase], chip(0, 0, 0, 1))
+
+    for owner in range(OWNERS):
+        mix_part[owner] = scale * mix_sum[SHARE * owner : SHARE * (owner + 1)]
+    spread(0, lambda owner: mix_part.at[owner], mix_in)
+    small = scale * backward(passed, folded, kappa, embed, features_ref, g_ref, cot_ref, z_ref)
+    for row in range(2 * OWNERS):
+        small_part[row // 2, row % 2] = small[row : row + 1]
+    spread(1, lambda owner: small_part.at[owner], small_in)
+
+    @pl.when(core == 1)
+    def _():
+        drain(mix_in, recvs.at[0])
+        mixed = mix_part[home]
+        for slot in range(31):
+            mixed = mixed + mix_in[slot]
+        for row in range(SHARE):
+            second[z, row] = mixed[row : row + 1]
+        drain(small_in, recvs.at[1])
+        rows = small_part[home]
+        for slot in range(31):
+            rows = rows + small_in[slot]
+        second[z, SHARE:PART] = rows
+        for k in (2, 1, 3):
+            copy_to(second.at[z], second.at[z], sends.at[2], recvs.at[2], chip(0, 0, k, 1))
+
+    outputs(embed, features_ref, hidden_ref, mix_ref, out_ref)
+    drain(held, ids_sems.at[3])
+
+    @pl.when(core == 1)
+    def _():
+        drain(second.at[pl.ds(0, 3)], recvs.at[2])
+        third[...] = (second[0] + second[1]) + (second[2] + second[3])
+        landing = whole.at[pl.ds(PART * home, PART)]
+        for i, j in plane:
+            copy_to(third, landing, sends.at[3], recvs.at[3], chip(i, j, 0, 0))
             if (i, j) in others:
-                place = chunk_of(core, moved(mine, i, j, 0))
-                copy_to(part.at[place], target.at[slot], sends.at[phase], recvs.at[phase], own_peer(i, j, 0))
-
-    for chunk in range(CHUNKS):
-        mix_part[chunk] = scale * mix_sum[8 * chunk : 8 * chunk + 8]
-    spread(0, mix_part, mix_in)
-    small = scale * backward(passed, folded, kappa, embed, features_ref, g_ref, cot_ref, z_ref)
-    for chunk in range(CHUNKS):
-        small_part[chunk] = small[chunk : chunk + 1]
-    spread(1, small_part, small_in)
-    drain(mix_in, recvs.at[0])
-    mixed = mix_part[home]
-    for slot in range(CHUNKS - 1):
-        mixed = mixed + mix_in[slot]
-    for row in range(8):
-        second[mine[2], row] = mixed[row : row + 1]
-    drain(small_in, recvs.at[1])
-    row = small_part[home]
-    for slot in range(CHUNKS - 1):
-        row = row + small_in[slot]
-    second[mine[2], 8] = row
-    spot = second.at[mine[2]]
-    for k in (2, 1, 3):
-        copy_to(spot, spot, sends.at[2], recvs.at[2], own_peer(0, 0, k))
-    outputs(embed, features_ref, hidden_ref, mix_ref, out_ref)
-    drain(second.at[pl.ds(0, 3)], recvs.at[2])
-    third[...] = (second[0] + second[1]) + (second[2] + second[3])
-    landing = whole.at[pl.ds(9 * home, 9)]
-    for i, j in plane:
-        copy_to(third, landing, sends.at[3], recvs.at[3], cross_peer(i, j))
-        if (i, j) in others:
-            copy_to(third, landing, sends.at[3], recvs.at[3], own_peer(i, j, 0))
-    whole[pl.ds(9 * home, 9)] = third[...]
-    drain(held, ids_sems.at[3])
-    drain(mix_in, sends.at[0])
-    drain(small_in, sends.at[1])
-    drain(second.at[pl.ds(0, 3)], sends.at[2])
-    gathered = whole.at[pl.ds(0, 9 * (CHUNKS - 1))]
-    drain(gathered, recvs.at[3])
-    drain(gathered, sends.at[3])
+                copy_to(third, landing, sends.at[3], recvs.at[3], chip(i, j, 0, 1))
+        whole[pl.ds(PART * home, PART)] = third[...]
+        drain(mix_in.at[pl.ds(0, 15)], sends.at[0])
+        drain(small_in.at[pl.ds(0, 15)], sends.at[1])
+        drain(second.at[pl.ds(0, 3)], sends.at[2])
+        drain(whole.at[pl.ds(0, 15 * PART)], recvs.at[3])
+        drain(whole.at[pl.ds(0, 15 * PART)], sends.at[3])
+        drain(whole, sends.at[3])
+
+    @pl.when(core == 0)
+    def _():
+        drain(mix_in.at[pl.ds(0, 16)], sends.at[0])
+        drain(small_in.at[pl.ds(0, 16)], sends.at[1])
+        drain(whole, recvs.at[3])
 
 
 def layer(count, scale, ids, embed, low, high, levels, mix, cot):
@@ -456,7 +466,7 @@
         functools.partial(layer_kernel, count, scale),
         out_shape=(
             jax.ShapeDtypeStruct((TOKENS, WIDTH), F32),
-            jax.ShapeDtypeStruct((9 * CHUNKS, 1, WIDTH), F32),
+            jax.ShapeDtypeStruct((OWNERS * PART, 1, WIDTH), F32),
             jax.ShapeDtypeStruct((32, WIDTH), F32),
         ),
         in_specs=[far] * 7,
@@ -481,12 +491,12 @@
             pltpu.VMEM((CLASSES * VOCAB, WIDTH), F32),
             *[pltpu.VMEM(array.shape, array.dtype) for array in arguments],
             pltpu.SemaphoreType.DMA((7,)),
-            pltpu.VMEM((CHUNKS, 8, WIDTH), F32),
-            pltpu.VMEM((CHUNKS, 1, WIDTH), F32),
-            pltpu.VMEM((CHUNKS - 1, 8, WIDTH), F32),
-            pltpu.VMEM((CHUNKS - 1, 1, WIDTH), F32),
-            pltpu.VMEM((4, 9, 1, WIDTH), F32),
-            pltpu.VMEM((9, 1, WIDTH), F32),
+            pltpu.VMEM((OWNERS, SHARE, WIDTH), F32),
+            pltpu.VMEM((OWNERS, 2, 1, WIDTH), F32),
+            pltpu.VMEM((31, SHARE, WIDTH), F32),
+            pltpu.VMEM((31, 2, 1, WIDTH), F32),
+            pltpu.VMEM((4, PART, 1, WIDTH), F32),
+            pltpu.VMEM((PART, 1, WIDTH), F32),
             pltpu.SemaphoreType.DMA((4,)),
             pltpu.SemaphoreType.DMA((4,)),
         ],
@@ -509,11 +519,10 @@
         stores.append(copy)
 
     store(out_ref, out_hbm)
-    for chunk in range(CHUNKS):
-        for row in range(8):
-            mix_ref[8 * chunk + row : 8 * chunk + row + 1, :] = whole[9 * chunk + row]
+    for row in range(WIDTH):
+        mix_ref[row : row + 1, :] = whole[PART * (row // SHARE) + row % SHARE]
     store(mix_ref, mix_hbm)
-    summed = [whole[9 * chunk + 8] for chunk in range(CHUNKS)]
+    summed = [whole[PART * (row // 2) + SHARE + row % 2] for row in range(2 * OWNERS)]
     for name in range(VOCAB):
         embed_ref[name : name + 1, :] = summed[16 + name]
     store(embed_ref, embed_hbm)

time: 37.5 us -> 37.6 us (level)
  no operation moved by 1% of the time
where the time goes in v7:
time: 37.6 us; the launch traced here: 37.5 us
  Pallas kernels  36.8 us (98%)
  between operations  0.64 us (2%)
    pallas_call x1, Pallas kernels, layer(): pl.pallas_call(functools.partial(layer_kernel, count, scale), out_shape=(...  35.7 us
    pallas_call x1, Pallas kernels, finish(): pl.pallas_call(finish_kernel, out_shape=tuple((jax.ShapeDtypeStruct(shape...  1.1 us

profile of v7, /device:TPU:1, one launch (start us, length us, event | category | flops | bytes accessed | tf_op | source)
XLA Modules:
  0.0 37.5 jit_solution(10064890101826222430)
XLA Ops:
  0.6 35.7 %shard_map.110 = (f32[1024,256]{1,0:T(8,128)S(1)}, f32[288,1,256]{2,1,0:T(1,128)S(1)}, f32[32,256]{1,0:T(8,128)S(1)}) custom-call(s32[8,128]{1,0:T(8,128)} %bitcast.4, f32[16,256]{1,0:T(8,128)} %embed_hbm.1, f32[2,256]{1,0:T(2,128)} %low_hbm.1, f32[2,256]{1,0:T(2,128)} %high_hbm.1, f32[14,256]{1,0:T(8,128)} %levels_hbm.1, bf16[256,256]{1,0:T(8,128)(2,1)} %mix_hbm.1, ...), custom_call_target="tpu_custom_call" | custom-call | tf_op jit(solution)/shard_map/pallas_call | solution.py:465
  36.4 1.1 %shard_map.111 = (f32[1024,256]{1,0:T(8,128)}, f32[2,2,256]{2,1,0:T(2,128)}, f32[14,256]{1,0:T(8,128)}, f32[256,256]{1,0:T(8,128)}, f32[16,256]{1,0:T(8,128)}) custom-call(f32[1024,256]{1,0:T(8,128)S(1)} %get-tuple-element.13.out_ref, f32[288,1,256]{2,1,0:T(1,128)S(1)} %get-tuple-element.14.whole, f32[32,256]{1,0:T(8,128)S(1)} %get-tuple-element.15.factors_ref), custom_call_target="tpu_custom_call" | custom-call | tf_op jit(solution)/shard_map/pallas_call | solution.py:556

commit v8 on v6

--- a/solution.py
+++ b/solution.py
@@ -17,19 +17,24 @@
 TOKENS = 1024
 BACK = 8
 TILES = (BACK + 1) * TOKENS // LANES
-CLASSES = 93
-ROWS = 96 * VOCAB
+SPLIT = {11: range(4, 8), 12: range(4, 9)}
+CLASSES = 101
+ROWS = 104 * VOCAB
 NEAR = 56 * VOCAB
-LAST = 80 * VOCAB
 CHUNKS = 32
 
 
 def class_of(level, ones):
-    return 1 + level * (level + 1) // 2 + ones + level // 12
+    return 1 + level * (level + 1) // 2 + ones
 
 
 def block_of(level, ones):
     return slice(class_of(level, ones) * VOCAB, (class_of(level, ones) + 1) * VOCAB)
+
+
+def rest_of(level, ones):
+    place = 92 + 4 * (level - 11) + ones - 4
+    return slice(place * VOCAB, (place + 1) * VOCAB)
 
 
 def dot(a, b):
@@ -66,8 +71,7 @@
 
 
 def clear_padding(ref):
-    for rows in (slice(LAST - VOCAB, LAST), slice(CLASSES * VOCAB, ROWS)):
-        ref[rows, :] = jnp.zeros((rows.stop - rows.start, ref.shape[1]), BF16)
+    ref[CLASSES * VOCAB :, :] = jnp.zeros((ROWS - CLASSES * VOCAB, ref.shape[1]), BF16)
 
 
 def make_weights(passed, folded, kappa, embed, weights_ref):
@@ -80,6 +84,8 @@
     for level in range(LEVELS):
         for ones in range(level + 1):
             put(block_of(level, ones), kappa[level] * passed(level, ones))
+            if ones in SPLIT.get(level, ()):
+                put(rest_of(level, ones), kappa[level] * passed(level, ones))
     clear_padding(weights_ref)
 
 
@@ -173,24 +179,34 @@
     place_level(s9, 9, features_ref)
 
 
-def make_middle(tokens_ref, ones_ref, s7, s8, s9, s10, features_ref):
-    count_tiles(tokens_ref, ones_ref, s7, 33, 57)
-    widen(s7, s8, 7, 34, 58)
-    widen(s8, s9, 8, 36, 60)
-    widen(s9, s10, 9, 40, 64)
+def put_sum(features_ref, level, ones, terms):
+    terms = [term for term in terms if term is not None]
+    if ones in SPLIT[level]:
+        total = sum(term.astype(F32) for term in terms)
+        high, rest = halves(total)
+        features_ref[block_of(level, ones), :] = high
+        features_ref[rest_of(level, ones), :] = rest
+    else:
+        features_ref[block_of(level, ones), :] = sum(terms[1:], terms[0])
+
+
+def make_far(tokens_ref, ones_ref, s7, s8, s9, s10, features_ref):
+    count_tiles(tokens_ref, ones_ref, s7, 1, 57)
+    widen(s7, s8, 7, 2, 58)
+    widen(s8, s9, 8, 4, 60)
+    widen(s9, s10, 9, 8, 64)
     place_level(s10, 10, features_ref)
+
+    def shard(back, ones):
+        first = (BACK - back) * 8
+        return s10[ones * VOCAB : (ones + 1) * VOCAB, first * LANES : (first + 8) * LANES] if 0 <= ones <= 10 else None
+
     for ones in range(12):
-        features_ref[block_of(11, ones), :] = widened(s10, 10, ones, 48, 56)
-
-
-def make_last(tokens_ref, ones_ref, s7, s8, s9, s10, features_ref):
-    count_tiles(tokens_ref, ones_ref, s7, 1, 33)
-    widen(s7, s8, 7, 2, 34)
-    widen(s8, s9, 8, 4, 36)
-    widen(s9, s10, 9, 8, 40)
+        put_sum(features_ref, 11, ones, [shard(2, ones), shard(3, ones - 1)])
     for ones in range(13):
-        near, late = widened(s10, 10, ones, 32, 40), widened(s10, 10, ones - 1, 16, 24)
-        features_ref[block_of(12, ones), :] = late if near is None else near if late is None else near + late
+        put_sum(
+            features_ref, 12, ones, [shard(4, ones), shard(5, ones - 1), shard(6, ones - 1), shard(7, ones - 2)]
+        )
 
 
 def gelu_parts(y):
@@ -202,12 +218,11 @@
     return y * half, slope
 
 
-def add_part(turned_ref, features_ref, y_ref, first, last):
+def near_part(turned_ref, features_ref, y_ref):
     for start in range(0, TOKENS, 256):
         span = slice(start, start + 256)
-        both = dot(turned_ref[:, first:last], features_ref[first:last, span])
-        part = both[:WIDTH] + both[WIDTH:]
-        y_ref[:, span] = part if first == 0 else y_ref[:, span] + part
+        both = dot(turned_ref[:, 0:NEAR], features_ref[0:NEAR, span])
+        y_ref[:, span] = both[:WIDTH] + both[WIDTH:]
 
 
 def before_gelu(mix_ref, cot_ref, g_hidden_ref):
@@ -221,7 +236,7 @@
     block = 256
     for start in range(0, TOKENS, block):
         span = slice(start, start + block)
-        both = dot(turned_ref[:, LAST:], features_ref[LAST:, span])
+        both = dot(turned_ref[:, NEAR:], features_ref[NEAR:, span])
         y = (y_ref[:, span] + both[:WIDTH] + both[WIDTH:]).T
         active, slope = gelu_parts(y)
         hidden = active.astype(BF16)
@@ -255,6 +270,11 @@
         z_ref[first:last, :] = both[:, :WIDTH] + both[:, WIDTH:]
 
     ends = {0: class_of(8, 0) * VOCAB, 8: class_of(11, 0) * VOCAB, 11: CLASSES * VOCAB}
+
+    def z_of(level, ones):
+        z = z_ref[block_of(level, ones), :]
+        return z + z_ref[rest_of(level, ones), :] if ones in SPLIT.get(level, ()) else z
+
     begin = 0
     rows = []
     for level in range(LEVELS):
@@ -266,10 +286,10 @@
             rows.append(over_names(z0))
             embed_sum = folded[0] * z0 + dot(features_ref[0:VOCAB, :], cot_ref[...])
             zero_sum = one_sum = jnp.zeros_like(z0)
-        total = passed(level, 0) * z_ref[block_of(level, 0), :]
+        total = passed(level, 0) * z_of(level, 0)
         counted = jnp.zeros_like(total)
         for ones in range(1, level + 1):
-            term = passed(level, ones) * z_ref[block_of(level, ones), :]
+            term = passed(level, ones) * z_of(level, ones)
             total = total + term
             counted = counted + float(ones) * term
         rows.append(over_names(total))
@@ -355,11 +375,11 @@
     def drain(ref, sem):
         pltpu.make_async_copy(ref, ref, sem).wait()
 
-    arrivals = [(0, 1), (1, 4), (4, BACK)]
+    arrivals = [(0, 1), (1, BACK)]
     for group, (first, last) in reversed(list(enumerate(arrivals))):
         for step in range(first, last):
             peer = lax.rem(seq + step + 1, count), batch
-            copy_to(ids_hbm, held.at[step], ids_sems.at[3], ids_sems.at[group], peer)
+            copy_to(ids_hbm, held.at[step], ids_sems.at[2], ids_sems.at[group], peer)
 
     for load in loads:
         load.wait()
@@ -389,12 +409,9 @@
 
     receive(0)
     make_near(tokens_ref, class_ref, ones_ref, s7, s8, s9, features_ref)
-    add_part(turned_ref, features_ref, y_ref, 0, NEAR)
+    near_part(turned_ref, features_ref, y_ref)
     receive(1)
-    make_middle(tokens_ref, ones_ref, s7, s8, s9, s10, features_ref)
-    add_part(turned_ref, features_ref, y_ref, NEAR, LAST)
-    receive(2)
-    make_last(tokens_ref, ones_ref, s7, s8, s9, s10, features_ref)
+    make_far(tokens_ref, ones_ref, s7, s8, s9, s10, features_ref)
     mix_sum = forward(turned_ref, features_ref, y_ref, g_hidden_ref, cot_ref, hidden_ref, g_ref)
 
     home = chunk_of(core, mine)
@@ -409,8 +426,8 @@
 
     for chunk in range(CHUNKS):
         mix_part[chunk] = scale * mix_sum[8 * chunk : 8 * chunk + 8]
+    small = scale * backward(passed, folded, kappa, embed, features_ref, g_ref, cot_ref, z_ref)
     spread(0, mix_part, mix_in)
-    small = scale * backward(passed, folded, kappa, embed, features_ref, g_ref, cot_ref, z_ref)
     for chunk in range(CHUNKS):
         small_part[chunk] = small[chunk : chunk + 1]
     spread(1, small_part, small_in)
@@ -437,7 +454,7 @@
         if (i, j) in others:
             copy_to(third, landing, sends.at[3], recvs.at[3], own_peer(i, j, 0))
     whole[pl.ds(9 * home, 9)] = third[...]
-    drain(held, ids_sems.at[3])
+    drain(held, ids_sems.at[2])
     drain(mix_in, sends.at[0])
     drain(small_in, sends.at[1])
     drain(second.at[pl.ds(0, 3)], sends.at[2])
@@ -463,7 +480,7 @@
         out_specs=(vmem,) * 3,
         scratch_shapes=[
             pltpu.VMEM((BACK, 8, LANES), jnp.int32),
-            pltpu.SemaphoreType.DMA((4,)),
+            pltpu.SemaphoreType.DMA((3,)),
             pltpu.VMEM((2 * LANES, 8 * LANES), BF16),
             pltpu.VMEM((2 * LANES, 29 * LANES), BF16),
             pltpu.VMEM((TILES * VOCAB, 2 * LANES), BF16),

time: 37.5 us -> 37 us (0.987)
  Pallas kernels: 36.8 us -> 36.2 us
    pallas_call x1, Pallas kernels: 35.7 us -> 35.1 us  [layer(): pl.pallas_call(functools.partial(layer_kernel, count, scale), out_shape=(...]
where the time goes in v8:
time: 37 us; the launch traced here: 36.9 us
  Pallas kernels  36.2 us (98%)
  between operations  0.64 us (2%)
    pallas_call x1, Pallas kernels, layer(): pl.pallas_call(functools.partial(layer_kernel, count, scale), out_shape=(...  35.1 us
    pallas_call x1, Pallas kernels, finish(): pl.pallas_call(finish_kernel, out_shape=tuple((jax.ShapeDtypeStruct(shape...  1.1 us

profile of v8, /device:TPU:1, one launch (start us, length us, event | category | flops | bytes accessed | tf_op | source)
XLA Modules:
  0.0 36.9 jit_solution(11551955704246839861)
XLA Ops:
  0.6 35.1 %shard_map.110 = (f32[1024,256]{1,0:T(8,128)S(1)}, f32[288,1,256]{2,1,0:T(1,128)S(1)}, f32[32,256]{1,0:T(8,128)S(1)}) custom-call(s32[8,128]{1,0:T(8,128)} %bitcast.4, f32[16,256]{1,0:T(8,128)} %embed_hbm.1, f32[2,256]{1,0:T(2,128)} %low_hbm.1, f32[2,256]{1,0:T(2,128)} %high_hbm.1, f32[14,256]{1,0:T(8,128)} %levels_hbm.1, bf16[256,256]{1,0:T(8,128)(2,1)} %mix_hbm.1, ...), custom_call_target="tpu_custom_call" | custom-call | tf_op jit(solution)/shard_map/pallas_call | solution.py:472
  35.8 1.1 %shard_map.111 = (f32[1024,256]{1,0:T(8,128)}, f32[2,2,256]{2,1,0:T(2,128)}, f32[14,256]{1,0:T(8,128)}, f32[256,256]{1,0:T(8,128)}, f32[16,256]{1,0:T(8,128)}) custom-call(f32[1024,256]{1,0:T(8,128)S(1)} %get-tuple-element.13.out_ref, f32[288,1,256]{2,1,0:T(1,128)S(1)} %get-tuple-element.14.whole, f32[32,256]{1,0:T(8,128)S(1)} %get-tuple-element.15.factors_ref), custom_call_target="tpu_custom_call" | custom-call | tf_op jit(solution)/shard_map/pallas_call | solution.py:564

commit v9 on v8

--- a/solution.py
+++ b/solution.py
@@ -21,6 +21,9 @@
 CLASSES = 101
 ROWS = 104 * VOCAB
 NEAR = 56 * VOCAB
+PIECES = ((0, 37 * VOCAB), (37 * VOCAB, 46 * VOCAB), (46 * VOCAB, NEAR), (NEAR, ROWS))
+STARTS = (0, 640, 896, 1152)
+WEIGHTS = STARTS[3] + ROWS - NEAR
 CHUNKS = 32
 
 
@@ -70,12 +73,12 @@
     return lambda level, ones: chains[0][level - ones] * chains[1][ones]
 
 
-def clear_padding(ref):
-    ref[CLASSES * VOCAB :, :] = jnp.zeros((ROWS - CLASSES * VOCAB, ref.shape[1]), BF16)
-
-
 def make_weights(passed, folded, kappa, embed, weights_ref):
+    weights_ref[...] = jnp.zeros_like(weights_ref)
+
     def put(rows, factor):
+        shift = next(start - piece[0] for piece, start in zip(PIECES, STARTS) if rows.start < piece[1])
+        rows = slice(rows.start + shift, rows.stop + shift)
         high, rest = halves(factor * embed)
         weights_ref[rows, 0:WIDTH] = high
         weights_ref[rows, WIDTH:] = rest
@@ -86,7 +89,6 @@
             put(block_of(level, ones), kappa[level] * passed(level, ones))
             if ones in SPLIT.get(level, ()):
                 put(rest_of(level, ones), kappa[level] * passed(level, ones))
-    clear_padding(weights_ref)
 
 
 def where_is(table, value):
@@ -161,21 +163,40 @@
     features_ref[rows, :] = source[:, begin : begin + TOKENS]
 
 
+def count_classes(tokens_ref, class_ref, features_ref, first, last):
+    tokens = tokens_ref[first * VOCAB : last * VOCAB, :]
+    for begin in range(0, 29, 2):
+        members = range(begin, min(begin + 2, 29))
+        result = dot(tokens, class_ref[:, begin * LANES : (begin + len(members)) * LANES]).astype(BF16)
+        for tile in range(first, last):
+            place = (tile - 8 * BACK) * LANES
+            for half, member in enumerate(members):
+                features_ref[member * VOCAB : (member + 1) * VOCAB, place : place + LANES] = result[
+                    (tile - first) * VOCAB : (tile - first + 1) * VOCAB, half * LANES : (half + 1) * LANES
+                ]
+
+
+def place_tiles(source, level, features_ref, first, last):
+    rows = slice(class_of(level, 0) * VOCAB, class_of(level + 1, 0) * VOCAB)
+    begin = BACK * TOKENS - 2**level
+    features_ref[rows, first * LANES : last * LANES] = source[:, begin + first * LANES : begin + last * LANES]
+
+
+def make_own(tokens_ref, class_ref, ones_ref, s7, s8, features_ref):
+    count_classes(tokens_ref, class_ref, features_ref, 65, 72)
+    count_tiles(tokens_ref, ones_ref, s7, 65, 71)
+    widen(s7, s8, 7, 66, 70)
+    place_tiles(s7, 7, features_ref, 2, 8)
+    place_tiles(s8, 8, features_ref, 4, 8)
+
+
 def make_near(tokens_ref, class_ref, ones_ref, s7, s8, s9, features_ref):
-    own = tokens_ref[64 * VOCAB : 72 * VOCAB, :]
-    for first in range(0, 29, 2):
-        members = range(first, min(first + 2, 29))
-        result = dot(own, class_ref[:, first * LANES : (first + len(members)) * LANES]).astype(BF16)
-        for tile in range(8):
-            for half, member in enumerate(members):
-                features_ref[member * VOCAB : (member + 1) * VOCAB, tile * LANES : (tile + 1) * LANES] = result[
-                    tile * VOCAB : (tile + 1) * VOCAB, half * LANES : (half + 1) * LANES
-                ]
-    count_tiles(tokens_ref, ones_ref, s7, 57, 71)
-    widen(s7, s8, 7, 58, 70)
+    count_classes(tokens_ref, class_ref, features_ref, 64, 65)
+    count_tiles(tokens_ref, ones_ref, s7, 57, 65)
+    widen(s7, s8, 7, 58, 66)
     widen(s8, s9, 8, 60, 68)
-    place_level(s7, 7, features_ref)
-    place_level(s8, 8, features_ref)
+    place_tiles(s7, 7, features_ref, 0, 2)
+    place_tiles(s8, 8, features_ref, 0, 4)
     place_level(s9, 9, features_ref)
 
 
@@ -218,11 +239,17 @@
     return y * half, slope
 
 
-def near_part(turned_ref, features_ref, y_ref):
-    for start in range(0, TOKENS, 256):
-        span = slice(start, start + 256)
-        both = dot(turned_ref[:, 0:NEAR], features_ref[0:NEAR, span])
-        y_ref[:, span] = both[:WIDTH] + both[WIDTH:]
+def piece_of_y(turned_ref, features_ref, piece, span):
+    (first, last), start = PIECES[piece], STARTS[piece]
+    both = dot(turned_ref[:, start : start + last - first], features_ref[first:last, span])
+    return both[:WIDTH] + both[WIDTH:]
+
+
+def parts_of_y(turned_ref, features_ref, y_ref, wanted):
+    for piece, first, last in wanted:
+        span = slice(first, last)
+        part = piece_of_y(turned_ref, features_ref, piece, span)
+        y_ref[:, span] = part if piece == 0 else y_ref[:, span] + part
 
 
 def before_gelu(mix_ref, cot_ref, g_hidden_ref):
@@ -233,11 +260,10 @@
 
 def forward(turned_ref, features_ref, y_ref, g_hidden_ref, cot_ref, hidden_ref, g_ref):
     mix_sum = None
-    block = 256
+    block = 512
     for start in range(0, TOKENS, block):
         span = slice(start, start + block)
-        both = dot(turned_ref[:, NEAR:], features_ref[NEAR:, span])
-        y = (y_ref[:, span] + both[:WIDTH] + both[WIDTH:]).T
+        y = (y_ref[:, span] + piece_of_y(turned_ref, features_ref, 3, span)).T
         active, slope = gelu_parts(y)
         hidden = active.astype(BF16)
         hidden_ref[span, :] = hidden
@@ -391,9 +417,11 @@
     turned_ref[...] = weights_ref[...].T
     make_tables(ones_ref, class_ref)
     tokens_ref[0:VOCAB, LANES:] = jnp.zeros((VOCAB, LANES), BF16)
-    clear_padding(features_ref)
+    features_ref[CLASSES * VOCAB :, :] = jnp.zeros((ROWS - CLASSES * VOCAB, TOKENS), BF16)
     before_gelu(mix_ref, cot_ref, g_hidden_ref)
     make_hot(tokens_ref, 8 * BACK, ids_ref[...])
+    make_own(tokens_ref, class_ref, ones_ref, s7, s8, features_ref)
+    parts_of_y(turned_ref, features_ref, y_ref, ((0, 256, 1024), (1, 512, 1024)))
 
     factors_ref[0:2, :] = low_ref[...]
     factors_ref[2:4, :] = high_ref[...]
@@ -409,7 +437,7 @@
 
     receive(0)
     make_near(tokens_ref, class_ref, ones_ref, s7, s8, s9, features_ref)
-    near_part(turned_ref, features_ref, y_ref)
+    parts_of_y(turned_ref, features_ref, y_ref, ((0, 0, 256), (1, 0, 512), (2, 0, 1024)))
     receive(1)
     make_far(tokens_ref, ones_ref, s7, s8, s9, s10, features_ref)
     mix_sum = forward(turned_ref, features_ref, y_ref, g_hidden_ref, cot_ref, hidden_ref, g_ref)
@@ -489,8 +517,8 @@
             pltpu.VMEM((10 * VOCAB, TILES * LANES), BF16),
             pltpu.VMEM((11 * VOCAB, TILES * LANES), BF16),
             pltpu.VMEM((ROWS, TOKENS), BF16),
-            pltpu.VMEM((ROWS, 2 * WIDTH), BF16),
-            pltpu.VMEM((2 * WIDTH, ROWS), BF16),
+            pltpu.VMEM((WEIGHTS, 2 * WIDTH), BF16),
+            pltpu.VMEM((2 * WIDTH, WEIGHTS), BF16),
             pltpu.VMEM((WIDTH, TOKENS), F32),
             pltpu.VMEM((TOKENS, WIDTH), F32),
             pltpu.VMEM((TOKENS, WIDTH), BF16),

time: 37 us -> 36 us (0.973)
  Pallas kernels: 36.2 us -> 35.2 us
    pallas_call x1, Pallas kernels: 35.1 us -> 34.1 us  [layer(): pl.pallas_call(functools.partial(layer_kernel, count, scale), out_shape=(...]
where the time goes in v9:
time: 36 us; the launch traced here: 35.9 us
  Pallas kernels  35.2 us (98%)
  between operations  0.64 us (2%)
    pallas_call x1, Pallas kernels, layer(): pl.pallas_call(functools.partial(layer_kernel, count, scale), out_shape=(...  34.1 us
    pallas_call x1, Pallas kernels, finish(): pl.pallas_call(finish_kernel, out_shape=tuple((jax.ShapeDtypeStruct(shape...  1.1 us

profile of v9, /device:TPU:1, one launch (start us, length us, event | category | flops | bytes accessed | tf_op | source)
XLA Modules:
  0.0 35.9 jit_solution(16974582512321051381)
XLA Ops:
  0.6 34.1 %shard_map.110 = (f32[1024,256]{1,0:T(8,128)S(1)}, f32[288,1,256]{2,1,0:T(1,128)S(1)}, f32[32,256]{1,0:T(8,128)S(1)}) custom-call(s32[8,128]{1,0:T(8,128)} %bitcast.4, f32[16,256]{1,0:T(8,128)} %embed_hbm.1, f32[2,256]{1,0:T(2,128)} %low_hbm.1, f32[2,256]{1,0:T(2,128)} %high_hbm.1, f32[14,256]{1,0:T(8,128)} %levels_hbm.1, bf16[256,256]{1,0:T(8,128)(2,1)} %mix_hbm.1, ...), custom_call_target="tpu_custom_call" | custom-call | tf_op jit(solution)/shard_map/pallas_call | solution.py:500
  34.8 1.1 %shard_map.111 = (f32[1024,256]{1,0:T(8,128)}, f32[2,2,256]{2,1,0:T(2,128)}, f32[14,256]{1,0:T(8,128)}, f32[256,256]{1,0:T(8,128)}, f32[16,256]{1,0:T(8,128)}) custom-call(f32[1024,256]{1,0:T(8,128)S(1)} %get-tuple-element.13.out_ref, f32[288,1,256]{2,1,0:T(1,128)S(1)} %get-tuple-element.14.whole, f32[32,256]{1,0:T(8,128)S(1)} %get-tuple-element.15.factors_ref), custom_call_target="tpu_custom_call" | custom-call | tf_op jit(solution)/shard_map/pallas_call | solution.py:592

commit v10 on v9

--- a/solution.py
+++ b/solution.py
@@ -123,20 +123,20 @@
             tokens_ref[(tile + 1) * VOCAB : (tile + 2) * VOCAB, LANES:] = hot
 
 
-def put_counts(result, s7, first, last, pair):
+def put_counts(result, s7, first, last, begin):
     for tile in range(first, last):
-        for half in range(2):
-            value = 2 * pair + half
+        for place in range(4):
+            value = begin + place
             s7[value * VOCAB : (value + 1) * VOCAB, tile * LANES : (tile + 1) * LANES] = result[
-                (tile - first) * VOCAB : (tile - first + 1) * VOCAB, half * LANES : (half + 1) * LANES
+                (tile - first) * VOCAB : (tile - first + 1) * VOCAB, place * LANES : (place + 1) * LANES
             ]
 
 
 def count_tiles(tokens_ref, ones_ref, s7, first, last):
-    for pair in range(4):
-        table = ones_ref[:, 2 * pair * LANES : 2 * (pair + 1) * LANES]
+    for half in range(2):
+        table = ones_ref[:, 4 * half * LANES : 4 * (half + 1) * LANES]
         result = dot(tokens_ref[first * VOCAB : last * VOCAB, :], table).astype(BF16)
-        put_counts(result, s7, first, last, pair)
+        put_counts(result, s7, first, last, 4 * half)
 
 
 def widened(source, level, ones, first, last):
@@ -165,8 +165,8 @@
 
 def count_classes(tokens_ref, class_ref, features_ref, first, last):
     tokens = tokens_ref[first * VOCAB : last * VOCAB, :]
-    for begin in range(0, 29, 2):
-        members = range(begin, min(begin + 2, 29))
+    for begin in range(0, 29, 8):
+        members = range(begin, min(begin + 8, 29))
         result = dot(tokens, class_ref[:, begin * LANES : (begin + len(members)) * LANES]).astype(BF16)
         for tile in range(first, last):
             place = (tile - 8 * BACK) * LANES
@@ -459,6 +459,7 @@
     for chunk in range(CHUNKS):
         small_part[chunk] = small[chunk : chunk + 1]
     spread(1, small_part, small_in)
+    outputs(embed, features_ref, hidden_ref, mix_ref, out_ref)
     drain(mix_in, recvs.at[0])
     mixed = mix_part[home]
     for slot in range(CHUNKS - 1):
@@ -473,7 +474,6 @@
     spot = second.at[mine[2]]
     for k in (2, 1, 3):
         copy_to(spot, spot, sends.at[2], recvs.at[2], own_peer(0, 0, k))
-    outputs(embed, features_ref, hidden_ref, mix_ref, out_ref)
     drain(second.at[pl.ds(0, 3)], recvs.at[2])
     third[...] = (second[0] + second[1]) + (second[2] + second[3])
     landing = whole.at[pl.ds(9 * home, 9)]

time: 36 us -> 36 us (level)
  no operation moved by 1% of the time
where the time goes in v10:
time: 36 us; the launch traced here: 35.9 us
  Pallas kernels  35.2 us (98%)
  between operations  0.64 us (2%)
    pallas_call x1, Pallas kernels, layer(): pl.pallas_call(functools.partial(layer_kernel, count, scale), out_shape=(...  34.1 us
    pallas_call x1, Pallas kernels, finish(): pl.pallas_call(finish_kernel, out_shape=tuple((jax.ShapeDtypeStruct(shape...  1.1 us

profile of v10, /device:TPU:1, one launch (start us, length us, event | category | flops | bytes accessed | tf_op | source)
XLA Modules:
  0.0 35.9 jit_solution(8886349139976756390)
XLA Ops:
  0.6 34.1 %shard_map.110 = (f32[1024,256]{1,0:T(8,128)S(1)}, f32[288,1,256]{2,1,0:T(1,128)S(1)}, f32[32,256]{1,0:T(8,128)S(1)}) custom-call(s32[8,128]{1,0:T(8,128)} %bitcast.4, f32[16,256]{1,0:T(8,128)} %embed_hbm.1, f32[2,256]{1,0:T(2,128)} %low_hbm.1, f32[2,256]{1,0:T(2,128)} %high_hbm.1, f32[14,256]{1,0:T(8,128)} %levels_hbm.1, bf16[256,256]{1,0:T(8,128)(2,1)} %mix_hbm.1, ...), custom_call_target="tpu_custom_call" | custom-call | tf_op jit(solution)/shard_map/pallas_call | solution.py:500
  34.8 1.1 %shard_map.111 = (f32[1024,256]{1,0:T(8,128)}, f32[2,2,256]{2,1,0:T(2,128)}, f32[14,256]{1,0:T(8,128)}, f32[256,256]{1,0:T(8,128)}, f32[16,256]{1,0:T(8,128)}) custom-call(f32[1024,256]{1,0:T(8,128)S(1)} %get-tuple-element.13.out_ref, f32[288,1,256]{2,1,0:T(1,128)S(1)} %get-tuple-element.14.whole, f32[32,256]{1,0:T(8,128)S(1)} %get-tuple-element.15.factors_ref), custom_call_target="tpu_custom_call" | custom-call | tf_op jit(solution)/shard_map/pallas_call | solution.py:592

commit v11 on v9

--- a/solution.py
+++ b/solution.py
@@ -259,7 +259,6 @@
 
 
 def forward(turned_ref, features_ref, y_ref, g_hidden_ref, cot_ref, hidden_ref, g_ref):
-    mix_sum = None
     block = 512
     for start in range(0, TOKENS, block):
         span = slice(start, start + block)
@@ -270,9 +269,9 @@
         g_high, g_rest = halves(g_hidden_ref[span, :] * slope)
         g_ref[span, 0:WIDTH] = g_high
         g_ref[span, WIDTH:] = g_rest
-        term = lax.dot_general(hidden, cot_ref[span, :], (((0,), (0,)), ((), ())), preferred_element_type=F32)
-        mix_sum = term if mix_sum is None else mix_sum + term
-    return mix_sum
+    return lax.dot_general(
+        hidden_ref[...], cot_ref[...], (((0,), (0,)), ((), ())), preferred_element_type=F32
+    )
 
 
 def outputs(embed, features_ref, hidden_ref, mix_ref, out_ref):

time: 36 us -> 36 us (level)
  no operation moved by 1% of the time
where the time goes in v11:
time: 36 us; the launch traced here: 35.9 us
  Pallas kernels  35.2 us (98%)
  between operations  0.64 us (2%)
    pallas_call x1, Pallas kernels, layer(): pl.pallas_call(functools.partial(layer_kernel, count, scale), out_shape=(...  34.1 us
    pallas_call x1, Pallas kernels, finish(): pl.pallas_call(finish_kernel, out_shape=tuple((jax.ShapeDtypeStruct(shape...  1.1 us

profile of v11, /device:TPU:1, one launch (start us, length us, event | category | flops | bytes accessed | tf_op | source)
XLA Modules:
  0.0 35.9 jit_solution(16314103534672993307)
XLA Ops:
  0.6 34.1 %shard_map.110 = (f32[1024,256]{1,0:T(8,128)S(1)}, f32[288,1,256]{2,1,0:T(1,128)S(1)}, f32[32,256]{1,0:T(8,128)S(1)}) custom-call(s32[8,128]{1,0:T(8,128)} %bitcast.4, f32[16,256]{1,0:T(8,128)} %embed_hbm.1, f32[2,256]{1,0:T(2,128)} %low_hbm.1, f32[2,256]{1,0:T(2,128)} %high_hbm.1, f32[14,256]{1,0:T(8,128)} %levels_hbm.1, bf16[256,256]{1,0:T(8,128)(2,1)} %mix_hbm.1, ...), custom_call_target="tpu_custom_call" | custom-call | tf_op jit(solution)/shard_map/pallas_call | solution.py:499
  34.8 1.1 %shard_map.111 = (f32[1024,256]{1,0:T(8,128)}, f32[2,2,256]{2,1,0:T(2,128)}, f32[14,256]{1,0:T(8,128)}, f32[256,256]{1,0:T(8,128)}, f32[16,256]{1,0:T(8,128)}) custom-call(f32[1024,256]{1,0:T(8,128)S(1)} %get-tuple-element.13.out_ref, f32[288,1,256]{2,1,0:T(1,128)S(1)} %get-tuple-element.14.whole, f32[32,256]{1,0:T(8,128)S(1)} %get-tuple-element.15.factors_ref), custom_call_target="tpu_custom_call" | custom-call | tf_op jit(solution)/shard_map/pallas_call | solution.py:591
